TPU v7x, 32 devices: a whole 2x2x4 slice. The times are simulated.
32 devices in a mesh: ctx: 8 (over z, x), tp: 4 (over y, core).
Axes of the slice: x: 2, y: 2, z: 4, core: 2. Of those that a mesh axis runs over, the one named last changes fastest.
Arguments:
- queries: bfloat16 [2048, 1024], P('ctx', 'tp'), may hold values from -6 to 6
- keys: bfloat16 [2048, 1024], P('ctx', 'tp'), may hold values from -6 to 6
- values: bfloat16 [2048, 1024], P('ctx', 'tp'), may hold values from -20 to 20, as said below
- gain: float32 [1024], P('tp'), may hold values from 0.25 to 1.75
- out_grad: bfloat16 [2048, 1024], P('ctx', 'tp'), may hold values from -6 to 6
Outputs:
- normed: bfloat16 [2048, 1024], P('ctx', 'tp')
- grad_queries: bfloat16 [2048, 1024], P('ctx', 'tp')
- grad_keys: bfloat16 [2048, 1024], P('ctx', 'tp')
- grad_values: bfloat16 [2048, 1024], P('ctx', 'tp')
Inputs may be any that keep to these rules, and one draw needn't show every extreme that they name: values of order one, each head at its own scale.
All inputs are finite; a program needn't handle non-finite values.
Results may differ from a plain program's by a relative error of at most 0.0065.
Values sent between devices are 32-bit elements; how exact they have to be, the bound alone decides.
No kernel may reach another device: no remote copies, remote signals or barrier semaphores. Data moves between devices by JAX's collectives and lax.ppermute only.
A program may use at most 64 MiB of HBM per device.

v0:
```python
import functools

import jax
import jax.numpy as jnp
from jax import lax
from jax.experimental import pallas as pl
from jax.experimental.pallas import tpu as pltpu
from jax.sharding import PartitionSpec as P

HEAD = 128

epsilon = 1e-06
F32 = jnp.float32
BF16 = jnp.bfloat16

NN = (((1,), (0,)), ((), ()))
NT = (((1,), (1,)), ((), ()))
TN = (((0,), (0,)), ((), ()))


def dot(a, b, dims):
    return lax.dot_general(a, b, dims, preferred_element_type=F32)


VMEM = pl.BlockSpec(memory_space=pltpu.VMEM)
HBM = pl.BlockSpec(memory_space=pltpu.HBM)


def call(body, outs, *args, ins=None, dests=None, scratch=(), flops=1e7):
    moved = sum(a.size * a.dtype.itemsize for a in args)
    return pl.pallas_call(
        body,
        out_shape=outs,
        in_specs=ins or [VMEM] * len(args),
        out_specs=dests or jax.tree.map(lambda _: VMEM, outs),
        scratch_shapes=scratch,
        compiler_params=pltpu.CompilerParams(vmem_limit_bytes=16 * 1024 * 1024),
        cost_estimate=pl.CostEstimate(flops=int(flops), bytes_accessed=int(moved), transcendentals=0),
    )(*args)


def head(h):
    return slice(h * HEAD, (h + 1) * HEAD)


def causal_mask(tokens):
    row = lax.broadcasted_iota(jnp.int32, (tokens, tokens), 0)
    col = lax.broadcasted_iota(jnp.int32, (tokens, tokens), 1)
    return row >= col


def rows_of(scratch, parts, place):
    rows = scratch.shape[0] // parts
    return scratch.at[pl.ds(pl.multiple_of(place * rows, rows), rows), :]


def partner(i, group):
    return group - 1 - i


def give(scratch, group, outs):
    if len(outs) == 1:
        outs[0][...] = scratch[...].reshape(outs[0].shape)
        return
    place = lax.rem(lax.axis_index("ctx"), group)
    for i, out in enumerate(outs):
        out[...] = rows_of(scratch, group, lax.bitwise_xor(place, partner(i, group)))[...]


def take(ins, scratch, group):
    if len(ins) == 1:
        scratch[...] = ins[0][...].reshape(scratch.shape)
        return
    place = lax.rem(lax.axis_index("ctx"), group)
    for i, piece in enumerate(ins):
        rows_of(scratch, group, lax.bitwise_xor(place, partner(i, group)))[...] = piece[...]


def running_sums(scratch, parts, reverse):
    rows = scratch.shape[0] // parts
    running = jnp.zeros((rows, scratch.shape[1]), F32)
    for place in range(parts - 1, -1, -1) if reverse else range(parts):
        own = slice(place * rows, (place + 1) * rows)
        here = scratch[own, :]
        scratch[own, :] = running
        running = running + here
    return running


def loads(pairs, sems):
    copies = [pltpu.make_async_copy(a, b, sems.at[i]) for i, (a, b) in enumerate(pairs)]
    for copy in copies:
        copy.start()
    return copies


def states_body(heads, group, k_hbm, v_hbm, k, v, *refs):
    outs, (state, sems) = refs[:-2], refs[-2:]
    parts = [(a.at[:, head(h)], b.at[:, head(h)]) for h in range(heads) for a, b in ((k_hbm, k), (v_hbm, v))]
    copies = loads(parts, sems)
    for h in range(heads):
        copies[2 * h].wait()
        copies[2 * h + 1].wait()
        state[head(h), :] = dot(k[:, head(h)], v[:, head(h)], TN)
    give(state, group, outs[:group])
    for i, again in enumerate(outs[group:]):
        again[...] = outs[i][...]


def scan_body(count, reverse, arrived, sums, scratch):
    take([arrived], scratch, count)
    running_sums(scratch, count, reverse)
    give(scratch, count, [sums])


def inner_body(group, reverse, *refs):
    arrived, total, outs, sums = refs[:group], refs[group], refs[group + 1 : 2 * group + 1], refs[-1]
    take(arrived, sums, group)
    total[...] = running_sums(sums, group, reverse)
    give(sums, group, outs)
    if not reverse:
        refs[-2][...] = arrived[-1][...]


def add_body(group, sums, over, *outs):
    place = lax.rem(lax.axis_index("ctx"), group)
    for i, out in enumerate(outs):
        out[...] = rows_of(sums, group, lax.bitwise_xor(place, partner(i, group)))[...] + over[...]


def late_body(group, reverse, *refs):
    arrived, over, outs, sums = refs[:group], refs[group], refs[group + 1 : -1], refs[-1]
    take(arrived, sums, group)
    running_sums(sums, group, reverse)
    add_body(group, sums, over, *outs)


def pick(pieces, scratch, group):
    many = len(pieces) // 2
    if many == 0:
        take(pieces, scratch, group)
        return
    early = lax.axis_index("ctx") < group
    place = lax.rem(lax.axis_index("ctx"), group)
    for i in range(many):
        rows = rows_of(scratch, group, lax.bitwise_xor(place, partner(i, group)))
        rows[...] = jnp.where(early, pieces[i][...], pieces[many + i][...])


def scores_body(heads, factor, k, v, q_hbm, og_hbm, gain_hbm, scores, attended, q, og, gain, sems):
    copies = loads(((q_hbm, q), (og_hbm, og), (gain_hbm, gain)), sems)
    copies[0].wait()
    causal = causal_mask(q.shape[0])
    for h in range(heads):
        raw = dot(q[:, head(h)], k[:, head(h)], NT) * factor
        sc = jnp.where(causal, raw, 0.0).astype(BF16)
        scores[h] = sc
        attended[:, head(h)] = dot(sc, v[:, head(h)], NN)
    for copy in copies[1:]:
        copy.wait()


def attend_body(heads, factor, group, q, og, gain, local, *refs):
    pieces, (attended, stats, prefix) = refs[:-3], refs[-3:]
    pick(pieces, prefix, group)
    power = 0.0
    inner = 0.0
    for h in range(heads):
        att = factor * dot(q[:, head(h)], prefix[head(h), :].astype(BF16), NN) + local[:, head(h)]
        attended[:, head(h)] = att
        weighted = og[:, head(h)].astype(F32) * gain[h : h + 1, :]
        power = power + att * att
        inner = inner + weighted * att
    stats[0:1, :] = jnp.sum(power.T, axis=0, keepdims=True)
    stats[1:2, :] = jnp.sum(inner.T, axis=0, keepdims=True)


def grad_body(heads, features, group, ways, attended, og, gain, q, *refs):
    stats, (normed, grad), outs, updates = refs[:ways], refs[ways : ways + 2], refs[ways + 2 : -1], refs[-1]
    total = stats[0][...]
    for other in stats[1:]:
        total = total + other[...]
    inv_rms = lax.rsqrt(total[0:1, :] / features + epsilon)
    bend = inv_rms * inv_rms * (total[1:2, :] / features)
    tokens = q.shape[0]
    inv_rms = jnp.broadcast_to(inv_rms, (HEAD, tokens)).T
    bend = jnp.broadcast_to(bend, (HEAD, tokens)).T
    for h in range(heads):
        att = attended[:, head(h)]
        gain_h = gain[h : h + 1, :]
        weighted = og[:, head(h)].astype(F32) * gain_h
        ga = (inv_rms * (weighted - att * bend)).astype(BF16)
        grad[:, head(h)] = ga
        updates[head(h), :] = dot(q[:, head(h)], ga, TN)
        normed[:, head(h)] = (att * inv_rms * gain_h).astype(BF16)
    give(updates, group, outs)


def local_body(heads, factor, ga, q, k, v, prefix, scores, normed, normed_out, gq, gk_part, gv_part):
    normed_out[...] = normed[...]
    causal = causal_mask(q.shape[0])
    for h in range(heads):
        gah = ga[:, head(h)]
        raw = dot(gah, v[:, head(h)], NT) * factor
        gs = jnp.where(causal, raw, 0.0).astype(BF16)
        out = factor * dot(gah, prefix[head(h), :].astype(BF16), NT)
        gq[:, head(h)] = (out + dot(gs, k[:, head(h)], NN)).astype(BF16)
        gk_part[:, head(h)] = dot(gs, q[:, head(h)], TN)
        gv_part[:, head(h)] = dot(scores[h], gah, TN)


def final_body(heads, factor, group, k, v, gk_part, gv_part, *refs):
    pieces, outs, (suffix, gk, gv, sems) = refs[:-6], refs[-6:-4], refs[-4:]
    pick(pieces, suffix, group)
    copies = []

    def send(h, held, out):
        copy = pltpu.make_async_copy(held.at[:, head(h)], out.at[:, head(h)], sems.at[len(copies)])
        copy.start()
        copies.append(copy)

    for h in range(heads):
        suf = suffix[head(h), :].astype(BF16)
        gk[:, head(h)] = (factor * dot(v[:, head(h)], suf, NT) + gk_part[:, head(h)]).astype(BF16)
        send(h, gk, outs[0])
        gv[:, head(h)] = (factor * dot(k[:, head(h)], suf, NN) + gv_part[:, head(h)]).astype(BF16)
        send(h, gv, outs[1])
    for copy in copies:
        copy.wait()


def exchange(pieces, active, group):
    ways = lax.axis_size("tp")
    return [
        lax.ppermute(
            piece,
            ("ctx", "tp"),
            [
                (j * ways + t, (j ^ partner(i, group) if j in active else j) * ways + (t ^ 1))
                for j in range(2 * group)
                for t in range(ways)
            ],
        )
        for i, piece in enumerate(pieces)
    ]


def carried_in(pieces, reverse, state):
    group = len(pieces) if reverse else (len(pieces) + 1) // 2
    pieces, again = pieces[:group], pieces[group:]
    count = lax.axis_size("ctx")
    sds = jax.ShapeDtypeStruct
    if group == 1:
        arrived = lax.all_to_all(pieces[0], "ctx", 0, 0, tiled=True)
        sums = call(
            functools.partial(scan_body, count, reverse),
            sds(arrived.shape, F32), arrived, scratch=[state],
        )
        return [lax.all_to_all(sums, "ctx", 0, 0, tiled=True)]
    rows, width = pieces[0].shape
    piece = sds((rows, width), F32)
    early, late, both = range(group), range(group, count), range(count)
    first, second = (late, early) if reverse else (early, late)
    arrived = exchange(pieces, both if reverse else first, group)
    kept = sds((group * rows, width), F32) if reverse else piece
    total, *back = call(
        functools.partial(inner_body, group, reverse),
        [piece] * (group + 1) + [kept],
        *arrived,
        scratch=[] if reverse else [state],
    )
    over = lax.ppermute(total, "ctx", [(j, j ^ group) for j in both])
    ahead = exchange(back[:group], first, group)
    if reverse:
        back = call(functools.partial(add_body, group), [piece] * group, back[group], over)
    else:
        back = call(
            functools.partial(late_body, group, reverse),
            [piece] * group, *exchange(again, second, group), back[group], over, scratch=[state],
        )
    behind = exchange(back, second, group)
    return [*behind, *ahead] if reverse else [*ahead, *behind]


def from_all(part, axis):
    count = lax.axis_size(axis)
    even = count & (count - 1) == 0
    steps = [1, 3, 2] if count == 4 else range(1, count)
    return [part] + [
        lax.ppermute(part, axis, [(i, i ^ step if even else (i + step) % count) for i in range(count)])
        for step in steps
    ]


def on_device(queries, keys, values, gain, out_grad):
    tokens, width = queries.shape
    heads = width // HEAD
    count = lax.axis_size("ctx")
    factor = (HEAD * tokens * count) ** (-0.5)
    features = width * lax.axis_size("tp")
    gains = gain.reshape(heads, HEAD)
    sds = jax.ShapeDtypeStruct
    wide = sds((tokens, width), F32)
    half = sds((tokens, width), BF16)
    state = pltpu.VMEM((width, HEAD), F32)
    if count in (4, 8) and lax.axis_size("tp") % 2 == 0:
        group = count // 2
        pieces = [sds((width // group, HEAD), F32)] * group
    else:
        group = count
        pieces = [sds((count, width // count, HEAD), F32)]

    def in_hbm(*arrays):
        return [pltpu.with_memory_space_constraint(array, pltpu.HBM) for array in arrays]

    def in_vmem(array):
        return pltpu.VMEM(array.shape, array.dtype)

    k_held, v_held, *states = call(
        functools.partial(states_body, heads, group),
        (in_vmem(keys), in_vmem(values), *pieces, *pieces[1:]),
        *in_hbm(keys, values),
        ins=[HBM, HBM],
        scratch=[state, pltpu.SemaphoreType.DMA((2 * heads,))],
    )
    prefix = carried_in(states, False, state)
    pairs = heads * tokens * tokens * HEAD
    scores, local, q_held, og_held, gain_held = call(
        functools.partial(scores_body, heads, factor),
        (
            sds((heads, tokens, tokens), BF16), wide,
            in_vmem(queries), in_vmem(out_grad), in_vmem(gains),
        ),
        k_held, v_held, *in_hbm(queries, out_grad, gains),
        ins=[VMEM, VMEM, HBM, HBM, HBM],
        scratch=[pltpu.SemaphoreType.DMA((3,))],
        flops=4 * pairs,
    )
    attended, stats, prefix = call(
        functools.partial(attend_body, heads, factor, group),
        (wide, sds((2, tokens), F32), sds((width, HEAD), F32)),
        q_held, og_held, gain_held, local, *prefix,
    )
    every = from_all(stats, "tp")
    normed, grad_attn, *updates = call(
        functools.partial(grad_body, heads, features, group, len(every)),
        (pltpu.VMEM((tokens, width), BF16), half, *pieces),
        attended, og_held, gain_held, q_held, *every,
        scratch=[state],
    )
    suffix = carried_in(updates, True, state)
    normed, grad_q, gk_part, gv_part = call(
        functools.partial(local_body, heads, factor),
        (half, half, wide, wide),
        grad_attn, q_held, k_held, v_held, prefix, scores, normed,
        flops=9 * pairs,
    )
    held = pltpu.VMEM((tokens, width), BF16)
    grad_k, grad_v = call(
        functools.partial(final_body, heads, factor, group),
        (half, half),
        k_held, v_held, gk_part, gv_part, *suffix,
        dests=(HBM, HBM),
        scratch=[state, held, held, pltpu.SemaphoreType.DMA((2 * heads,))],
    )
    return normed, grad_q, grad_k, grad_v


def solution(mesh):
    placed = (P("ctx", "tp"), P("ctx", "tp"), P("ctx", "tp"), P("tp"), P("ctx", "tp"))
    return jax.shard_map(
        on_device,
        mesh=mesh,
        in_specs=placed,
        out_specs=(P("ctx", "tp"), P("ctx", "tp"), P("ctx", "tp"), P("ctx", "tp")),
        check_vma=False,
    )
```

profile of v0, /device:TPU:0, one launch (start us, length us, event | category | flops | bytes accessed | tf_op | source)
XLA Modules:
  0.0 40.8 jit_solution(9768949946219396092)
XLA Ops:
  0.6 1.3 %shard_map.84 = (bf16[256,256]{1,0:T(8,128)(2,1)S(1)}, bf16[256,256]{1,0:T(8,128)(2,1)S(1)}, f32[64,128]{1,0:T(8,128)S(1)}, f32[64,128]{1,0:T(8,128)S(1)}, f32[6...) custom-call(bf16[256,256]{1,0:T(8,128)(2,1)} %k_hbm.1, ...), custom_call_target="tpu_custom_call" | custom-call | flops 10000000 | bytes 262144 | tf_op jit(solution)/shard_map/pallas_call | solution.py:31
  2.0 3.5 %collective-permute-start = (f32[64,128]{1,0:T(8,128)S(1)}, f32[64,128]{1,0:T(8,128)S(1)}, u32[]{:S(2)}, u32[]{:S(2)}) collective-permute-start(f32[64,128]{1,0:T(8,128)S(1)} %get-tuple-element.59), channel_id=1, source_target_pairs={{0,13},{1,12},{2,15},{3,14},{4,9},{5,8},{6,11},{7,10},{8,5},{9,4},... | collective-permute-start | bytes 98312 | tf_op jit(solution)/shard_map/ppermute | solution.py:235
  5.4 0.7 %collective-permute-start.1 = (f32[64,128]{1,0:T(8,128)S(1)}, f32[64,128]{1,0:T(8,128)S(1)}, u32[]{:S(2)}, u32[]{:S(2)}) collective-permute-start(f32[64,128]{1,0:T(8,128)S(1)} %get-tuple-element.60), channel_id=1, source_target_pairs={{0,9},{1,8},{2,11},{3,10},{4,13},{5,12},{6,15},{7,14},{8,1},{9,0},... | collective-permute-start | bytes 98312 | tf_op jit(solution)/shard_map/ppermute | solution.py:235
  6.4 0.5 %collective-permute-start.8 = (f32[64,128]{1,0:T(8,128)S(1)}, f32[64,128]{1,0:T(8,128)S(1)}, u32[]{:S(2)}, u32[]{:S(2)}) collective-permute-start(f32[64,128]{1,0:T(8,128)S(1)} %get-tuple-element.67), channel_id=1, source_target_pairs={{0,1},{1,0},{2,3},{3,2},{4,5},{5,4},{6,7},{7,6},{8,9},{9,8},{10,11... | collective-permute-start | bytes 98312 | tf_op jit(solution)/shard_map/ppermute | solution.py:235
  7.2 0.5 %collective-permute-start.9 = (f32[64,128]{1,0:T(8,128)S(1)}, f32[64,128]{1,0:T(8,128)S(1)}, u32[]{:S(2)}, u32[]{:S(2)}) collective-permute-start(f32[64,128]{1,0:T(8,128)S(1)} %get-tuple-element.68), channel_id=1, source_target_pairs={{0,1},{1,0},{2,3},{3,2},{4,5},{5,4},{6,7},{7,6},{8,9},{9,8},{10,11... | collective-permute-start | bytes 98312 | tf_op jit(solution)/shard_map/ppermute | solution.py:235
  7.7 1.1 %collective-permute-done.1.refs_1_ = f32[64,128]{1,0:T(8,128)S(1)} collective-permute-done((f32[64,128]{1,0:T(8,128)S(1)}, f32[64,128]{1,0:T(8,128)S(1)}, u32[]{:S(2)}, u32[]{:S(2)}) %collective-permute-start.1) | collective-permute-done | bytes 32800 | tf_op jit(solution)/shard_map/ppermute | solution.py:235
  8.8 1.0 %collective-permute-start.10 = (f32[64,128]{1,0:T(8,128)S(1)}, f32[64,128]{1,0:T(8,128)S(1)}, u32[]{:S(2)}, u32[]{:S(2)}) collective-permute-start(f32[64,128]{1,0:T(8,128)S(1)} %get-tuple-element.69), channel_id=1, source_target_pairs={{0,1},{1,0},{2,3},{3,2},{4,5},{5,4},{6,7},{7,6},{8,9},{9,8},{10,11... | collective-permute-start | bytes 98312 | tf_op jit(solution)/shard_map/ppermute | solution.py:235
  9.8 0.4 collective-permute-start.11
  10.2 2.2 %collective-permute-start.4 = (f32[64,128]{1,0:T(8,128)S(1)}, f32[64,128]{1,0:T(8,128)S(1)}, u32[]{:S(2)}, u32[]{:S(2)}) collective-permute-start(f32[64,128]{1,0:T(8,128)S(1)} %get-tuple-element.63), channel_id=1, source_target_pairs={{0,13},{1,12},{2,15},{3,14},{4,9},{5,8},{6,11},{7,10},{8,5},{9,4},... | collective-permute-start | bytes 98312 | tf_op jit(solution)/shard_map/ppermute | solution.py:235
  12.4 0.4 collective-permute-start.5
  13.1 0.4 %collective-permute-start.7 = (f32[64,128]{1,0:T(8,128)S(1)}, f32[64,128]{1,0:T(8,128)S(1)}, u32[]{:S(2)}, u32[]{:S(2)}) collective-permute-start(f32[64,128]{1,0:T(8,128)S(1)} %get-tuple-element.66), channel_id=1, source_target_pairs={{0,1},{1,0},{2,3},{3,2},{4,5},{5,4},{6,7},{7,6},{8,9},{9,8},{10,11... | collective-permute-start | bytes 98312 | tf_op jit(solution)/shard_map/ppermute | solution.py:235
  13.5 1.2 %collective-permute-done.11.refs_4_ = f32[64,128]{1,0:T(8,128)S(1)} collective-permute-done((f32[64,128]{1,0:T(8,128)S(1)}, f32[64,128]{1,0:T(8,128)S(1)}, u32[]{:S(2)}, u32[]{:S(2)}) %collective-permute-start.11) | collective-permute-done | bytes 32800 | tf_op jit(solution)/shard_map/ppermute | solution.py:272
  15.0 0.4 collective-permute-start.13
  15.7 0.5 %collective-permute-start.14 = (f32[64,128]{1,0:T(8,128)S(1)}, f32[64,128]{1,0:T(8,128)S(1)}, u32[]{:S(2)}, u32[]{:S(2)}) collective-permute-start(f32[64,128]{1,0:T(8,128)S(1)} %get-tuple-element.74), channel_id=1, source_target_pairs={{0,1},{1,0},{2,3},{3,2},{4,5},{5,4},{6,7},{7,6},{8,9},{9,8},{10,11... | collective-permute-start | bytes 98312 | tf_op jit(solution)/shard_map/ppermute | solution.py:235
  16.3 1.5 %shard_map.85 = (bf16[2,256,256]{2,1,0:T(8,128)(2,1)S(1)}, f32[256,256]{1,0:T(8,128)S(1)}, bf16[256,256]{1,0:T(8,128)(2,1)S(1)}, bf16[256,256]{1,0:T(8,128)(2,1)S(1)}, f32[2,128]{1,0:T(2,128)S(1)}) custom-call(bf16[256,256]{1,0:T(8,128)(2,1)S(1)} %get-tuple-element.53.k, bf16[256,256]{1,0:T(8,128)(2,1)S(1)} %get-tuple-element.54.v, bf16[256,256]{1,0:T(8,128)(2,1)} %q_hbm.1, ...), custom_call_target="tpu_custom_call" | custom-call | flops 67108864 | bytes 525312 | tf_op jit(solution)/shard_map/pallas_call | solution.py:31
  18.2 1.6 %collective-permute-start.18 = (f32[2,256]{1,0:T(2,128)S(1)}, f32[2,256]{1,0:T(2,128)S(1)}, u32[]{:S(2)}, u32[]{:S(2)}) collective-permute-start(f32[2,256]{1,0:T(2,128)S(1)} %get-tuple-element.77.refs_0_), channel_id=1, source_target_pairs={{0,2},{1,3},{2,0},{3,1},{4,6},{5,7},{6,4},{7,5},{8,10},{9,11},{10,... | collective-permute-start | bytes 6152 | tf_op jit(solution)/shard_map/ppermute | solution.py:290
  20.4 1.4 %collective-permute-done.18.refs_3_ = f32[2,256]{1,0:T(2,128)S(1)} collective-permute-done((f32[2,256]{1,0:T(2,128)S(1)}, f32[2,256]{1,0:T(2,128)S(1)}, u32[]{:S(2)}, u32[]{:S(2)}) %collective-permute-start.18) | collective-permute-done | bytes 2080 | tf_op jit(solution)/shard_map/ppermute | solution.py:290
  21.8 0.9 %collective-permute-done.17.refs_2_ = f32[2,256]{1,0:T(2,128)S(1)} collective-permute-done((f32[2,256]{1,0:T(2,128)S(1)}, f32[2,256]{1,0:T(2,128)S(1)}, u32[]{:S(2)}, u32[]{:S(2)}) %collective-permute-start.17) | collective-permute-done | bytes 2080 | tf_op jit(solution)/shard_map/ppermute | solution.py:290
  23.1 1.5 %collective-permute-start.19 = (f32[64,128]{1,0:T(8,128)S(1)}, f32[64,128]{1,0:T(8,128)S(1)}, u32[]{:S(2)}, u32[]{:S(2)}) collective-permute-start(f32[64,128]{1,0:T(8,128)S(1)} %get-tuple-element.86), channel_id=1, source_target_pairs={{0,13},{1,12},{2,15},{3,14},{4,9},{5,8},{6,11},{7,10},{8,5},{9,4},... | collective-permute-start | bytes 98312 | tf_op jit(solution)/shard_map/ppermute | solution.py:235
  24.6 0.8 %collective-permute-start.20 = (f32[64,128]{1,0:T(8,128)S(1)}, f32[64,128]{1,0:T(8,128)S(1)}, u32[]{:S(2)}, u32[]{:S(2)}) collective-permute-start(f32[64,128]{1,0:T(8,128)S(1)} %get-tuple-element.87), channel_id=1, source_target_pairs={{0,9},{1,8},{2,11},{3,10},{4,13},{5,12},{6,15},{7,14},{8,1},{9,0},... | collective-permute-start | bytes 98312 | tf_op jit(solution)/shard_map/ppermute | solution.py:235
  25.4 0.8 %collective-permute-start.21 = (f32[64,128]{1,0:T(8,128)S(1)}, f32[64,128]{1,0:T(8,128)S(1)}, u32[]{:S(2)}, u32[]{:S(2)}) collective-permute-start(f32[64,128]{1,0:T(8,128)S(1)} %get-tuple-element.88), channel_id=1, source_target_pairs={{0,5},{1,4},{2,7},{3,6},{4,1},{5,0},{6,3},{7,2},{8,13},{9,12},{10,... | collective-permute-start | bytes 98312 | tf_op jit(solution)/shard_map/ppermute | solution.py:235
  26.5 0.9 %collective-permute-done.19.refs_0_ = f32[64,128]{1,0:T(8,128)S(1)} collective-permute-done((f32[64,128]{1,0:T(8,128)S(1)}, f32[64,128]{1,0:T(8,128)S(1)}, u32[]{:S(2)}, u32[]{:S(2)}) %collective-permute-start.19) | collective-permute-done | bytes 32800 | tf_op jit(solution)/shard_map/ppermute | solution.py:235
  27.4 0.5 %collective-permute-done.20.refs_1_ = f32[64,128]{1,0:T(8,128)S(1)} collective-permute-done((f32[64,128]{1,0:T(8,128)S(1)}, f32[64,128]{1,0:T(8,128)S(1)}, u32[]{:S(2)}, u32[]{:S(2)}) %collective-permute-start.20) | collective-permute-done | bytes 32800 | tf_op jit(solution)/shard_map/ppermute | solution.py:235
  27.9 0.9 %collective-permute-done.21.refs_2_ = f32[64,128]{1,0:T(8,128)S(1)} collective-permute-done((f32[64,128]{1,0:T(8,128)S(1)}, f32[64,128]{1,0:T(8,128)S(1)}, u32[]{:S(2)}, u32[]{:S(2)}) %collective-permute-start.21) | collective-permute-done | bytes 32800 | tf_op jit(solution)/shard_map/ppermute | solution.py:235
  28.9 3.0 %collective-permute-start.23 = (f32[64,128]{1,0:T(8,128)S(1)}, f32[64,128]{1,0:T(8,128)S(1)}, u32[]{:S(2)}, u32[]{:S(2)}) collective-permute-start(f32[64,128]{1,0:T(8,128)S(1)} %get-tuple-element.91), channel_id=1, source_target_pairs={{0,16},{4,20},{8,24},{12,28},{16,0},{20,4},{24,8},{28,12},{1,17},{... | collective-permute-start | bytes 98312 | tf_op jit(solution)/shard_map/ppermute | solution.py:272
  32.9 1.0 %collective-permute-done.23.over = f32[64,128]{1,0:T(8,128)S(1)} collective-permute-done((f32[64,128]{1,0:T(8,128)S(1)}, f32[64,128]{1,0:T(8,128)S(1)}, u32[]{:S(2)}, u32[]{:S(2)}) %collective-permute-start.23) | collective-permute-done | bytes 32800 | tf_op jit(solution)/shard_map/ppermute | solution.py:272
  33.9 1.8 %collective-permute-start.24 = (f32[64,128]{1,0:T(8,128)S(1)}, f32[64,128]{1,0:T(8,128)S(1)}, u32[]{:S(2)}, u32[]{:S(2)}) collective-permute-start(f32[64,128]{1,0:T(8,128)S(1)} %get-tuple-element.92), channel_id=1, source_target_pairs={{0,13},{1,12},{2,15},{3,14},{4,9},{5,8},{6,11},{7,10},{8,5},{9,4},... | collective-permute-start | bytes 98312 | tf_op jit(solution)/shard_map/ppermute | solution.py:235
  35.7 0.8 %collective-permute-start.25 = (f32[64,128]{1,0:T(8,128)S(1)}, f32[64,128]{1,0:T(8,128)S(1)}, u32[]{:S(2)}, u32[]{:S(2)}) collective-permute-start(f32[64,128]{1,0:T(8,128)S(1)} %get-tuple-element.93), channel_id=1, source_target_pairs={{0,9},{1,8},{2,11},{3,10},{4,13},{5,12},{6,15},{7,14},{8,1},{9,0},... | collective-permute-start | bytes 98312 | tf_op jit(solution)/shard_map/ppermute | solution.py:235
  36.6 0.8 %collective-permute-start.26 = (f32[64,128]{1,0:T(8,128)S(1)}, f32[64,128]{1,0:T(8,128)S(1)}, u32[]{:S(2)}, u32[]{:S(2)}) collective-permute-start(f32[64,128]{1,0:T(8,128)S(1)} %get-tuple-element.94), channel_id=1, source_target_pairs={{0,5},{1,4},{2,7},{3,6},{4,1},{5,0},{6,3},{7,2},{8,13},{9,12},{10,... | collective-permute-start | bytes 98312 | tf_op jit(solution)/shard_map/ppermute | solution.py:235
  37.4 1.3 %shard_map.90 = (bf16[256,256]{1,0:T(8,128)(2,1)}, bf16[256,256]{1,0:T(8,128)(2,1)}, f32[256,256]{1,0:T(8,128)S(1)}, f32[256,256]{1,0:T(8,128)S(1)}) custom-call(bf16[256,256]{1,0:T(8,128)(2,1)S(1)} %get-tuple-element.78.ga, bf16[256,256]{1,0:T(8,128)(2,1)S(1)} %get-tuple-element.55.q, bf16[256,256]{1,0:T(8,128)(2,1)S(1)} %get-tuple-element.53.k, ...), custom_call_target="tpu_custom_call" | custom-call | flops 150994944 | bytes 1048576 | tf_op jit(solution)/shard_map/pallas_call | solution.py:31
  39.0 0.8 %collective-permute-done.26.refs_2_ = f32[64,128]{1,0:T(8,128)S(1)} collective-permute-done((f32[64,128]{1,0:T(8,128)S(1)}, f32[64,128]{1,0:T(8,128)S(1)}, u32[]{:S(2)}, u32[]{:S(2)}) %collective-permute-start.26) | collective-permute-done | bytes 32800 | tf_op jit(solution)/shard_map/ppermute | solution.py:235
  39.9 0.9 %shard_map.93 = (bf16[256,256]{1,0:T(8,128)(2,1)}, bf16[256,256]{1,0:T(8,128)(2,1)}) custom-call(bf16[256,256]{1,0:T(8,128)(2,1)S(1)} %get-tuple-element.53.k, bf16[256,256]{1,0:T(8,128)(2,1)S(1)} %get-tuple-element.54.v, f32[256,256]{1,0:T(8,128)S(1)} %get-tuple-element.84.gk_part, f32[256,256]{1,0:T(8,128)S(1)} %get-tuple-element.85.gv_part, ...), custom_call_target="tpu_custom_call" | custom-call | flops 10000000 | bytes 1048576 | tf_op jit(solution)/shard_map/pallas_call | solution.py:31
  (42 shorter events, 4.6 us)
Async XLA Ops:
  2.0 5.2 %collective-permute-start = (f32[64,128]{1,0:T(8,128)S(1)}, f32[64,128]{1,0:T(8,128)S(1)}, u32[]{:S(2)}, u32[]{:S(2)}) collective-permute-start(f32[64,128]{1,0:T(8,128)S(1)} %get-tuple-element.59), channel_id=1, source_target_pairs={{0,13},{1,12},{2,15},{3,14},{4,9},{5,8},{6,11},{7,10},{8,5},{9,4},... | collective-permute-start | bytes 98312 | tf_op jit(solution)/shard_map/ppermute | solution.py:235
  5.4 3.3 %collective-permute-start.1 = (f32[64,128]{1,0:T(8,128)S(1)}, f32[64,128]{1,0:T(8,128)S(1)}, u32[]{:S(2)}, u32[]{:S(2)}) collective-permute-start(f32[64,128]{1,0:T(8,128)S(1)} %get-tuple-element.60), channel_id=1, source_target_pairs={{0,9},{1,8},{2,11},{3,10},{4,13},{5,12},{6,15},{7,14},{8,1},{9,0},... | collective-permute-start | bytes 98312 | tf_op jit(solution)/shard_map/ppermute | solution.py:235
  6.2 3.6 %collective-permute-start.2 = (f32[64,128]{1,0:T(8,128)S(1)}, f32[64,128]{1,0:T(8,128)S(1)}, u32[]{:S(2)}, u32[]{:S(2)}) collective-permute-start(f32[64,128]{1,0:T(8,128)S(1)} %get-tuple-element.61), channel_id=1, source_target_pairs={{0,5},{1,4},{2,7},{3,6},{4,1},{5,0},{6,3},{7,2},{8,13},{9,12},{10,... | collective-permute-start | bytes 98312 | tf_op jit(solution)/shard_map/ppermute | solution.py:235
  6.4 3.4 %collective-permute-start.3 = (f32[64,128]{1,0:T(8,128)S(1)}, f32[64,128]{1,0:T(8,128)S(1)}, u32[]{:S(2)}, u32[]{:S(2)}) collective-permute-start(f32[64,128]{1,0:T(8,128)S(1)} %get-tuple-element.62), channel_id=1, source_target_pairs={{0,1},{1,0},{2,3},{3,2},{4,5},{5,4},{6,7},{7,6},{8,9},{9,8},{10,11... | collective-permute-start | bytes 98312 | tf_op jit(solution)/shard_map/ppermute | solution.py:235
  6.4 6.0 %collective-permute-start.8 = (f32[64,128]{1,0:T(8,128)S(1)}, f32[64,128]{1,0:T(8,128)S(1)}, u32[]{:S(2)}, u32[]{:S(2)}) collective-permute-start(f32[64,128]{1,0:T(8,128)S(1)} %get-tuple-element.67), channel_id=1, source_target_pairs={{0,1},{1,0},{2,3},{3,2},{4,5},{5,4},{6,7},{7,6},{8,9},{9,8},{10,11... | collective-permute-start | bytes 98312 | tf_op jit(solution)/shard_map/ppermute | solution.py:235
  7.2 5.6 %collective-permute-start.9 = (f32[64,128]{1,0:T(8,128)S(1)}, f32[64,128]{1,0:T(8,128)S(1)}, u32[]{:S(2)}, u32[]{:S(2)}) collective-permute-start(f32[64,128]{1,0:T(8,128)S(1)} %get-tuple-element.68), channel_id=1, source_target_pairs={{0,1},{1,0},{2,3},{3,2},{4,5},{5,4},{6,7},{7,6},{8,9},{9,8},{10,11... | collective-permute-start | bytes 98312 | tf_op jit(solution)/shard_map/ppermute | solution.py:235
  8.8 4.3 %collective-permute-start.10 = (f32[64,128]{1,0:T(8,128)S(1)}, f32[64,128]{1,0:T(8,128)S(1)}, u32[]{:S(2)}, u32[]{:S(2)}) collective-permute-start(f32[64,128]{1,0:T(8,128)S(1)} %get-tuple-element.69), channel_id=1, source_target_pairs={{0,1},{1,0},{2,3},{3,2},{4,5},{5,4},{6,7},{7,6},{8,9},{9,8},{10,11... | collective-permute-start | bytes 98312 | tf_op jit(solution)/shard_map/ppermute | solution.py:235
  9.8 5.0 %collective-permute-start.11 = (f32[64,128]{1,0:T(8,128)S(1)}, f32[64,128]{1,0:T(8,128)S(1)}, u32[]{:S(2)}, u32[]{:S(2)}) collective-permute-start(f32[64,128]{1,0:T(8,128)S(1)} %get-tuple-element.71), channel_id=1, source_target_pairs={{0,16},{4,20},{8,24},{12,28},{16,0},{20,4},{24,8},{28,12},{1,17},{... | collective-permute-start | bytes 98312 | tf_op jit(solution)/shard_map/ppermute | solution.py:272
  10.2 4.8 %collective-permute-start.4 = (f32[64,128]{1,0:T(8,128)S(1)}, f32[64,128]{1,0:T(8,128)S(1)}, u32[]{:S(2)}, u32[]{:S(2)}) collective-permute-start(f32[64,128]{1,0:T(8,128)S(1)} %get-tuple-element.63), channel_id=1, source_target_pairs={{0,13},{1,12},{2,15},{3,14},{4,9},{5,8},{6,11},{7,10},{8,5},{9,4},... | collective-permute-start | bytes 98312 | tf_op jit(solution)/shard_map/ppermute | solution.py:235
  12.4 3.3 %collective-permute-start.5 = (f32[64,128]{1,0:T(8,128)S(1)}, f32[64,128]{1,0:T(8,128)S(1)}, u32[]{:S(2)}, u32[]{:S(2)}) collective-permute-start(f32[64,128]{1,0:T(8,128)S(1)} %get-tuple-element.64), channel_id=1, source_target_pairs={{0,9},{1,8},{2,11},{3,10},{4,13},{5,12},{6,15},{7,14},{8,1},{9,0},... | collective-permute-start | bytes 98312 | tf_op jit(solution)/shard_map/ppermute | solution.py:235
  12.8 3.5 %collective-permute-start.6 = (f32[64,128]{1,0:T(8,128)S(1)}, f32[64,128]{1,0:T(8,128)S(1)}, u32[]{:S(2)}, u32[]{:S(2)}) collective-permute-start(f32[64,128]{1,0:T(8,128)S(1)} %get-tuple-element.65), channel_id=1, source_target_pairs={{0,5},{1,4},{2,7},{3,6},{4,1},{5,0},{6,3},{7,2},{8,13},{9,12},{10,... | collective-permute-start | bytes 98312 | tf_op jit(solution)/shard_map/ppermute | solution.py:235
  13.1 4.7 %collective-permute-start.7 = (f32[64,128]{1,0:T(8,128)S(1)}, f32[64,128]{1,0:T(8,128)S(1)}, u32[]{:S(2)}, u32[]{:S(2)}) collective-permute-start(f32[64,128]{1,0:T(8,128)S(1)} %get-tuple-element.66), channel_id=1, source_target_pairs={{0,1},{1,0},{2,3},{3,2},{4,5},{5,4},{6,7},{7,6},{8,9},{9,8},{10,11... | collective-permute-start | bytes 98312 | tf_op jit(solution)/shard_map/ppermute | solution.py:235
  14.8 3.0 %collective-permute-start.12 = (f32[64,128]{1,0:T(8,128)S(1)}, f32[64,128]{1,0:T(8,128)S(1)}, u32[]{:S(2)}, u32[]{:S(2)}) collective-permute-start(f32[64,128]{1,0:T(8,128)S(1)} %get-tuple-element.72), channel_id=1, source_target_pairs={{0,1},{1,0},{2,3},{3,2},{4,5},{5,4},{6,7},{7,6},{8,9},{9,8},{10,11... | collective-permute-start | bytes 98312 | tf_op jit(solution)/shard_map/ppermute | solution.py:235
  15.0 2.8 %collective-permute-start.13 = (f32[64,128]{1,0:T(8,128)S(1)}, f32[64,128]{1,0:T(8,128)S(1)}, u32[]{:S(2)}, u32[]{:S(2)}) collective-permute-start(f32[64,128]{1,0:T(8,128)S(1)} %get-tuple-element.73), channel_id=1, source_target_pairs={{0,1},{1,0},{2,3},{3,2},{4,5},{5,4},{6,7},{7,6},{8,9},{9,8},{10,11... | collective-permute-start | bytes 98312 | tf_op jit(solution)/shard_map/ppermute | solution.py:235
  15.7 2.1 %collective-permute-start.14 = (f32[64,128]{1,0:T(8,128)S(1)}, f32[64,128]{1,0:T(8,128)S(1)}, u32[]{:S(2)}, u32[]{:S(2)}) collective-permute-start(f32[64,128]{1,0:T(8,128)S(1)} %get-tuple-element.74), channel_id=1, source_target_pairs={{0,1},{1,0},{2,3},{3,2},{4,5},{5,4},{6,7},{7,6},{8,9},{9,8},{10,11... | collective-permute-start | bytes 98312 | tf_op jit(solution)/shard_map/ppermute | solution.py:235
  16.3 1.6 %collective-permute-start.15 = (f32[64,128]{1,0:T(8,128)S(1)}, f32[64,128]{1,0:T(8,128)S(1)}, u32[]{:S(2)}, u32[]{:S(2)}) collective-permute-start(f32[64,128]{1,0:T(8,128)S(1)} %get-tuple-element.75), channel_id=1, source_target_pairs={{0,1},{1,0},{2,3},{3,2},{4,5},{5,4},{6,7},{7,6},{8,9},{9,8},{10,11... | collective-permute-start | bytes 98312 | tf_op jit(solution)/shard_map/ppermute | solution.py:235
  18.2 3.7 %collective-permute-start.18 = (f32[2,256]{1,0:T(2,128)S(1)}, f32[2,256]{1,0:T(2,128)S(1)}, u32[]{:S(2)}, u32[]{:S(2)}) collective-permute-start(f32[2,256]{1,0:T(2,128)S(1)} %get-tuple-element.77.refs_0_), channel_id=1, source_target_pairs={{0,2},{1,3},{2,0},{3,1},{4,6},{5,7},{6,4},{7,5},{8,10},{9,11},{10,... | collective-permute-start | bytes 6152 | tf_op jit(solution)/shard_map/ppermute | solution.py:290
  19.8 3.0 %collective-permute-start.17 = (f32[2,256]{1,0:T(2,128)S(1)}, f32[2,256]{1,0:T(2,128)S(1)}, u32[]{:S(2)}, u32[]{:S(2)}) collective-permute-start(f32[2,256]{1,0:T(2,128)S(1)} %get-tuple-element.77.refs_0_), channel_id=1, source_target_pairs={{0,3},{1,2},{2,1},{3,0},{4,7},{5,6},{6,5},{7,4},{8,11},{9,10},{10,... | collective-permute-start | bytes 6152 | tf_op jit(solution)/shard_map/ppermute | solution.py:290
  20.0 2.7 %collective-permute-start.16 = (f32[2,256]{1,0:T(2,128)S(1)}, f32[2,256]{1,0:T(2,128)S(1)}, u32[]{:S(2)}, u32[]{:S(2)}) collective-permute-start(f32[2,256]{1,0:T(2,128)S(1)} %get-tuple-element.77.refs_0_), channel_id=1, source_target_pairs={{0,1},{1,0},{2,3},{3,2},{4,5},{5,4},{6,7},{7,6},{8,9},{9,8},{10,11... | collective-permute-start | bytes 6152 | tf_op jit(solution)/shard_map/ppermute | solution.py:290
  23.1 4.3 %collective-permute-start.19 = (f32[64,128]{1,0:T(8,128)S(1)}, f32[64,128]{1,0:T(8,128)S(1)}, u32[]{:S(2)}, u32[]{:S(2)}) collective-permute-start(f32[64,128]{1,0:T(8,128)S(1)} %get-tuple-element.86), channel_id=1, source_target_pairs={{0,13},{1,12},{2,15},{3,14},{4,9},{5,8},{6,11},{7,10},{8,5},{9,4},... | collective-permute-start | bytes 98312 | tf_op jit(solution)/shard_map/ppermute | solution.py:235
  24.6 3.3 %collective-permute-start.20 = (f32[64,128]{1,0:T(8,128)S(1)}, f32[64,128]{1,0:T(8,128)S(1)}, u32[]{:S(2)}, u32[]{:S(2)}) collective-permute-start(f32[64,128]{1,0:T(8,128)S(1)} %get-tuple-element.87), channel_id=1, source_target_pairs={{0,9},{1,8},{2,11},{3,10},{4,13},{5,12},{6,15},{7,14},{8,1},{9,0},... | collective-permute-start | bytes 98312 | tf_op jit(solution)/shard_map/ppermute | solution.py:235
  25.4 3.4 %collective-permute-start.21 = (f32[64,128]{1,0:T(8,128)S(1)}, f32[64,128]{1,0:T(8,128)S(1)}, u32[]{:S(2)}, u32[]{:S(2)}) collective-permute-start(f32[64,128]{1,0:T(8,128)S(1)} %get-tuple-element.88), channel_id=1, source_target_pairs={{0,5},{1,4},{2,7},{3,6},{4,1},{5,0},{6,3},{7,2},{8,13},{9,12},{10,... | collective-permute-start | bytes 98312 | tf_op jit(solution)/shard_map/ppermute | solution.py:235
  26.2 2.6 %collective-permute-start.22 = (f32[64,128]{1,0:T(8,128)S(1)}, f32[64,128]{1,0:T(8,128)S(1)}, u32[]{:S(2)}, u32[]{:S(2)}) collective-permute-start(f32[64,128]{1,0:T(8,128)S(1)} %get-tuple-element.89), channel_id=1, source_target_pairs={{0,1},{1,0},{2,3},{3,2},{4,5},{5,4},{6,7},{7,6},{8,9},{9,8},{10,11... | collective-permute-start | bytes 98312 | tf_op jit(solution)/shard_map/ppermute | solution.py:235
  28.9 5.0 %collective-permute-start.23 = (f32[64,128]{1,0:T(8,128)S(1)}, f32[64,128]{1,0:T(8,128)S(1)}, u32[]{:S(2)}, u32[]{:S(2)}) collective-permute-start(f32[64,128]{1,0:T(8,128)S(1)} %get-tuple-element.91), channel_id=1, source_target_pairs={{0,16},{4,20},{8,24},{12,28},{16,0},{20,4},{24,8},{28,12},{1,17},{... | collective-permute-start | bytes 98312 | tf_op jit(solution)/shard_map/ppermute | solution.py:272
  31.9 3.8 %collective-permute-start.28 = (f32[64,128]{1,0:T(8,128)S(1)}, f32[64,128]{1,0:T(8,128)S(1)}, u32[]{:S(2)}, u32[]{:S(2)}) collective-permute-start(f32[64,128]{1,0:T(8,128)S(1)} %get-tuple-element.96), channel_id=1, source_target_pairs={{0,1},{1,0},{2,3},{3,2},{4,5},{5,4},{6,7},{7,6},{8,9},{9,8},{10,11... | collective-permute-start | bytes 98312 | tf_op jit(solution)/shard_map/ppermute | solution.py:235
  32.1 4.5 %collective-permute-start.29 = (f32[64,128]{1,0:T(8,128)S(1)}, f32[64,128]{1,0:T(8,128)S(1)}, u32[]{:S(2)}, u32[]{:S(2)}) collective-permute-start(f32[64,128]{1,0:T(8,128)S(1)} %get-tuple-element.97), channel_id=1, source_target_pairs={{0,1},{1,0},{2,3},{3,2},{4,5},{5,4},{6,7},{7,6},{8,9},{9,8},{10,11... | collective-permute-start | bytes 98312 | tf_op jit(solution)/shard_map/ppermute | solution.py:235
  32.4 5.0 %collective-permute-start.30 = (f32[64,128]{1,0:T(8,128)S(1)}, f32[64,128]{1,0:T(8,128)S(1)}, u32[]{:S(2)}, u32[]{:S(2)}) collective-permute-start(f32[64,128]{1,0:T(8,128)S(1)} %get-tuple-element.98), channel_id=1, source_target_pairs={{0,1},{1,0},{2,3},{3,2},{4,5},{5,4},{6,7},{7,6},{8,9},{9,8},{10,11... | collective-permute-start | bytes 98312 | tf_op jit(solution)/shard_map/ppermute | solution.py:235
  32.6 6.1 %collective-permute-start.31 = (f32[64,128]{1,0:T(8,128)S(1)}, f32[64,128]{1,0:T(8,128)S(1)}, u32[]{:S(2)}, u32[]{:S(2)}) collective-permute-start(f32[64,128]{1,0:T(8,128)S(1)} %get-tuple-element.99), channel_id=1, source_target_pairs={{0,1},{1,0},{2,3},{3,2},{4,5},{5,4},{6,7},{7,6},{8,9},{9,8},{10,11... | collective-permute-start | bytes 98312 | tf_op jit(solution)/shard_map/ppermute | solution.py:235
  33.9 4.8 %collective-permute-start.24 = (f32[64,128]{1,0:T(8,128)S(1)}, f32[64,128]{1,0:T(8,128)S(1)}, u32[]{:S(2)}, u32[]{:S(2)}) collective-permute-start(f32[64,128]{1,0:T(8,128)S(1)} %get-tuple-element.92), channel_id=1, source_target_pairs={{0,13},{1,12},{2,15},{3,14},{4,9},{5,8},{6,11},{7,10},{8,5},{9,4},... | collective-permute-start | bytes 98312 | tf_op jit(solution)/shard_map/ppermute | solution.py:235
  35.7 3.3 %collective-permute-start.25 = (f32[64,128]{1,0:T(8,128)S(1)}, f32[64,128]{1,0:T(8,128)S(1)}, u32[]{:S(2)}, u32[]{:S(2)}) collective-permute-start(f32[64,128]{1,0:T(8,128)S(1)} %get-tuple-element.93), channel_id=1, source_target_pairs={{0,9},{1,8},{2,11},{3,10},{4,13},{5,12},{6,15},{7,14},{8,1},{9,0},... | collective-permute-start | bytes 98312 | tf_op jit(solution)/shard_map/ppermute | solution.py:235
  36.6 3.3 %collective-permute-start.26 = (f32[64,128]{1,0:T(8,128)S(1)}, f32[64,128]{1,0:T(8,128)S(1)}, u32[]{:S(2)}, u32[]{:S(2)}) collective-permute-start(f32[64,128]{1,0:T(8,128)S(1)} %get-tuple-element.94), channel_id=1, source_target_pairs={{0,5},{1,4},{2,7},{3,6},{4,1},{5,0},{6,3},{7,2},{8,13},{9,12},{10,... | collective-permute-start | bytes 98312 | tf_op jit(solution)/shard_map/ppermute | solution.py:235
  37.4 2.5 %collective-permute-start.27 = (f32[64,128]{1,0:T(8,128)S(1)}, f32[64,128]{1,0:T(8,128)S(1)}, u32[]{:S(2)}, u32[]{:S(2)}) collective-permute-start(f32[64,128]{1,0:T(8,128)S(1)} %get-tuple-element.95), channel_id=1, source_target_pairs={{0,1},{1,0},{2,3},{3,2},{4,5},{5,4},{6,7},{7,6},{8,9},{9,8},{10,11... | collective-permute-start | bytes 98312 | tf_op jit(solution)/shard_map/ppermute | solution.py:235
where the time goes:
time: 41.2 us; the launch traced here: 40.8 us
  starting transfers between devices  24.2 us (59%)
  waiting for transfers between devices  9.94 us (24%)
  Pallas kernels  5.91 us (14%)
  between operations  0.75 us (2%)
    ppermute x27, starting transfers between devices, exchange(): lax.ppermute(piece, ('ctx', 'tp'), [(j * ways + t, (j ^ partner(i, group)...  18.6 us
    pallas_call x10, Pallas kernels, call(): pl.pallas_call(body, out_shape=outs, in_specs=ins or [VMEM] * len(args),...  5.91 us
    ppermute x27, waiting for transfers between devices, exchange(): lax.ppermute(piece, ('ctx', 'tp'), [(j * ways + t, (j ^ partner(i, group)...  5.35 us
    ppermute x2, starting transfers between devices, carried_in(): over = lax.ppermute(total, 'ctx', [(j, j ^ group) for j in both])  3.44 us
    ppermute x3, waiting for transfers between devices, from_all(): lax.ppermute(part, axis, [(i, i ^ step if even else (i + step) % count) f...  2.39 us
    ppermute x3, starting transfers between devices, from_all(): lax.ppermute(part, axis, [(i, i ^ step if even else (i + step) % count) f...  2.21 us
    ppermute x2, waiting for transfers between devices, carried_in(): over = lax.ppermute(total, 'ctx', [(j, j ^ group) for j in both])  2.2 us
  transfers between devices with their start and end apart: 32, of which 13 were waited for; matrix products, arithmetic and copies ran while one was open for 0% of the time, Pallas kernels for 7%

commit v1 on v0

--- a/solution.py
+++ b/solution.py
@@ -10,6 +10,8 @@
 HEAD = 128
 
 epsilon = 1e-06
+ALONE = (0, 2)
+SHARED = (1, 3)
 F32 = jnp.float32
 BF16 = jnp.bfloat16
 
@@ -96,14 +98,12 @@
 
 def states_body(heads, group, k_hbm, v_hbm, k, v, *refs):
     outs, (state, sems) = refs[:-2], refs[-2:]
-    parts = [(a.at[:, head(h)], b.at[:, head(h)]) for h in range(heads) for a, b in ((k_hbm, k), (v_hbm, v))]
-    copies = loads(parts, sems)
-    for h in range(heads):
-        copies[2 * h].wait()
-        copies[2 * h + 1].wait()
+    for copy in loads(((k_hbm, k), (v_hbm, v)), sems):
+        copy.wait()
+    for h in range(heads):
         state[head(h), :] = dot(k[:, head(h)], v[:, head(h)], TN)
     give(state, group, outs[:group])
-    for i, again in enumerate(outs[group:]):
+    for again, i in zip(outs[group:], ALONE):
         again[...] = outs[i][...]
 
 
@@ -119,7 +119,8 @@
     total[...] = running_sums(sums, group, reverse)
     give(sums, group, outs)
     if not reverse:
-        refs[-2][...] = arrived[-1][...]
+        for passed, i in zip(refs[2 * group + 1 : -1], SHARED):
+            passed[...] = arrived[i][...]
 
 
 def add_body(group, sums, over, *outs):
@@ -147,7 +148,7 @@
         rows[...] = jnp.where(early, pieces[i][...], pieces[many + i][...])
 
 
-def scores_body(heads, factor, k, v, q_hbm, og_hbm, gain_hbm, scores, attended, q, og, gain, sems):
+def scores_body(heads, factor, k, v, q_hbm, og_hbm, gain_hbm, scores, attended, q, weighted, gain, og, sems):
     copies = loads(((q_hbm, q), (og_hbm, og), (gain_hbm, gain)), sems)
     copies[0].wait()
     causal = causal_mask(q.shape[0])
@@ -158,9 +159,11 @@
         attended[:, head(h)] = dot(sc, v[:, head(h)], NN)
     for copy in copies[1:]:
         copy.wait()
-
-
-def attend_body(heads, factor, group, q, og, gain, local, *refs):
+    for h in range(heads):
+        weighted[:, head(h)] = og[:, head(h)].astype(F32) * gain[h : h + 1, :]
+
+
+def attend_body(heads, factor, group, q, weighted, local, *refs):
     pieces, (attended, stats, prefix) = refs[:-3], refs[-3:]
     pick(pieces, prefix, group)
     power = 0.0
@@ -168,15 +171,14 @@
     for h in range(heads):
         att = factor * dot(q[:, head(h)], prefix[head(h), :].astype(BF16), NN) + local[:, head(h)]
         attended[:, head(h)] = att
-        weighted = og[:, head(h)].astype(F32) * gain[h : h + 1, :]
         power = power + att * att
-        inner = inner + weighted * att
+        inner = inner + weighted[:, head(h)] * att
     stats[0:1, :] = jnp.sum(power.T, axis=0, keepdims=True)
     stats[1:2, :] = jnp.sum(inner.T, axis=0, keepdims=True)
 
 
-def grad_body(heads, features, group, ways, attended, og, gain, q, *refs):
-    stats, (normed, grad), outs, updates = refs[:ways], refs[ways : ways + 2], refs[ways + 2 : -1], refs[-1]
+def grad_body(heads, features, group, ways, attended, weighted, q, *refs):
+    stats, (spread, grad), outs, updates = refs[:ways], refs[ways : ways + 2], refs[ways + 2 : -1], refs[-1]
     total = stats[0][...]
     for other in stats[1:]:
         total = total + other[...]
@@ -185,21 +187,18 @@
     tokens = q.shape[0]
     inv_rms = jnp.broadcast_to(inv_rms, (HEAD, tokens)).T
     bend = jnp.broadcast_to(bend, (HEAD, tokens)).T
-    for h in range(heads):
-        att = attended[:, head(h)]
-        gain_h = gain[h : h + 1, :]
-        weighted = og[:, head(h)].astype(F32) * gain_h
-        ga = (inv_rms * (weighted - att * bend)).astype(BF16)
+    spread[...] = inv_rms
+    for h in range(heads):
+        ga = (inv_rms * (weighted[:, head(h)] - attended[:, head(h)] * bend)).astype(BF16)
         grad[:, head(h)] = ga
         updates[head(h), :] = dot(q[:, head(h)], ga, TN)
-        normed[:, head(h)] = (att * inv_rms * gain_h).astype(BF16)
     give(updates, group, outs)
 
 
-def local_body(heads, factor, ga, q, k, v, prefix, scores, normed, normed_out, gq, gk_part, gv_part):
-    normed_out[...] = normed[...]
+def local_body(heads, factor, ga, q, k, v, prefix, scores, attended, inv_rms, gain, normed, gq, gk_part, gv_part):
     causal = causal_mask(q.shape[0])
     for h in range(heads):
+        normed[:, head(h)] = (attended[:, head(h)] * inv_rms[...] * gain[h : h + 1, :]).astype(BF16)
         gah = ga[:, head(h)]
         raw = dot(gah, v[:, head(h)], NT) * factor
         gs = jnp.where(causal, raw, 0.0).astype(BF16)
@@ -229,25 +228,20 @@
         copy.wait()
 
 
-def exchange(pieces, active, group):
+def exchange(piece, i, active, group):
     ways = lax.axis_size("tp")
-    return [
-        lax.ppermute(
-            piece,
-            ("ctx", "tp"),
-            [
-                (j * ways + t, (j ^ partner(i, group) if j in active else j) * ways + (t ^ 1))
-                for j in range(2 * group)
-                for t in range(ways)
-            ],
-        )
-        for i, piece in enumerate(pieces)
+    pairs = [
+        (j * ways + t, (j ^ partner(i, group) if j in active else j) * ways + (t ^ 1))
+        for j in range(2 * group)
+        for t in range(ways)
     ]
+    return lax.ppermute(piece, ("ctx", "tp"), pairs)
 
 
 def carried_in(pieces, reverse, state):
-    group = len(pieces) if reverse else (len(pieces) + 1) // 2
-    pieces, again = pieces[:group], pieces[group:]
+    again = () if reverse or len(pieces) == 1 else pieces[-len(ALONE) :]
+    group = len(pieces) - len(again)
+    pieces = pieces[:group]
     count = lax.axis_size("ctx")
     sds = jax.ShapeDtypeStruct
     if group == 1:
@@ -261,24 +255,29 @@
     piece = sds((rows, width), F32)
     early, late, both = range(group), range(group, count), range(count)
     first, second = (late, early) if reverse else (early, late)
-    arrived = exchange(pieces, both if reverse else first, group)
-    kept = sds((group * rows, width), F32) if reverse else piece
+    everyone = range(group)
+    arrived = [
+        exchange(pieces[i], i, both if reverse or i in SHARED else first, group) for i in everyone
+    ]
+    kept = [sds((group * rows, width), F32)] if reverse else [piece] * len(SHARED)
     total, *back = call(
         functools.partial(inner_body, group, reverse),
-        [piece] * (group + 1) + [kept],
+        [piece] * (group + 1) + kept,
         *arrived,
         scratch=[] if reverse else [state],
     )
     over = lax.ppermute(total, "ctx", [(j, j ^ group) for j in both])
-    ahead = exchange(back[:group], first, group)
+    ahead = [exchange(back[i], i, first, group) for i in everyone]
     if reverse:
         back = call(functools.partial(add_body, group), [piece] * group, back[group], over)
     else:
+        own = [exchange(part, i, second, group) for part, i in zip(again, ALONE)]
+        mixed = [own[ALONE.index(i)] if i in ALONE else back[group + SHARED.index(i)] for i in everyone]
         back = call(
             functools.partial(late_body, group, reverse),
-            [piece] * group, *exchange(again, second, group), back[group], over, scratch=[state],
+            [piece] * group, *mixed, over, scratch=[state],
         )
-    behind = exchange(back, second, group)
+    behind = [exchange(back[i], i, second, group) for i in everyone]
     return [*behind, *ahead] if reverse else [*ahead, *behind]
 
 
@@ -303,7 +302,7 @@
     wide = sds((tokens, width), F32)
     half = sds((tokens, width), BF16)
     state = pltpu.VMEM((width, HEAD), F32)
-    if count in (4, 8) and lax.axis_size("tp") % 2 == 0:
+    if count == 8 and lax.axis_size("tp") % 2 == 0:
         group = count // 2
         pieces = [sds((width // group, HEAD), F32)] * group
     else:
@@ -318,41 +317,41 @@
 
     k_held, v_held, *states = call(
         functools.partial(states_body, heads, group),
-        (in_vmem(keys), in_vmem(values), *pieces, *pieces[1:]),
+        (in_vmem(keys), in_vmem(values), *pieces, *(pieces[i] for i in ALONE if len(pieces) > 1)),
         *in_hbm(keys, values),
         ins=[HBM, HBM],
-        scratch=[state, pltpu.SemaphoreType.DMA((2 * heads,))],
+        scratch=[state, pltpu.SemaphoreType.DMA((2,))],
     )
     prefix = carried_in(states, False, state)
     pairs = heads * tokens * tokens * HEAD
-    scores, local, q_held, og_held, gain_held = call(
+    scores, local, q_held, weighted, gain_held = call(
         functools.partial(scores_body, heads, factor),
         (
             sds((heads, tokens, tokens), BF16), wide,
-            in_vmem(queries), in_vmem(out_grad), in_vmem(gains),
+            in_vmem(queries), in_vmem(wide), in_vmem(gains),
         ),
         k_held, v_held, *in_hbm(queries, out_grad, gains),
         ins=[VMEM, VMEM, HBM, HBM, HBM],
-        scratch=[pltpu.SemaphoreType.DMA((3,))],
+        scratch=[in_vmem(out_grad), pltpu.SemaphoreType.DMA((3,))],
         flops=4 * pairs,
     )
     attended, stats, prefix = call(
         functools.partial(attend_body, heads, factor, group),
         (wide, sds((2, tokens), F32), sds((width, HEAD), F32)),
-        q_held, og_held, gain_held, local, *prefix,
+        q_held, weighted, local, *prefix,
     )
     every = from_all(stats, "tp")
-    normed, grad_attn, *updates = call(
+    inv_rms, grad_attn, *updates = call(
         functools.partial(grad_body, heads, features, group, len(every)),
-        (pltpu.VMEM((tokens, width), BF16), half, *pieces),
-        attended, og_held, gain_held, q_held, *every,
+        (pltpu.VMEM((tokens, HEAD), F32), half, *pieces),
+        attended, weighted, q_held, *every,
         scratch=[state],
     )
     suffix = carried_in(updates, True, state)
     normed, grad_q, gk_part, gv_part = call(
         functools.partial(local_body, heads, factor),
         (half, half, wide, wide),
-        grad_attn, q_held, k_held, v_held, prefix, scores, normed,
+        grad_attn, q_held, k_held, v_held, prefix, scores, attended, inv_rms, gain_held,
         flops=9 * pairs,
     )
     held = pltpu.VMEM((tokens, width), BF16)

time: 41.2 us -> 41 us (level)
  waiting for transfers between devices: 9.94 us -> 11 us
  starting transfers between devices: 24.2 us -> 23.2 us
    ppermute x27 -> x26, waiting for transfers between devices: 5.35 us -> 6.16 us  [exchange(): return lax.ppermute(piece, ('ctx', 'tp'), pairs)]
    ppermute x27 -> x26, starting transfers between devices: 18.6 us -> 18 us  [exchange(): return lax.ppermute(piece, ('ctx', 'tp'), pairs)]
    ppermute x2, starting transfers between devices: 3.44 us -> 3.02 us  [carried_in(): over = lax.ppermute(total, 'ctx', [(j, j ^ group) for j in both])]
  transfers between devices with their start and end apart: 32 -> 31, of which waited for: 13 -> 12; matrix products, arithmetic and copies ran while one was open for 0% -> 0% of each run, Pallas kernels for 7% -> 7%
where the time goes in v1:
time: 41 us; the launch traced here: 40.9 us
  starting transfers between devices  23.2 us (57%)
  waiting for transfers between devices  11 us (27%)
  Pallas kernels  5.85 us (14%)
  between operations  0.75 us (2%)
    ppermute x26, starting transfers between devices, exchange(): return lax.ppermute(piece, ('ctx', 'tp'), pairs)  18 us
    ppermute x26, waiting for transfers between devices, exchange(): return lax.ppermute(piece, ('ctx', 'tp'), pairs)  6.16 us
    pallas_call x10, Pallas kernels, call(): pl.pallas_call(body, out_shape=outs, in_specs=ins or [VMEM] * len(args),...  5.85 us
    ppermute x2, starting transfers between devices, carried_in(): over = lax.ppermute(total, 'ctx', [(j, j ^ group) for j in both])  3.02 us
    ppermute x2, waiting for transfers between devices, carried_in(): over = lax.ppermute(total, 'ctx', [(j, j ^ group) for j in both])  2.48 us
    ppermute x3, waiting for transfers between devices, from_all(): lax.ppermute(part, axis, [(i, i ^ step if even else (i + step) % count) f...  2.39 us
    ppermute x3, starting transfers between devices, from_all(): lax.ppermute(part, axis, [(i, i ^ step if even else (i + step) % count) f...  2.2 us
  transfers between devices with their start and end apart: 31, of which 12 were waited for; matrix products, arithmetic and copies ran while one was open for 0% of the time, Pallas kernels for 7%

profile of v1, /device:TPU:0, one launch (start us, length us, event | category | flops | bytes accessed | tf_op | source)
XLA Modules:
  0.0 40.9 jit_solution(3496970829803600067)
XLA Ops:
  0.6 1.2 %shard_map.84 = (bf16[256,256]{1,0:T(8,128)(2,1)S(1)}, bf16[256,256]{1,0:T(8,128)(2,1)S(1)}, f32[64,128]{1,0:T(8,128)S(1)}, f32[64,128]{1,0:T(8,128)S(1)}, f32[6...) custom-call(bf16[256,256]{1,0:T(8,128)(2,1)} %k_hbm.1, ...), custom_call_target="tpu_custom_call" | custom-call | flops 10000000 | bytes 262144 | tf_op jit(solution)/shard_map/pallas_call | solution.py:33
  1.9 3.5 %collective-permute-start = (f32[64,128]{1,0:T(8,128)S(1)}, f32[64,128]{1,0:T(8,128)S(1)}, u32[]{:S(2)}, u32[]{:S(2)}) collective-permute-start(f32[64,128]{1,0:T(8,128)S(1)} %get-tuple-element.58), channel_id=1, source_target_pairs={{0,13},{1,12},{2,15},{3,14},{4,9},{5,8},{6,11},{7,10},{8,5},{9,4},... | collective-permute-start | bytes 98312 | tf_op jit(solution)/shard_map/ppermute | solution.py:238
  5.3 0.7 %collective-permute-start.1 = (f32[64,128]{1,0:T(8,128)S(1)}, f32[64,128]{1,0:T(8,128)S(1)}, u32[]{:S(2)}, u32[]{:S(2)}) collective-permute-start(f32[64,128]{1,0:T(8,128)S(1)} %get-tuple-element.59), channel_id=1, source_target_pairs={{0,9},{1,8},{2,11},{3,10},{4,13},{5,12},{6,15},{7,14},{8,1},{9,0},... | collective-permute-start | bytes 98312 | tf_op jit(solution)/shard_map/ppermute | solution.py:238
  6.3 0.5 %collective-permute-start.8 = (f32[64,128]{1,0:T(8,128)S(1)}, f32[64,128]{1,0:T(8,128)S(1)}, u32[]{:S(2)}, u32[]{:S(2)}) collective-permute-start(f32[64,128]{1,0:T(8,128)S(1)} %get-tuple-element.66), channel_id=1, source_target_pairs={{0,1},{1,0},{2,3},{3,2},{4,5},{5,4},{6,7},{7,6},{8,9},{9,8},{10,11... | collective-permute-start | bytes 98312 | tf_op jit(solution)/shard_map/ppermute | solution.py:238
  7.1 0.5 %collective-permute-start.9 = (f32[64,128]{1,0:T(8,128)S(1)}, f32[64,128]{1,0:T(8,128)S(1)}, u32[]{:S(2)}, u32[]{:S(2)}) collective-permute-start(f32[64,128]{1,0:T(8,128)S(1)} %get-tuple-element.68), channel_id=1, source_target_pairs={{0,1},{1,0},{2,3},{3,2},{4,5},{5,4},{6,7},{7,6},{8,9},{9,8},{10,11... | collective-permute-start | bytes 98312 | tf_op jit(solution)/shard_map/ppermute | solution.py:238
  7.6 1.1 %collective-permute-done.1.refs_1_ = f32[64,128]{1,0:T(8,128)S(1)} collective-permute-done((f32[64,128]{1,0:T(8,128)S(1)}, f32[64,128]{1,0:T(8,128)S(1)}, u32[]{:S(2)}, u32[]{:S(2)}) %collective-permute-start.1) | collective-permute-done | bytes 32800 | tf_op jit(solution)/shard_map/ppermute | solution.py:238
  8.7 1.0 %collective-permute-done.2.refs_2_ = f32[64,128]{1,0:T(8,128)S(1)} collective-permute-done((f32[64,128]{1,0:T(8,128)S(1)}, f32[64,128]{1,0:T(8,128)S(1)}, u32[]{:S(2)}, u32[]{:S(2)}) %collective-permute-start.2) | collective-permute-done | bytes 32800 | tf_op jit(solution)/shard_map/ppermute | solution.py:238
  10.0 1.9 %collective-permute-start.4 = (f32[64,128]{1,0:T(8,128)S(1)}, f32[64,128]{1,0:T(8,128)S(1)}, u32[]{:S(2)}, u32[]{:S(2)}) collective-permute-start(f32[64,128]{1,0:T(8,128)S(1)} %get-tuple-element.62), channel_id=1, source_target_pairs={{0,13},{1,12},{2,15},{3,14},{4,9},{5,8},{6,11},{7,10},{8,5},{9,4},... | collective-permute-start | bytes 98312 | tf_op jit(solution)/shard_map/ppermute | solution.py:238
  11.9 0.8 %collective-permute-start.5 = (f32[64,128]{1,0:T(8,128)S(1)}, f32[64,128]{1,0:T(8,128)S(1)}, u32[]{:S(2)}, u32[]{:S(2)}) collective-permute-start(f32[64,128]{1,0:T(8,128)S(1)} %get-tuple-element.63), channel_id=1, source_target_pairs={{0,9},{1,8},{2,11},{3,10},{4,13},{5,12},{6,15},{7,14},{8,1},{9,0},... | collective-permute-start | bytes 98312 | tf_op jit(solution)/shard_map/ppermute | solution.py:238
  12.8 0.5 %collective-permute-start.7 = (f32[64,128]{1,0:T(8,128)S(1)}, f32[64,128]{1,0:T(8,128)S(1)}, u32[]{:S(2)}, u32[]{:S(2)}) collective-permute-start(f32[64,128]{1,0:T(8,128)S(1)} %get-tuple-element.65), channel_id=1, source_target_pairs={{0,1},{1,0},{2,3},{3,2},{4,5},{5,4},{6,7},{7,6},{8,9},{9,8},{10,11... | collective-permute-start | bytes 98312 | tf_op jit(solution)/shard_map/ppermute | solution.py:238
  13.3 1.4 %collective-permute-done.10.refs_4_ = f32[64,128]{1,0:T(8,128)S(1)} collective-permute-done((f32[64,128]{1,0:T(8,128)S(1)}, f32[64,128]{1,0:T(8,128)S(1)}, u32[]{:S(2)}, u32[]{:S(2)}) %collective-permute-start.10) | collective-permute-done | bytes 32800 | tf_op jit(solution)/shard_map/ppermute | solution.py:269
  14.9 0.4 collective-permute-start.12
  15.3 0.9 %collective-permute-start.13 = (f32[64,128]{1,0:T(8,128)S(1)}, f32[64,128]{1,0:T(8,128)S(1)}, u32[]{:S(2)}, u32[]{:S(2)}) collective-permute-start(f32[64,128]{1,0:T(8,128)S(1)} %get-tuple-element.73), channel_id=1, source_target_pairs={{0,1},{1,0},{2,3},{3,2},{4,5},{5,4},{6,7},{7,6},{8,9},{9,8},{10,11... | collective-permute-start | bytes 98312 | tf_op jit(solution)/shard_map/ppermute | solution.py:238
  16.3 1.5 %shard_map.85 = (bf16[2,256,256]{2,1,0:T(8,128)(2,1)S(1)}, f32[256,256]{1,0:T(8,128)S(1)}, bf16[256,256]{1,0:T(8,128)(2,1)S(1)}, f32[256,256]{1,0:T(8,128)S(1)}, f32[2,128]{1,0:T(2,128)S(1)}) custom-call(bf16[256,256]{1,0:T(8,128)(2,1)S(1)} %get-tuple-element.53.k, bf16[256,256]{1,0:T(8,128)(2,1)S(1)} %get-tuple-element.54.v, bf16[256,256]{1,0:T(8,128)(2,1)} %q_hbm.1, ...), custom_call_target="tpu_custom_call" | custom-call | flops 67108864 | bytes 525312 | tf_op jit(solution)/shard_map/pallas_call | solution.py:33
  18.2 1.6 %collective-permute-start.17 = (f32[2,256]{1,0:T(2,128)S(1)}, f32[2,256]{1,0:T(2,128)S(1)}, u32[]{:S(2)}, u32[]{:S(2)}) collective-permute-start(f32[2,256]{1,0:T(2,128)S(1)} %get-tuple-element.76.refs_0_), channel_id=1, source_target_pairs={{0,2},{1,3},{2,0},{3,1},{4,6},{5,7},{6,4},{7,5},{8,10},{9,11},{10,... | collective-permute-start | bytes 6152 | tf_op jit(solution)/shard_map/ppermute | solution.py:289
  20.0 0.4 collective-permute-start.15
  20.4 1.4 %collective-permute-done.17.refs_3_ = f32[2,256]{1,0:T(2,128)S(1)} collective-permute-done((f32[2,256]{1,0:T(2,128)S(1)}, f32[2,256]{1,0:T(2,128)S(1)}, u32[]{:S(2)}, u32[]{:S(2)}) %collective-permute-start.17) | collective-permute-done | bytes 2080 | tf_op jit(solution)/shard_map/ppermute | solution.py:289
  21.8 0.9 %collective-permute-done.16.refs_2_ = f32[2,256]{1,0:T(2,128)S(1)} collective-permute-done((f32[2,256]{1,0:T(2,128)S(1)}, f32[2,256]{1,0:T(2,128)S(1)}, u32[]{:S(2)}, u32[]{:S(2)}) %collective-permute-start.16) | collective-permute-done | bytes 2080 | tf_op jit(solution)/shard_map/ppermute | solution.py:289
  23.1 1.3 %collective-permute-start.18 = (f32[64,128]{1,0:T(8,128)S(1)}, f32[64,128]{1,0:T(8,128)S(1)}, u32[]{:S(2)}, u32[]{:S(2)}) collective-permute-start(f32[64,128]{1,0:T(8,128)S(1)} %get-tuple-element.86), channel_id=1, source_target_pairs={{0,13},{1,12},{2,15},{3,14},{4,9},{5,8},{6,11},{7,10},{8,5},{9,4},... | collective-permute-start | bytes 98312 | tf_op jit(solution)/shard_map/ppermute | solution.py:238
  24.4 0.9 %collective-permute-start.19 = (f32[64,128]{1,0:T(8,128)S(1)}, f32[64,128]{1,0:T(8,128)S(1)}, u32[]{:S(2)}, u32[]{:S(2)}) collective-permute-start(f32[64,128]{1,0:T(8,128)S(1)} %get-tuple-element.87), channel_id=1, source_target_pairs={{0,9},{1,8},{2,11},{3,10},{4,13},{5,12},{6,15},{7,14},{8,1},{9,0},... | collective-permute-start | bytes 98312 | tf_op jit(solution)/shard_map/ppermute | solution.py:238
  25.3 0.9 %collective-permute-start.20 = (f32[64,128]{1,0:T(8,128)S(1)}, f32[64,128]{1,0:T(8,128)S(1)}, u32[]{:S(2)}, u32[]{:S(2)}) collective-permute-start(f32[64,128]{1,0:T(8,128)S(1)} %get-tuple-element.88), channel_id=1, source_target_pairs={{0,5},{1,4},{2,7},{3,6},{4,1},{5,0},{6,3},{7,2},{8,13},{9,12},{10,... | collective-permute-start | bytes 98312 | tf_op jit(solution)/shard_map/ppermute | solution.py:238
  26.2 0.3 collective-permute-start.21
  26.5 0.9 %collective-permute-done.18.refs_0_ = f32[64,128]{1,0:T(8,128)S(1)} collective-permute-done((f32[64,128]{1,0:T(8,128)S(1)}, f32[64,128]{1,0:T(8,128)S(1)}, u32[]{:S(2)}, u32[]{:S(2)}) %collective-permute-start.18) | collective-permute-done | bytes 32800 | tf_op jit(solution)/shard_map/ppermute | solution.py:238
  27.8 1.0 %collective-permute-done.20.refs_2_ = f32[64,128]{1,0:T(8,128)S(1)} collective-permute-done((f32[64,128]{1,0:T(8,128)S(1)}, f32[64,128]{1,0:T(8,128)S(1)}, u32[]{:S(2)}, u32[]{:S(2)}) %collective-permute-start.20) | collective-permute-done | bytes 32800 | tf_op jit(solution)/shard_map/ppermute | solution.py:238
  28.8 2.7 %collective-permute-start.22 = (f32[64,128]{1,0:T(8,128)S(1)}, f32[64,128]{1,0:T(8,128)S(1)}, u32[]{:S(2)}, u32[]{:S(2)}) collective-permute-start(f32[64,128]{1,0:T(8,128)S(1)} %get-tuple-element.91), channel_id=1, source_target_pairs={{0,16},{4,20},{8,24},{12,28},{16,0},{20,4},{24,8},{28,12},{1,17},{... | collective-permute-start | bytes 98312 | tf_op jit(solution)/shard_map/ppermute | solution.py:269
  32.5 1.1 %collective-permute-done.22.over = f32[64,128]{1,0:T(8,128)S(1)} collective-permute-done((f32[64,128]{1,0:T(8,128)S(1)}, f32[64,128]{1,0:T(8,128)S(1)}, u32[]{:S(2)}, u32[]{:S(2)}) %collective-permute-start.22) | collective-permute-done | bytes 32800 | tf_op jit(solution)/shard_map/ppermute | solution.py:269
  33.7 1.2 %collective-permute-start.23 = (f32[64,128]{1,0:T(8,128)S(1)}, f32[64,128]{1,0:T(8,128)S(1)}, u32[]{:S(2)}, u32[]{:S(2)}) collective-permute-start(f32[64,128]{1,0:T(8,128)S(1)} %get-tuple-element.92), channel_id=1, source_target_pairs={{0,13},{1,12},{2,15},{3,14},{4,9},{5,8},{6,11},{7,10},{8,5},{9,4},... | collective-permute-start | bytes 98312 | tf_op jit(solution)/shard_map/ppermute | solution.py:238
  34.9 1.6 %collective-permute-start.24 = (f32[64,128]{1,0:T(8,128)S(1)}, f32[64,128]{1,0:T(8,128)S(1)}, u32[]{:S(2)}, u32[]{:S(2)}) collective-permute-start(f32[64,128]{1,0:T(8,128)S(1)} %get-tuple-element.93), channel_id=1, source_target_pairs={{0,9},{1,8},{2,11},{3,10},{4,13},{5,12},{6,15},{7,14},{8,1},{9,0},... | collective-permute-start | bytes 98312 | tf_op jit(solution)/shard_map/ppermute | solution.py:238
  36.5 0.4 %collective-permute-start.25 = (f32[64,128]{1,0:T(8,128)S(1)}, f32[64,128]{1,0:T(8,128)S(1)}, u32[]{:S(2)}, u32[]{:S(2)}) collective-permute-start(f32[64,128]{1,0:T(8,128)S(1)} %get-tuple-element.94), channel_id=1, source_target_pairs={{0,5},{1,4},{2,7},{3,6},{4,1},{5,0},{6,3},{7,2},{8,13},{9,12},{10,... | collective-permute-start | bytes 98312 | tf_op jit(solution)/shard_map/ppermute | solution.py:238
  37.1 1.4 %shard_map.90 = (bf16[256,256]{1,0:T(8,128)(2,1)}, bf16[256,256]{1,0:T(8,128)(2,1)}, f32[256,256]{1,0:T(8,128)S(1)}, f32[256,256]{1,0:T(8,128)S(1)}) custom-call(bf16[256,256]{1,0:T(8,128)(2,1)S(1)} %get-tuple-element.77.ga, bf16[256,256]{1,0:T(8,128)(2,1)S(1)} %get-tuple-element.55.q, bf16[256,256]{1,0:T(8,128)(2,1)S(1)} %get-tuple-element.53.k, ...), custom_call_target="tpu_custom_call" | custom-call | flops 150994944 | bytes 1311744 | tf_op jit(solution)/shard_map/pallas_call | solution.py:33
  38.5 1.5 %collective-permute-done.25.refs_2_ = f32[64,128]{1,0:T(8,128)S(1)} collective-permute-done((f32[64,128]{1,0:T(8,128)S(1)}, f32[64,128]{1,0:T(8,128)S(1)}, u32[]{:S(2)}, u32[]{:S(2)}) %collective-permute-start.25) | collective-permute-done | bytes 32800 | tf_op jit(solution)/shard_map/ppermute | solution.py:238
  39.9 0.9 %shard_map.93 = (bf16[256,256]{1,0:T(8,128)(2,1)}, bf16[256,256]{1,0:T(8,128)(2,1)}) custom-call(bf16[256,256]{1,0:T(8,128)(2,1)S(1)} %get-tuple-element.53.k, bf16[256,256]{1,0:T(8,128)(2,1)S(1)} %get-tuple-element.54.v, f32[256,256]{1,0:T(8,128)S(1)} %get-tuple-element.84.gk_part, f32[256,256]{1,0:T(8,128)S(1)} %get-tuple-element.85.gv_part, ...), custom_call_target="tpu_custom_call" | custom-call | flops 10000000 | bytes 1048576 | tf_op jit(solution)/shard_map/pallas_call | solution.py:33
  (40 shorter events, 3.8 us)
Async XLA Ops:
  1.9 5.2 %collective-permute-start = (f32[64,128]{1,0:T(8,128)S(1)}, f32[64,128]{1,0:T(8,128)S(1)}, u32[]{:S(2)}, u32[]{:S(2)}) collective-permute-start(f32[64,128]{1,0:T(8,128)S(1)} %get-tuple-element.58), channel_id=1, source_target_pairs={{0,13},{1,12},{2,15},{3,14},{4,9},{5,8},{6,11},{7,10},{8,5},{9,4},... | collective-permute-start | bytes 98312 | tf_op jit(solution)/shard_map/ppermute | solution.py:238
  5.3 3.3 %collective-permute-start.1 = (f32[64,128]{1,0:T(8,128)S(1)}, f32[64,128]{1,0:T(8,128)S(1)}, u32[]{:S(2)}, u32[]{:S(2)}) collective-permute-start(f32[64,128]{1,0:T(8,128)S(1)} %get-tuple-element.59), channel_id=1, source_target_pairs={{0,9},{1,8},{2,11},{3,10},{4,13},{5,12},{6,15},{7,14},{8,1},{9,0},... | collective-permute-start | bytes 98312 | tf_op jit(solution)/shard_map/ppermute | solution.py:238
  6.1 3.6 %collective-permute-start.2 = (f32[64,128]{1,0:T(8,128)S(1)}, f32[64,128]{1,0:T(8,128)S(1)}, u32[]{:S(2)}, u32[]{:S(2)}) collective-permute-start(f32[64,128]{1,0:T(8,128)S(1)} %get-tuple-element.60), channel_id=1, source_target_pairs={{0,5},{1,4},{2,7},{3,6},{4,1},{5,0},{6,3},{7,2},{8,13},{9,12},{10,... | collective-permute-start | bytes 98312 | tf_op jit(solution)/shard_map/ppermute | solution.py:238
  6.3 3.4 %collective-permute-start.3 = (f32[64,128]{1,0:T(8,128)S(1)}, f32[64,128]{1,0:T(8,128)S(1)}, u32[]{:S(2)}, u32[]{:S(2)}) collective-permute-start(f32[64,128]{1,0:T(8,128)S(1)} %get-tuple-element.61), channel_id=1, source_target_pairs={{0,1},{1,0},{2,3},{3,2},{4,5},{5,4},{6,7},{7,6},{8,9},{9,8},{10,11... | collective-permute-start | bytes 98312 | tf_op jit(solution)/shard_map/ppermute | solution.py:238
  6.3 6.4 %collective-permute-start.8 = (f32[64,128]{1,0:T(8,128)S(1)}, f32[64,128]{1,0:T(8,128)S(1)}, u32[]{:S(2)}, u32[]{:S(2)}) collective-permute-start(f32[64,128]{1,0:T(8,128)S(1)} %get-tuple-element.66), channel_id=1, source_target_pairs={{0,1},{1,0},{2,3},{3,2},{4,5},{5,4},{6,7},{7,6},{8,9},{9,8},{10,11... | collective-permute-start | bytes 98312 | tf_op jit(solution)/shard_map/ppermute | solution.py:238
  7.1 5.6 %collective-permute-start.9 = (f32[64,128]{1,0:T(8,128)S(1)}, f32[64,128]{1,0:T(8,128)S(1)}, u32[]{:S(2)}, u32[]{:S(2)}) collective-permute-start(f32[64,128]{1,0:T(8,128)S(1)} %get-tuple-element.68), channel_id=1, source_target_pairs={{0,1},{1,0},{2,3},{3,2},{4,5},{5,4},{6,7},{7,6},{8,9},{9,8},{10,11... | collective-permute-start | bytes 98312 | tf_op jit(solution)/shard_map/ppermute | solution.py:238
  9.7 5.0 %collective-permute-start.10 = (f32[64,128]{1,0:T(8,128)S(1)}, f32[64,128]{1,0:T(8,128)S(1)}, u32[]{:S(2)}, u32[]{:S(2)}) collective-permute-start(f32[64,128]{1,0:T(8,128)S(1)} %get-tuple-element.70), channel_id=1, source_target_pairs={{0,16},{4,20},{8,24},{12,28},{16,0},{20,4},{24,8},{28,12},{1,17},{... | collective-permute-start | bytes 98312 | tf_op jit(solution)/shard_map/ppermute | solution.py:269
  10.0 4.9 %collective-permute-start.4 = (f32[64,128]{1,0:T(8,128)S(1)}, f32[64,128]{1,0:T(8,128)S(1)}, u32[]{:S(2)}, u32[]{:S(2)}) collective-permute-start(f32[64,128]{1,0:T(8,128)S(1)} %get-tuple-element.62), channel_id=1, source_target_pairs={{0,13},{1,12},{2,15},{3,14},{4,9},{5,8},{6,11},{7,10},{8,5},{9,4},... | collective-permute-start | bytes 98312 | tf_op jit(solution)/shard_map/ppermute | solution.py:238
  11.9 3.4 %collective-permute-start.5 = (f32[64,128]{1,0:T(8,128)S(1)}, f32[64,128]{1,0:T(8,128)S(1)}, u32[]{:S(2)}, u32[]{:S(2)}) collective-permute-start(f32[64,128]{1,0:T(8,128)S(1)} %get-tuple-element.63), channel_id=1, source_target_pairs={{0,9},{1,8},{2,11},{3,10},{4,13},{5,12},{6,15},{7,14},{8,1},{9,0},... | collective-permute-start | bytes 98312 | tf_op jit(solution)/shard_map/ppermute | solution.py:238
  12.6 3.6 %collective-permute-start.6 = (f32[64,128]{1,0:T(8,128)S(1)}, f32[64,128]{1,0:T(8,128)S(1)}, u32[]{:S(2)}, u32[]{:S(2)}) collective-permute-start(f32[64,128]{1,0:T(8,128)S(1)} %get-tuple-element.64), channel_id=1, source_target_pairs={{0,5},{1,4},{2,7},{3,6},{4,1},{5,0},{6,3},{7,2},{8,13},{9,12},{10,... | collective-permute-start | bytes 98312 | tf_op jit(solution)/shard_map/ppermute | solution.py:238
  12.8 5.0 %collective-permute-start.7 = (f32[64,128]{1,0:T(8,128)S(1)}, f32[64,128]{1,0:T(8,128)S(1)}, u32[]{:S(2)}, u32[]{:S(2)}) collective-permute-start(f32[64,128]{1,0:T(8,128)S(1)} %get-tuple-element.65), channel_id=1, source_target_pairs={{0,1},{1,0},{2,3},{3,2},{4,5},{5,4},{6,7},{7,6},{8,9},{9,8},{10,11... | collective-permute-start | bytes 98312 | tf_op jit(solution)/shard_map/ppermute | solution.py:238
  14.7 3.1 %collective-permute-start.11 = (f32[64,128]{1,0:T(8,128)S(1)}, f32[64,128]{1,0:T(8,128)S(1)}, u32[]{:S(2)}, u32[]{:S(2)}) collective-permute-start(f32[64,128]{1,0:T(8,128)S(1)} %get-tuple-element.71), channel_id=1, source_target_pairs={{0,1},{1,0},{2,3},{3,2},{4,5},{5,4},{6,7},{7,6},{8,9},{9,8},{10,11... | collective-permute-start | bytes 98312 | tf_op jit(solution)/shard_map/ppermute | solution.py:238
  14.9 2.9 %collective-permute-start.12 = (f32[64,128]{1,0:T(8,128)S(1)}, f32[64,128]{1,0:T(8,128)S(1)}, u32[]{:S(2)}, u32[]{:S(2)}) collective-permute-start(f32[64,128]{1,0:T(8,128)S(1)} %get-tuple-element.72), channel_id=1, source_target_pairs={{0,1},{1,0},{2,3},{3,2},{4,5},{5,4},{6,7},{7,6},{8,9},{9,8},{10,11... | collective-permute-start | bytes 98312 | tf_op jit(solution)/shard_map/ppermute | solution.py:238
  15.3 2.6 %collective-permute-start.13 = (f32[64,128]{1,0:T(8,128)S(1)}, f32[64,128]{1,0:T(8,128)S(1)}, u32[]{:S(2)}, u32[]{:S(2)}) collective-permute-start(f32[64,128]{1,0:T(8,128)S(1)} %get-tuple-element.73), channel_id=1, source_target_pairs={{0,1},{1,0},{2,3},{3,2},{4,5},{5,4},{6,7},{7,6},{8,9},{9,8},{10,11... | collective-permute-start | bytes 98312 | tf_op jit(solution)/shard_map/ppermute | solution.py:238
  16.2 1.6 %collective-permute-start.14 = (f32[64,128]{1,0:T(8,128)S(1)}, f32[64,128]{1,0:T(8,128)S(1)}, u32[]{:S(2)}, u32[]{:S(2)}) collective-permute-start(f32[64,128]{1,0:T(8,128)S(1)} %get-tuple-element.74), channel_id=1, source_target_pairs={{0,1},{1,0},{2,3},{3,2},{4,5},{5,4},{6,7},{7,6},{8,9},{9,8},{10,11... | collective-permute-start | bytes 98312 | tf_op jit(solution)/shard_map/ppermute | solution.py:238
  18.2 3.6 %collective-permute-start.17 = (f32[2,256]{1,0:T(2,128)S(1)}, f32[2,256]{1,0:T(2,128)S(1)}, u32[]{:S(2)}, u32[]{:S(2)}) collective-permute-start(f32[2,256]{1,0:T(2,128)S(1)} %get-tuple-element.76.refs_0_), channel_id=1, source_target_pairs={{0,2},{1,3},{2,0},{3,1},{4,6},{5,7},{6,4},{7,5},{8,10},{9,11},{10,... | collective-permute-start | bytes 6152 | tf_op jit(solution)/shard_map/ppermute | solution.py:289
  19.8 3.0 %collective-permute-start.16 = (f32[2,256]{1,0:T(2,128)S(1)}, f32[2,256]{1,0:T(2,128)S(1)}, u32[]{:S(2)}, u32[]{:S(2)}) collective-permute-start(f32[2,256]{1,0:T(2,128)S(1)} %get-tuple-element.76.refs_0_), channel_id=1, source_target_pairs={{0,3},{1,2},{2,1},{3,0},{4,7},{5,6},{6,5},{7,4},{8,11},{9,10},{10,... | collective-permute-start | bytes 6152 | tf_op jit(solution)/shard_map/ppermute | solution.py:289
  20.0 2.8 %collective-permute-start.15 = (f32[2,256]{1,0:T(2,128)S(1)}, f32[2,256]{1,0:T(2,128)S(1)}, u32[]{:S(2)}, u32[]{:S(2)}) collective-permute-start(f32[2,256]{1,0:T(2,128)S(1)} %get-tuple-element.76.refs_0_), channel_id=1, source_target_pairs={{0,1},{1,0},{2,3},{3,2},{4,5},{5,4},{6,7},{7,6},{8,9},{9,8},{10,11... | collective-permute-start | bytes 6152 | tf_op jit(solution)/shard_map/ppermute | solution.py:289
  23.1 4.3 %collective-permute-start.18 = (f32[64,128]{1,0:T(8,128)S(1)}, f32[64,128]{1,0:T(8,128)S(1)}, u32[]{:S(2)}, u32[]{:S(2)}) collective-permute-start(f32[64,128]{1,0:T(8,128)S(1)} %get-tuple-element.86), channel_id=1, source_target_pairs={{0,13},{1,12},{2,15},{3,14},{4,9},{5,8},{6,11},{7,10},{8,5},{9,4},... | collective-permute-start | bytes 98312 | tf_op jit(solution)/shard_map/ppermute | solution.py:238
  24.4 3.4 %collective-permute-start.19 = (f32[64,128]{1,0:T(8,128)S(1)}, f32[64,128]{1,0:T(8,128)S(1)}, u32[]{:S(2)}, u32[]{:S(2)}) collective-permute-start(f32[64,128]{1,0:T(8,128)S(1)} %get-tuple-element.87), channel_id=1, source_target_pairs={{0,9},{1,8},{2,11},{3,10},{4,13},{5,12},{6,15},{7,14},{8,1},{9,0},... | collective-permute-start | bytes 98312 | tf_op jit(solution)/shard_map/ppermute | solution.py:238
  25.3 3.4 %collective-permute-start.20 = (f32[64,128]{1,0:T(8,128)S(1)}, f32[64,128]{1,0:T(8,128)S(1)}, u32[]{:S(2)}, u32[]{:S(2)}) collective-permute-start(f32[64,128]{1,0:T(8,128)S(1)} %get-tuple-element.88), channel_id=1, source_target_pairs={{0,5},{1,4},{2,7},{3,6},{4,1},{5,0},{6,3},{7,2},{8,13},{9,12},{10,... | collective-permute-start | bytes 98312 | tf_op jit(solution)/shard_map/ppermute | solution.py:238
  26.2 2.6 %collective-permute-start.21 = (f32[64,128]{1,0:T(8,128)S(1)}, f32[64,128]{1,0:T(8,128)S(1)}, u32[]{:S(2)}, u32[]{:S(2)}) collective-permute-start(f32[64,128]{1,0:T(8,128)S(1)} %get-tuple-element.89), channel_id=1, source_target_pairs={{0,1},{1,0},{2,3},{3,2},{4,5},{5,4},{6,7},{7,6},{8,9},{9,8},{10,11... | collective-permute-start | bytes 98312 | tf_op jit(solution)/shard_map/ppermute | solution.py:238
  28.8 4.9 %collective-permute-start.22 = (f32[64,128]{1,0:T(8,128)S(1)}, f32[64,128]{1,0:T(8,128)S(1)}, u32[]{:S(2)}, u32[]{:S(2)}) collective-permute-start(f32[64,128]{1,0:T(8,128)S(1)} %get-tuple-element.91), channel_id=1, source_target_pairs={{0,16},{4,20},{8,24},{12,28},{16,0},{20,4},{24,8},{28,12},{1,17},{... | collective-permute-start | bytes 98312 | tf_op jit(solution)/shard_map/ppermute | solution.py:269
  31.5 3.4 %collective-permute-start.27 = (f32[64,128]{1,0:T(8,128)S(1)}, f32[64,128]{1,0:T(8,128)S(1)}, u32[]{:S(2)}, u32[]{:S(2)}) collective-permute-start(f32[64,128]{1,0:T(8,128)S(1)} %get-tuple-element.96), channel_id=1, source_target_pairs={{0,1},{1,0},{2,3},{3,2},{4,5},{5,4},{6,7},{7,6},{8,9},{9,8},{10,11... | collective-permute-start | bytes 98312 | tf_op jit(solution)/shard_map/ppermute | solution.py:238
  31.7 4.8 %collective-permute-start.28 = (f32[64,128]{1,0:T(8,128)S(1)}, f32[64,128]{1,0:T(8,128)S(1)}, u32[]{:S(2)}, u32[]{:S(2)}) collective-permute-start(f32[64,128]{1,0:T(8,128)S(1)} %get-tuple-element.97), channel_id=1, source_target_pairs={{0,1},{1,0},{2,3},{3,2},{4,5},{5,4},{6,7},{7,6},{8,9},{9,8},{10,11... | collective-permute-start | bytes 98312 | tf_op jit(solution)/shard_map/ppermute | solution.py:238
  32.0 4.9 %collective-permute-start.29 = (f32[64,128]{1,0:T(8,128)S(1)}, f32[64,128]{1,0:T(8,128)S(1)}, u32[]{:S(2)}, u32[]{:S(2)}) collective-permute-start(f32[64,128]{1,0:T(8,128)S(1)} %get-tuple-element.98), channel_id=1, source_target_pairs={{0,1},{1,0},{2,3},{3,2},{4,5},{5,4},{6,7},{7,6},{8,9},{9,8},{10,11... | collective-permute-start | bytes 98312 | tf_op jit(solution)/shard_map/ppermute | solution.py:238
  32.2 6.3 %collective-permute-start.30 = (f32[64,128]{1,0:T(8,128)S(1)}, f32[64,128]{1,0:T(8,128)S(1)}, u32[]{:S(2)}, u32[]{:S(2)}) collective-permute-start(f32[64,128]{1,0:T(8,128)S(1)} %get-tuple-element.99), channel_id=1, source_target_pairs={{0,1},{1,0},{2,3},{3,2},{4,5},{5,4},{6,7},{7,6},{8,9},{9,8},{10,11... | collective-permute-start | bytes 98312 | tf_op jit(solution)/shard_map/ppermute | solution.py:238
  33.7 4.8 %collective-permute-start.23 = (f32[64,128]{1,0:T(8,128)S(1)}, f32[64,128]{1,0:T(8,128)S(1)}, u32[]{:S(2)}, u32[]{:S(2)}) collective-permute-start(f32[64,128]{1,0:T(8,128)S(1)} %get-tuple-element.92), channel_id=1, source_target_pairs={{0,13},{1,12},{2,15},{3,14},{4,9},{5,8},{6,11},{7,10},{8,5},{9,4},... | collective-permute-start | bytes 98312 | tf_op jit(solution)/shard_map/ppermute | solution.py:238
  34.9 3.6 %collective-permute-start.24 = (f32[64,128]{1,0:T(8,128)S(1)}, f32[64,128]{1,0:T(8,128)S(1)}, u32[]{:S(2)}, u32[]{:S(2)}) collective-permute-start(f32[64,128]{1,0:T(8,128)S(1)} %get-tuple-element.93), channel_id=1, source_target_pairs={{0,9},{1,8},{2,11},{3,10},{4,13},{5,12},{6,15},{7,14},{8,1},{9,0},... | collective-permute-start | bytes 98312 | tf_op jit(solution)/shard_map/ppermute | solution.py:238
  36.5 3.4 %collective-permute-start.25 = (f32[64,128]{1,0:T(8,128)S(1)}, f32[64,128]{1,0:T(8,128)S(1)}, u32[]{:S(2)}, u32[]{:S(2)}) collective-permute-start(f32[64,128]{1,0:T(8,128)S(1)} %get-tuple-element.94), channel_id=1, source_target_pairs={{0,5},{1,4},{2,7},{3,6},{4,1},{5,0},{6,3},{7,2},{8,13},{9,12},{10,... | collective-permute-start | bytes 98312 | tf_op jit(solution)/shard_map/ppermute | solution.py:238
  36.9 3.0 %collective-permute-start.26 = (f32[64,128]{1,0:T(8,128)S(1)}, f32[64,128]{1,0:T(8,128)S(1)}, u32[]{:S(2)}, u32[]{:S(2)}) collective-permute-start(f32[64,128]{1,0:T(8,128)S(1)} %get-tuple-element.95), channel_id=1, source_target_pairs={{0,1},{1,0},{2,3},{3,2},{4,5},{5,4},{6,7},{7,6},{8,9},{9,8},{10,11... | collective-permute-start | bytes 98312 | tf_op jit(solution)/shard_map/ppermute | solution.py:238

commit v2 on v1

--- a/solution.py
+++ b/solution.py
@@ -284,10 +284,9 @@
 def from_all(part, axis):
     count = lax.axis_size(axis)
     even = count & (count - 1) == 0
-    steps = [1, 3, 2] if count == 4 else range(1, count)
     return [part] + [
         lax.ppermute(part, axis, [(i, i ^ step if even else (i + step) % count) for i in range(count)])
-        for step in steps
+        for step in range(1, count)
     ]
 
 

time: 41 us -> 41.4 us (level)
  waiting for transfers between devices: 11 us -> 11.8 us
    ppermute x3, waiting for transfers between devices: 2.39 us -> 3.08 us  [from_all(): lax.ppermute(part, axis, [(i, i ^ step if even else (i + step) % count) f...]
  transfers between devices with their start and end apart: 31 -> 31, of which waited for: 12 -> 11; matrix products, arithmetic and copies ran while one was open for 0% -> 0% of each run, Pallas kernels for 7% -> 7%
where the time goes in v2:
time: 41.4 us; the launch traced here: 41.2 us
  starting transfers between devices  22.8 us (55%)
  waiting for transfers between devices  11.8 us (29%)
  Pallas kernels  5.85 us (14%)
  between operations  0.77 us (2%)
    ppermute x26, starting transfers between devices, exchange(): return lax.ppermute(piece, ('ctx', 'tp'), pairs)  18 us
    ppermute x26, waiting for transfers between devices, exchange(): return lax.ppermute(piece, ('ctx', 'tp'), pairs)  5.93 us
    pallas_call x10, Pallas kernels, call(): pl.pallas_call(body, out_shape=outs, in_specs=ins or [VMEM] * len(args),...  5.85 us
    ppermute x3, waiting for transfers between devices, from_all(): lax.ppermute(part, axis, [(i, i ^ step if even else (i + step) % count) f...  3.08 us
    ppermute x2, waiting for transfers between devices, carried_in(): over = lax.ppermute(total, 'ctx', [(j, j ^ group) for j in both])  2.84 us
    ppermute x2, starting transfers between devices, carried_in(): over = lax.ppermute(total, 'ctx', [(j, j ^ group) for j in both])  2.67 us
    ppermute x3, starting transfers between devices, from_all(): lax.ppermute(part, axis, [(i, i ^ step if even else (i + step) % count) f...  2.13 us
  transfers between devices with their start and end apart: 31, of which 11 were waited for; matrix products, arithmetic and copies ran while one was open for 0% of the time, Pallas kernels for 7%

profile of v2, /device:TPU:0, one launch (start us, length us, event | category | flops | bytes accessed | tf_op | source)
XLA Modules:
  0.0 41.2 jit_solution(9244820776318901777)
XLA Ops:
  0.6 1.2 %shard_map.84 = (bf16[256,256]{1,0:T(8,128)(2,1)S(1)}, bf16[256,256]{1,0:T(8,128)(2,1)S(1)}, f32[64,128]{1,0:T(8,128)S(1)}, f32[64,128]{1,0:T(8,128)S(1)}, f32[6...) custom-call(bf16[256,256]{1,0:T(8,128)(2,1)} %k_hbm.1, ...), custom_call_target="tpu_custom_call" | custom-call | flops 10000000 | bytes 262144 | tf_op jit(solution)/shard_map/pallas_call | solution.py:33
  1.9 3.5 %collective-permute-start = (f32[64,128]{1,0:T(8,128)S(1)}, f32[64,128]{1,0:T(8,128)S(1)}, u32[]{:S(2)}, u32[]{:S(2)}) collective-permute-start(f32[64,128]{1,0:T(8,128)S(1)} %get-tuple-element.58), channel_id=1, source_target_pairs={{0,13},{1,12},{2,15},{3,14},{4,9},{5,8},{6,11},{7,10},{8,5},{9,4},... | collective-permute-start | bytes 98312 | tf_op jit(solution)/shard_map/ppermute | solution.py:238
  5.3 0.7 %collective-permute-start.1 = (f32[64,128]{1,0:T(8,128)S(1)}, f32[64,128]{1,0:T(8,128)S(1)}, u32[]{:S(2)}, u32[]{:S(2)}) collective-permute-start(f32[64,128]{1,0:T(8,128)S(1)} %get-tuple-element.59), channel_id=1, source_target_pairs={{0,9},{1,8},{2,11},{3,10},{4,13},{5,12},{6,15},{7,14},{8,1},{9,0},... | collective-permute-start | bytes 98312 | tf_op jit(solution)/shard_map/ppermute | solution.py:238
  6.3 0.5 %collective-permute-start.8 = (f32[64,128]{1,0:T(8,128)S(1)}, f32[64,128]{1,0:T(8,128)S(1)}, u32[]{:S(2)}, u32[]{:S(2)}) collective-permute-start(f32[64,128]{1,0:T(8,128)S(1)} %get-tuple-element.66), channel_id=1, source_target_pairs={{0,1},{1,0},{2,3},{3,2},{4,5},{5,4},{6,7},{7,6},{8,9},{9,8},{10,11... | collective-permute-start | bytes 98312 | tf_op jit(solution)/shard_map/ppermute | solution.py:238
  7.1 0.5 %collective-permute-start.9 = (f32[64,128]{1,0:T(8,128)S(1)}, f32[64,128]{1,0:T(8,128)S(1)}, u32[]{:S(2)}, u32[]{:S(2)}) collective-permute-start(f32[64,128]{1,0:T(8,128)S(1)} %get-tuple-element.68), channel_id=1, source_target_pairs={{0,1},{1,0},{2,3},{3,2},{4,5},{5,4},{6,7},{7,6},{8,9},{9,8},{10,11... | collective-permute-start | bytes 98312 | tf_op jit(solution)/shard_map/ppermute | solution.py:238
  7.6 1.1 %collective-permute-done.1.refs_1_ = f32[64,128]{1,0:T(8,128)S(1)} collective-permute-done((f32[64,128]{1,0:T(8,128)S(1)}, f32[64,128]{1,0:T(8,128)S(1)}, u32[]{:S(2)}, u32[]{:S(2)}) %collective-permute-start.1) | collective-permute-done | bytes 32800 | tf_op jit(solution)/shard_map/ppermute | solution.py:238
  8.7 1.0 %collective-permute-done.2.refs_2_ = f32[64,128]{1,0:T(8,128)S(1)} collective-permute-done((f32[64,128]{1,0:T(8,128)S(1)}, f32[64,128]{1,0:T(8,128)S(1)}, u32[]{:S(2)}, u32[]{:S(2)}) %collective-permute-start.2) | collective-permute-done | bytes 32800 | tf_op jit(solution)/shard_map/ppermute | solution.py:238
  10.0 1.9 %collective-permute-start.4 = (f32[64,128]{1,0:T(8,128)S(1)}, f32[64,128]{1,0:T(8,128)S(1)}, u32[]{:S(2)}, u32[]{:S(2)}) collective-permute-start(f32[64,128]{1,0:T(8,128)S(1)} %get-tuple-element.62), channel_id=1, source_target_pairs={{0,13},{1,12},{2,15},{3,14},{4,9},{5,8},{6,11},{7,10},{8,5},{9,4},... | collective-permute-start | bytes 98312 | tf_op jit(solution)/shard_map/ppermute | solution.py:238
  11.9 0.8 %collective-permute-start.5 = (f32[64,128]{1,0:T(8,128)S(1)}, f32[64,128]{1,0:T(8,128)S(1)}, u32[]{:S(2)}, u32[]{:S(2)}) collective-permute-start(f32[64,128]{1,0:T(8,128)S(1)} %get-tuple-element.63), channel_id=1, source_target_pairs={{0,9},{1,8},{2,11},{3,10},{4,13},{5,12},{6,15},{7,14},{8,1},{9,0},... | collective-permute-start | bytes 98312 | tf_op jit(solution)/shard_map/ppermute | solution.py:238
  12.8 0.5 %collective-permute-start.7 = (f32[64,128]{1,0:T(8,128)S(1)}, f32[64,128]{1,0:T(8,128)S(1)}, u32[]{:S(2)}, u32[]{:S(2)}) collective-permute-start(f32[64,128]{1,0:T(8,128)S(1)} %get-tuple-element.65), channel_id=1, source_target_pairs={{0,1},{1,0},{2,3},{3,2},{4,5},{5,4},{6,7},{7,6},{8,9},{9,8},{10,11... | collective-permute-start | bytes 98312 | tf_op jit(solution)/shard_map/ppermute | solution.py:238
  13.3 1.4 %collective-permute-done.10.refs_4_ = f32[64,128]{1,0:T(8,128)S(1)} collective-permute-done((f32[64,128]{1,0:T(8,128)S(1)}, f32[64,128]{1,0:T(8,128)S(1)}, u32[]{:S(2)}, u32[]{:S(2)}) %collective-permute-start.10) | collective-permute-done | bytes 32800 | tf_op jit(solution)/shard_map/ppermute | solution.py:269
  14.9 0.4 collective-permute-start.12
  15.3 0.9 %collective-permute-start.13 = (f32[64,128]{1,0:T(8,128)S(1)}, f32[64,128]{1,0:T(8,128)S(1)}, u32[]{:S(2)}, u32[]{:S(2)}) collective-permute-start(f32[64,128]{1,0:T(8,128)S(1)} %get-tuple-element.73), channel_id=1, source_target_pairs={{0,1},{1,0},{2,3},{3,2},{4,5},{5,4},{6,7},{7,6},{8,9},{9,8},{10,11... | collective-permute-start | bytes 98312 | tf_op jit(solution)/shard_map/ppermute | solution.py:238
  16.3 1.5 %shard_map.85 = (bf16[2,256,256]{2,1,0:T(8,128)(2,1)S(1)}, f32[256,256]{1,0:T(8,128)S(1)}, bf16[256,256]{1,0:T(8,128)(2,1)S(1)}, f32[256,256]{1,0:T(8,128)S(1)}, f32[2,128]{1,0:T(2,128)S(1)}) custom-call(bf16[256,256]{1,0:T(8,128)(2,1)S(1)} %get-tuple-element.53.k, bf16[256,256]{1,0:T(8,128)(2,1)S(1)} %get-tuple-element.54.v, bf16[256,256]{1,0:T(8,128)(2,1)} %q_hbm.1, ...), custom_call_target="tpu_custom_call" | custom-call | flops 67108864 | bytes 525312 | tf_op jit(solution)/shard_map/pallas_call | solution.py:33
  18.2 1.6 %collective-permute-start.17 = (f32[2,256]{1,0:T(2,128)S(1)}, f32[2,256]{1,0:T(2,128)S(1)}, u32[]{:S(2)}, u32[]{:S(2)}) collective-permute-start(f32[2,256]{1,0:T(2,128)S(1)} %get-tuple-element.76.refs_0_), channel_id=1, source_target_pairs={{0,3},{1,2},{2,1},{3,0},{4,7},{5,6},{6,5},{7,4},{8,11},{9,10},{10,... | collective-permute-start | bytes 6152 | tf_op jit(solution)/shard_map/ppermute | solution.py:288
  19.8 0.5 %collective-permute-start.16 = (f32[2,256]{1,0:T(2,128)S(1)}, f32[2,256]{1,0:T(2,128)S(1)}, u32[]{:S(2)}, u32[]{:S(2)}) collective-permute-start(f32[2,256]{1,0:T(2,128)S(1)} %get-tuple-element.76.refs_0_), channel_id=1, source_target_pairs={{0,2},{1,3},{2,0},{3,1},{4,6},{5,7},{6,4},{7,5},{8,10},{9,11},{10,... | collective-permute-start | bytes 6152 | tf_op jit(solution)/shard_map/ppermute | solution.py:288
  20.3 0.9 %collective-permute-done.17.refs_3_ = f32[2,256]{1,0:T(2,128)S(1)} collective-permute-done((f32[2,256]{1,0:T(2,128)S(1)}, f32[2,256]{1,0:T(2,128)S(1)}, u32[]{:S(2)}, u32[]{:S(2)}) %collective-permute-start.17) | collective-permute-done | bytes 2080 | tf_op jit(solution)/shard_map/ppermute | solution.py:288
  21.3 2.1 %collective-permute-done.16.refs_2_ = f32[2,256]{1,0:T(2,128)S(1)} collective-permute-done((f32[2,256]{1,0:T(2,128)S(1)}, f32[2,256]{1,0:T(2,128)S(1)}, u32[]{:S(2)}, u32[]{:S(2)}) %collective-permute-start.16) | collective-permute-done | bytes 2080 | tf_op jit(solution)/shard_map/ppermute | solution.py:288
  23.8 2.0 %collective-permute-start.19 = (f32[64,128]{1,0:T(8,128)S(1)}, f32[64,128]{1,0:T(8,128)S(1)}, u32[]{:S(2)}, u32[]{:S(2)}) collective-permute-start(f32[64,128]{1,0:T(8,128)S(1)} %get-tuple-element.87), channel_id=1, source_target_pairs={{0,9},{1,8},{2,11},{3,10},{4,13},{5,12},{6,15},{7,14},{8,1},{9,0},... | collective-permute-start | bytes 98312 | tf_op jit(solution)/shard_map/ppermute | solution.py:238
  25.8 0.8 %collective-permute-start.20 = (f32[64,128]{1,0:T(8,128)S(1)}, f32[64,128]{1,0:T(8,128)S(1)}, u32[]{:S(2)}, u32[]{:S(2)}) collective-permute-start(f32[64,128]{1,0:T(8,128)S(1)} %get-tuple-element.88), channel_id=1, source_target_pairs={{0,5},{1,4},{2,7},{3,6},{4,1},{5,0},{6,3},{7,2},{8,13},{9,12},{10,... | collective-permute-start | bytes 98312 | tf_op jit(solution)/shard_map/ppermute | solution.py:238
  26.7 0.5 %collective-permute-start.21 = (f32[64,128]{1,0:T(8,128)S(1)}, f32[64,128]{1,0:T(8,128)S(1)}, u32[]{:S(2)}, u32[]{:S(2)}) collective-permute-start(f32[64,128]{1,0:T(8,128)S(1)} %get-tuple-element.89), channel_id=1, source_target_pairs={{0,1},{1,0},{2,3},{3,2},{4,5},{5,4},{6,7},{7,6},{8,9},{9,8},{10,11... | collective-permute-start | bytes 98312 | tf_op jit(solution)/shard_map/ppermute | solution.py:238
  27.1 0.9 %collective-permute-done.18.refs_0_ = f32[64,128]{1,0:T(8,128)S(1)} collective-permute-done((f32[64,128]{1,0:T(8,128)S(1)}, f32[64,128]{1,0:T(8,128)S(1)}, u32[]{:S(2)}, u32[]{:S(2)}) %collective-permute-start.18) | collective-permute-done | bytes 32800 | tf_op jit(solution)/shard_map/ppermute | solution.py:238
  28.1 1.4 %collective-permute-done.20.refs_2_ = f32[64,128]{1,0:T(8,128)S(1)} collective-permute-done((f32[64,128]{1,0:T(8,128)S(1)}, f32[64,128]{1,0:T(8,128)S(1)}, u32[]{:S(2)}, u32[]{:S(2)}) %collective-permute-start.20) | collective-permute-done | bytes 32800 | tf_op jit(solution)/shard_map/ppermute | solution.py:238
  29.5 2.4 %collective-permute-start.22 = (f32[64,128]{1,0:T(8,128)S(1)}, f32[64,128]{1,0:T(8,128)S(1)}, u32[]{:S(2)}, u32[]{:S(2)}) collective-permute-start(f32[64,128]{1,0:T(8,128)S(1)} %get-tuple-element.91), channel_id=1, source_target_pairs={{0,16},{4,20},{8,24},{12,28},{16,0},{20,4},{24,8},{28,12},{1,17},{... | collective-permute-start | bytes 98312 | tf_op jit(solution)/shard_map/ppermute | solution.py:269
  32.0 0.5 %collective-permute-start.28 = (f32[64,128]{1,0:T(8,128)S(1)}, f32[64,128]{1,0:T(8,128)S(1)}, u32[]{:S(2)}, u32[]{:S(2)}) collective-permute-start(f32[64,128]{1,0:T(8,128)S(1)} %get-tuple-element.97), channel_id=1, source_target_pairs={{0,1},{1,0},{2,3},{3,2},{4,5},{5,4},{6,7},{7,6},{8,9},{9,8},{10,11... | collective-permute-start | bytes 98312 | tf_op jit(solution)/shard_map/ppermute | solution.py:238
  32.5 0.5 %collective-permute-start.30 = (f32[64,128]{1,0:T(8,128)S(1)}, f32[64,128]{1,0:T(8,128)S(1)}, u32[]{:S(2)}, u32[]{:S(2)}) collective-permute-start(f32[64,128]{1,0:T(8,128)S(1)} %get-tuple-element.99), channel_id=1, source_target_pairs={{0,1},{1,0},{2,3},{3,2},{4,5},{5,4},{6,7},{7,6},{8,9},{9,8},{10,11... | collective-permute-start | bytes 98312 | tf_op jit(solution)/shard_map/ppermute | solution.py:238
  32.9 1.5 %collective-permute-done.22.over = f32[64,128]{1,0:T(8,128)S(1)} collective-permute-done((f32[64,128]{1,0:T(8,128)S(1)}, f32[64,128]{1,0:T(8,128)S(1)}, u32[]{:S(2)}, u32[]{:S(2)}) %collective-permute-start.22) | collective-permute-done | bytes 32800 | tf_op jit(solution)/shard_map/ppermute | solution.py:269
  34.5 2.2 %collective-permute-start.24 = (f32[64,128]{1,0:T(8,128)S(1)}, f32[64,128]{1,0:T(8,128)S(1)}, u32[]{:S(2)}, u32[]{:S(2)}) collective-permute-start(f32[64,128]{1,0:T(8,128)S(1)} %get-tuple-element.93), channel_id=1, source_target_pairs={{0,9},{1,8},{2,11},{3,10},{4,13},{5,12},{6,15},{7,14},{8,1},{9,0},... | collective-permute-start | bytes 98312 | tf_op jit(solution)/shard_map/ppermute | solution.py:238
  37.1 0.7 %collective-permute-start.26 = (f32[64,128]{1,0:T(8,128)S(1)}, f32[64,128]{1,0:T(8,128)S(1)}, u32[]{:S(2)}, u32[]{:S(2)}) collective-permute-start(f32[64,128]{1,0:T(8,128)S(1)} %get-tuple-element.95), channel_id=1, source_target_pairs={{0,1},{1,0},{2,3},{3,2},{4,5},{5,4},{6,7},{7,6},{8,9},{9,8},{10,11... | collective-permute-start | bytes 98312 | tf_op jit(solution)/shard_map/ppermute | solution.py:238
  37.8 1.4 %shard_map.90 = (bf16[256,256]{1,0:T(8,128)(2,1)}, bf16[256,256]{1,0:T(8,128)(2,1)}, f32[256,256]{1,0:T(8,128)S(1)}, f32[256,256]{1,0:T(8,128)S(1)}) custom-call(bf16[256,256]{1,0:T(8,128)(2,1)S(1)} %get-tuple-element.77.ga, bf16[256,256]{1,0:T(8,128)(2,1)S(1)} %get-tuple-element.55.q, bf16[256,256]{1,0:T(8,128)(2,1)S(1)} %get-tuple-element.53.k, ...), custom_call_target="tpu_custom_call" | custom-call | flops 150994944 | bytes 1311744 | tf_op jit(solution)/shard_map/pallas_call | solution.py:33
  39.2 1.1 %collective-permute-done.25.refs_2_ = f32[64,128]{1,0:T(8,128)S(1)} collective-permute-done((f32[64,128]{1,0:T(8,128)S(1)}, f32[64,128]{1,0:T(8,128)S(1)}, u32[]{:S(2)}, u32[]{:S(2)}) %collective-permute-start.25) | collective-permute-done | bytes 32800 | tf_op jit(solution)/shard_map/ppermute | solution.py:238
  40.3 0.9 %shard_map.93 = (bf16[256,256]{1,0:T(8,128)(2,1)}, bf16[256,256]{1,0:T(8,128)(2,1)}) custom-call(bf16[256,256]{1,0:T(8,128)(2,1)S(1)} %get-tuple-element.53.k, bf16[256,256]{1,0:T(8,128)(2,1)S(1)} %get-tuple-element.54.v, f32[256,256]{1,0:T(8,128)S(1)} %get-tuple-element.84.gk_part, f32[256,256]{1,0:T(8,128)S(1)} %get-tuple-element.85.gv_part, ...), custom_call_target="tpu_custom_call" | custom-call | flops 10000000 | bytes 1048576 | tf_op jit(solution)/shard_map/pallas_call | solution.py:33
  (40 shorter events, 2.7 us)
Async XLA Ops:
  1.9 5.2 %collective-permute-start = (f32[64,128]{1,0:T(8,128)S(1)}, f32[64,128]{1,0:T(8,128)S(1)}, u32[]{:S(2)}, u32[]{:S(2)}) collective-permute-start(f32[64,128]{1,0:T(8,128)S(1)} %get-tuple-element.58), channel_id=1, source_target_pairs={{0,13},{1,12},{2,15},{3,14},{4,9},{5,8},{6,11},{7,10},{8,5},{9,4},... | collective-permute-start | bytes 98312 | tf_op jit(solution)/shard_map/ppermute | solution.py:238
  5.3 3.3 %collective-permute-start.1 = (f32[64,128]{1,0:T(8,128)S(1)}, f32[64,128]{1,0:T(8,128)S(1)}, u32[]{:S(2)}, u32[]{:S(2)}) collective-permute-start(f32[64,128]{1,0:T(8,128)S(1)} %get-tuple-element.59), channel_id=1, source_target_pairs={{0,9},{1,8},{2,11},{3,10},{4,13},{5,12},{6,15},{7,14},{8,1},{9,0},... | collective-permute-start | bytes 98312 | tf_op jit(solution)/shard_map/ppermute | solution.py:238
  6.1 3.6 %collective-permute-start.2 = (f32[64,128]{1,0:T(8,128)S(1)}, f32[64,128]{1,0:T(8,128)S(1)}, u32[]{:S(2)}, u32[]{:S(2)}) collective-permute-start(f32[64,128]{1,0:T(8,128)S(1)} %get-tuple-element.60), channel_id=1, source_target_pairs={{0,5},{1,4},{2,7},{3,6},{4,1},{5,0},{6,3},{7,2},{8,13},{9,12},{10,... | collective-permute-start | bytes 98312 | tf_op jit(solution)/shard_map/ppermute | solution.py:238
  6.3 3.4 %collective-permute-start.3 = (f32[64,128]{1,0:T(8,128)S(1)}, f32[64,128]{1,0:T(8,128)S(1)}, u32[]{:S(2)}, u32[]{:S(2)}) collective-permute-start(f32[64,128]{1,0:T(8,128)S(1)} %get-tuple-element.61), channel_id=1, source_target_pairs={{0,1},{1,0},{2,3},{3,2},{4,5},{5,4},{6,7},{7,6},{8,9},{9,8},{10,11... | collective-permute-start | bytes 98312 | tf_op jit(solution)/shard_map/ppermute | solution.py:238
  6.3 6.4 %collective-permute-start.8 = (f32[64,128]{1,0:T(8,128)S(1)}, f32[64,128]{1,0:T(8,128)S(1)}, u32[]{:S(2)}, u32[]{:S(2)}) collective-permute-start(f32[64,128]{1,0:T(8,128)S(1)} %get-tuple-element.66), channel_id=1, source_target_pairs={{0,1},{1,0},{2,3},{3,2},{4,5},{5,4},{6,7},{7,6},{8,9},{9,8},{10,11... | collective-permute-start | bytes 98312 | tf_op jit(solution)/shard_map/ppermute | solution.py:238
  7.1 5.6 %collective-permute-start.9 = (f32[64,128]{1,0:T(8,128)S(1)}, f32[64,128]{1,0:T(8,128)S(1)}, u32[]{:S(2)}, u32[]{:S(2)}) collective-permute-start(f32[64,128]{1,0:T(8,128)S(1)} %get-tuple-element.68), channel_id=1, source_target_pairs={{0,1},{1,0},{2,3},{3,2},{4,5},{5,4},{6,7},{7,6},{8,9},{9,8},{10,11... | collective-permute-start | bytes 98312 | tf_op jit(solution)/shard_map/ppermute | solution.py:238
  9.7 5.0 %collective-permute-start.10 = (f32[64,128]{1,0:T(8,128)S(1)}, f32[64,128]{1,0:T(8,128)S(1)}, u32[]{:S(2)}, u32[]{:S(2)}) collective-permute-start(f32[64,128]{1,0:T(8,128)S(1)} %get-tuple-element.70), channel_id=1, source_target_pairs={{0,16},{4,20},{8,24},{12,28},{16,0},{20,4},{24,8},{28,12},{1,17},{... | collective-permute-start | bytes 98312 | tf_op jit(solution)/shard_map/ppermute | solution.py:269
  10.0 4.9 %collective-permute-start.4 = (f32[64,128]{1,0:T(8,128)S(1)}, f32[64,128]{1,0:T(8,128)S(1)}, u32[]{:S(2)}, u32[]{:S(2)}) collective-permute-start(f32[64,128]{1,0:T(8,128)S(1)} %get-tuple-element.62), channel_id=1, source_target_pairs={{0,13},{1,12},{2,15},{3,14},{4,9},{5,8},{6,11},{7,10},{8,5},{9,4},... | collective-permute-start | bytes 98312 | tf_op jit(solution)/shard_map/ppermute | solution.py:238
  11.9 3.4 %collective-permute-start.5 = (f32[64,128]{1,0:T(8,128)S(1)}, f32[64,128]{1,0:T(8,128)S(1)}, u32[]{:S(2)}, u32[]{:S(2)}) collective-permute-start(f32[64,128]{1,0:T(8,128)S(1)} %get-tuple-element.63), channel_id=1, source_target_pairs={{0,9},{1,8},{2,11},{3,10},{4,13},{5,12},{6,15},{7,14},{8,1},{9,0},... | collective-permute-start | bytes 98312 | tf_op jit(solution)/shard_map/ppermute | solution.py:238
  12.6 3.6 %collective-permute-start.6 = (f32[64,128]{1,0:T(8,128)S(1)}, f32[64,128]{1,0:T(8,128)S(1)}, u32[]{:S(2)}, u32[]{:S(2)}) collective-permute-start(f32[64,128]{1,0:T(8,128)S(1)} %get-tuple-element.64), channel_id=1, source_target_pairs={{0,5},{1,4},{2,7},{3,6},{4,1},{5,0},{6,3},{7,2},{8,13},{9,12},{10,... | collective-permute-start | bytes 98312 | tf_op jit(solution)/shard_map/ppermute | solution.py:238
  12.8 5.0 %collective-permute-start.7 = (f32[64,128]{1,0:T(8,128)S(1)}, f32[64,128]{1,0:T(8,128)S(1)}, u32[]{:S(2)}, u32[]{:S(2)}) collective-permute-start(f32[64,128]{1,0:T(8,128)S(1)} %get-tuple-element.65), channel_id=1, source_target_pairs={{0,1},{1,0},{2,3},{3,2},{4,5},{5,4},{6,7},{7,6},{8,9},{9,8},{10,11... | collective-permute-start | bytes 98312 | tf_op jit(solution)/shard_map/ppermute | solution.py:238
  14.7 3.1 %collective-permute-start.11 = (f32[64,128]{1,0:T(8,128)S(1)}, f32[64,128]{1,0:T(8,128)S(1)}, u32[]{:S(2)}, u32[]{:S(2)}) collective-permute-start(f32[64,128]{1,0:T(8,128)S(1)} %get-tuple-element.71), channel_id=1, source_target_pairs={{0,1},{1,0},{2,3},{3,2},{4,5},{5,4},{6,7},{7,6},{8,9},{9,8},{10,11... | collective-permute-start | bytes 98312 | tf_op jit(solution)/shard_map/ppermute | solution.py:238
  14.9 2.9 %collective-permute-start.12 = (f32[64,128]{1,0:T(8,128)S(1)}, f32[64,128]{1,0:T(8,128)S(1)}, u32[]{:S(2)}, u32[]{:S(2)}) collective-permute-start(f32[64,128]{1,0:T(8,128)S(1)} %get-tuple-element.72), channel_id=1, source_target_pairs={{0,1},{1,0},{2,3},{3,2},{4,5},{5,4},{6,7},{7,6},{8,9},{9,8},{10,11... | collective-permute-start | bytes 98312 | tf_op jit(solution)/shard_map/ppermute | solution.py:238
  15.3 2.6 %collective-permute-start.13 = (f32[64,128]{1,0:T(8,128)S(1)}, f32[64,128]{1,0:T(8,128)S(1)}, u32[]{:S(2)}, u32[]{:S(2)}) collective-permute-start(f32[64,128]{1,0:T(8,128)S(1)} %get-tuple-element.73), channel_id=1, source_target_pairs={{0,1},{1,0},{2,3},{3,2},{4,5},{5,4},{6,7},{7,6},{8,9},{9,8},{10,11... | collective-permute-start | bytes 98312 | tf_op jit(solution)/shard_map/ppermute | solution.py:238
  16.2 1.6 %collective-permute-start.14 = (f32[64,128]{1,0:T(8,128)S(1)}, f32[64,128]{1,0:T(8,128)S(1)}, u32[]{:S(2)}, u32[]{:S(2)}) collective-permute-start(f32[64,128]{1,0:T(8,128)S(1)} %get-tuple-element.74), channel_id=1, source_target_pairs={{0,1},{1,0},{2,3},{3,2},{4,5},{5,4},{6,7},{7,6},{8,9},{9,8},{10,11... | collective-permute-start | bytes 98312 | tf_op jit(solution)/shard_map/ppermute | solution.py:238
  18.2 3.1 %collective-permute-start.17 = (f32[2,256]{1,0:T(2,128)S(1)}, f32[2,256]{1,0:T(2,128)S(1)}, u32[]{:S(2)}, u32[]{:S(2)}) collective-permute-start(f32[2,256]{1,0:T(2,128)S(1)} %get-tuple-element.76.refs_0_), channel_id=1, source_target_pairs={{0,3},{1,2},{2,1},{3,0},{4,7},{5,6},{6,5},{7,4},{8,11},{9,10},{10,... | collective-permute-start | bytes 6152 | tf_op jit(solution)/shard_map/ppermute | solution.py:288
  19.8 3.6 %collective-permute-start.16 = (f32[2,256]{1,0:T(2,128)S(1)}, f32[2,256]{1,0:T(2,128)S(1)}, u32[]{:S(2)}, u32[]{:S(2)}) collective-permute-start(f32[2,256]{1,0:T(2,128)S(1)} %get-tuple-element.76.refs_0_), channel_id=1, source_target_pairs={{0,2},{1,3},{2,0},{3,1},{4,6},{5,7},{6,4},{7,5},{8,10},{9,11},{10,... | collective-permute-start | bytes 6152 | tf_op jit(solution)/shard_map/ppermute | solution.py:288
  20.3 3.1 %collective-permute-start.15 = (f32[2,256]{1,0:T(2,128)S(1)}, f32[2,256]{1,0:T(2,128)S(1)}, u32[]{:S(2)}, u32[]{:S(2)}) collective-permute-start(f32[2,256]{1,0:T(2,128)S(1)} %get-tuple-element.76.refs_0_), channel_id=1, source_target_pairs={{0,1},{1,0},{2,3},{3,2},{4,5},{5,4},{6,7},{7,6},{8,9},{9,8},{10,11... | collective-permute-start | bytes 6152 | tf_op jit(solution)/shard_map/ppermute | solution.py:288
  23.8 4.3 %collective-permute-start.18 = (f32[64,128]{1,0:T(8,128)S(1)}, f32[64,128]{1,0:T(8,128)S(1)}, u32[]{:S(2)}, u32[]{:S(2)}) collective-permute-start(f32[64,128]{1,0:T(8,128)S(1)} %get-tuple-element.86), channel_id=1, source_target_pairs={{0,13},{1,12},{2,15},{3,14},{4,9},{5,8},{6,11},{7,10},{8,5},{9,4},... | collective-permute-start | bytes 98312 | tf_op jit(solution)/shard_map/ppermute | solution.py:238
  23.8 4.2 %collective-permute-start.19 = (f32[64,128]{1,0:T(8,128)S(1)}, f32[64,128]{1,0:T(8,128)S(1)}, u32[]{:S(2)}, u32[]{:S(2)}) collective-permute-start(f32[64,128]{1,0:T(8,128)S(1)} %get-tuple-element.87), channel_id=1, source_target_pairs={{0,9},{1,8},{2,11},{3,10},{4,13},{5,12},{6,15},{7,14},{8,1},{9,0},... | collective-permute-start | bytes 98312 | tf_op jit(solution)/shard_map/ppermute | solution.py:238
  25.8 3.7 %collective-permute-start.20 = (f32[64,128]{1,0:T(8,128)S(1)}, f32[64,128]{1,0:T(8,128)S(1)}, u32[]{:S(2)}, u32[]{:S(2)}) collective-permute-start(f32[64,128]{1,0:T(8,128)S(1)} %get-tuple-element.88), channel_id=1, source_target_pairs={{0,5},{1,4},{2,7},{3,6},{4,1},{5,0},{6,3},{7,2},{8,13},{9,12},{10,... | collective-permute-start | bytes 98312 | tf_op jit(solution)/shard_map/ppermute | solution.py:238
  26.7 2.8 %collective-permute-start.21 = (f32[64,128]{1,0:T(8,128)S(1)}, f32[64,128]{1,0:T(8,128)S(1)}, u32[]{:S(2)}, u32[]{:S(2)}) collective-permute-start(f32[64,128]{1,0:T(8,128)S(1)} %get-tuple-element.89), channel_id=1, source_target_pairs={{0,1},{1,0},{2,3},{3,2},{4,5},{5,4},{6,7},{7,6},{8,9},{9,8},{10,11... | collective-permute-start | bytes 98312 | tf_op jit(solution)/shard_map/ppermute | solution.py:238
  29.5 4.9 %collective-permute-start.22 = (f32[64,128]{1,0:T(8,128)S(1)}, f32[64,128]{1,0:T(8,128)S(1)}, u32[]{:S(2)}, u32[]{:S(2)}) collective-permute-start(f32[64,128]{1,0:T(8,128)S(1)} %get-tuple-element.91), channel_id=1, source_target_pairs={{0,16},{4,20},{8,24},{12,28},{16,0},{20,4},{24,8},{28,12},{1,17},{... | collective-permute-start | bytes 98312 | tf_op jit(solution)/shard_map/ppermute | solution.py:269
  31.9 2.6 %collective-permute-start.27 = (f32[64,128]{1,0:T(8,128)S(1)}, f32[64,128]{1,0:T(8,128)S(1)}, u32[]{:S(2)}, u32[]{:S(2)}) collective-permute-start(f32[64,128]{1,0:T(8,128)S(1)} %get-tuple-element.96), channel_id=1, source_target_pairs={{0,1},{1,0},{2,3},{3,2},{4,5},{5,4},{6,7},{7,6},{8,9},{9,8},{10,11... | collective-permute-start | bytes 98312 | tf_op jit(solution)/shard_map/ppermute | solution.py:238
  32.0 4.8 %collective-permute-start.28 = (f32[64,128]{1,0:T(8,128)S(1)}, f32[64,128]{1,0:T(8,128)S(1)}, u32[]{:S(2)}, u32[]{:S(2)}) collective-permute-start(f32[64,128]{1,0:T(8,128)S(1)} %get-tuple-element.97), channel_id=1, source_target_pairs={{0,1},{1,0},{2,3},{3,2},{4,5},{5,4},{6,7},{7,6},{8,9},{9,8},{10,11... | collective-permute-start | bytes 98312 | tf_op jit(solution)/shard_map/ppermute | solution.py:238
  32.4 4.7 %collective-permute-start.29 = (f32[64,128]{1,0:T(8,128)S(1)}, f32[64,128]{1,0:T(8,128)S(1)}, u32[]{:S(2)}, u32[]{:S(2)}) collective-permute-start(f32[64,128]{1,0:T(8,128)S(1)} %get-tuple-element.98), channel_id=1, source_target_pairs={{0,1},{1,0},{2,3},{3,2},{4,5},{5,4},{6,7},{7,6},{8,9},{9,8},{10,11... | collective-permute-start | bytes 98312 | tf_op jit(solution)/shard_map/ppermute | solution.py:238
  32.5 6.7 %collective-permute-start.30 = (f32[64,128]{1,0:T(8,128)S(1)}, f32[64,128]{1,0:T(8,128)S(1)}, u32[]{:S(2)}, u32[]{:S(2)}) collective-permute-start(f32[64,128]{1,0:T(8,128)S(1)} %get-tuple-element.99), channel_id=1, source_target_pairs={{0,1},{1,0},{2,3},{3,2},{4,5},{5,4},{6,7},{7,6},{8,9},{9,8},{10,11... | collective-permute-start | bytes 98312 | tf_op jit(solution)/shard_map/ppermute | solution.py:238
  34.4 4.8 %collective-permute-start.23 = (f32[64,128]{1,0:T(8,128)S(1)}, f32[64,128]{1,0:T(8,128)S(1)}, u32[]{:S(2)}, u32[]{:S(2)}) collective-permute-start(f32[64,128]{1,0:T(8,128)S(1)} %get-tuple-element.92), channel_id=1, source_target_pairs={{0,13},{1,12},{2,15},{3,14},{4,9},{5,8},{6,11},{7,10},{8,5},{9,4},... | collective-permute-start | bytes 98312 | tf_op jit(solution)/shard_map/ppermute | solution.py:238
  34.5 4.7 %collective-permute-start.24 = (f32[64,128]{1,0:T(8,128)S(1)}, f32[64,128]{1,0:T(8,128)S(1)}, u32[]{:S(2)}, u32[]{:S(2)}) collective-permute-start(f32[64,128]{1,0:T(8,128)S(1)} %get-tuple-element.93), channel_id=1, source_target_pairs={{0,9},{1,8},{2,11},{3,10},{4,13},{5,12},{6,15},{7,14},{8,1},{9,0},... | collective-permute-start | bytes 98312 | tf_op jit(solution)/shard_map/ppermute | solution.py:238
  36.7 3.6 %collective-permute-start.25 = (f32[64,128]{1,0:T(8,128)S(1)}, f32[64,128]{1,0:T(8,128)S(1)}, u32[]{:S(2)}, u32[]{:S(2)}) collective-permute-start(f32[64,128]{1,0:T(8,128)S(1)} %get-tuple-element.94), channel_id=1, source_target_pairs={{0,5},{1,4},{2,7},{3,6},{4,1},{5,0},{6,3},{7,2},{8,13},{9,12},{10,... | collective-permute-start | bytes 98312 | tf_op jit(solution)/shard_map/ppermute | solution.py:238
  37.1 3.2 %collective-permute-start.26 = (f32[64,128]{1,0:T(8,128)S(1)}, f32[64,128]{1,0:T(8,128)S(1)}, u32[]{:S(2)}, u32[]{:S(2)}) collective-permute-start(f32[64,128]{1,0:T(8,128)S(1)} %get-tuple-element.95), channel_id=1, source_target_pairs={{0,1},{1,0},{2,3},{3,2},{4,5},{5,4},{6,7},{7,6},{8,9},{9,8},{10,11... | collective-permute-start | bytes 98312 | tf_op jit(solution)/shard_map/ppermute | solution.py:238

commit v3 on v1

--- a/solution.py
+++ b/solution.py
@@ -71,7 +71,7 @@
 
 def take(ins, scratch, group):
     if len(ins) == 1:
-        scratch[...] = ins[0][...].reshape(scratch.shape)
+        scratch[...] = ins[0][...].reshape(scratch.shape).astype(scratch.dtype)
         return
     place = lax.rem(lax.axis_index("ctx"), group)
     for i, piece in enumerate(ins):
@@ -145,7 +145,7 @@
     place = lax.rem(lax.axis_index("ctx"), group)
     for i in range(many):
         rows = rows_of(scratch, group, lax.bitwise_xor(place, partner(i, group)))
-        rows[...] = jnp.where(early, pieces[i][...], pieces[many + i][...])
+        rows[...] = jnp.where(early, pieces[i][...], pieces[many + i][...]).astype(scratch.dtype)
 
 
 def scores_body(heads, factor, k, v, q_hbm, og_hbm, gain_hbm, scores, attended, q, weighted, gain, og, sems):
@@ -169,12 +169,14 @@
     power = 0.0
     inner = 0.0
     for h in range(heads):
-        att = factor * dot(q[:, head(h)], prefix[head(h), :].astype(BF16), NN) + local[:, head(h)]
+        att = factor * dot(q[:, head(h)], prefix[head(h), :], NN) + local[:, head(h)]
         attended[:, head(h)] = att
         power = power + att * att
         inner = inner + weighted[:, head(h)] * att
-    stats[0:1, :] = jnp.sum(power.T, axis=0, keepdims=True)
-    stats[1:2, :] = jnp.sum(inner.T, axis=0, keepdims=True)
+    lane = lax.broadcasted_iota(jnp.int32, power.shape, 1)
+    power = jnp.sum(power, axis=1, keepdims=True)
+    inner = jnp.sum(inner, axis=1, keepdims=True)
+    stats[...] = jnp.where(lane == 0, power, inner)[:, :8].T[:2, :]
 
 
 def grad_body(heads, features, group, ways, attended, weighted, q, *refs):
@@ -184,9 +186,10 @@
         total = total + other[...]
     inv_rms = lax.rsqrt(total[0:1, :] / features + epsilon)
     bend = inv_rms * inv_rms * (total[1:2, :] / features)
-    tokens = q.shape[0]
-    inv_rms = jnp.broadcast_to(inv_rms, (HEAD, tokens)).T
-    bend = jnp.broadcast_to(bend, (HEAD, tokens)).T
+    row = lax.broadcasted_iota(jnp.int32, (8, q.shape[0]), 0)
+    columns = jnp.where(row == 0, inv_rms, bend).T
+    inv_rms = jnp.broadcast_to(columns[:, 0:1], (q.shape[0], HEAD))
+    bend = jnp.broadcast_to(columns[:, 1:2], (q.shape[0], HEAD))
     spread[...] = inv_rms
     for h in range(heads):
         ga = (inv_rms * (weighted[:, head(h)] - attended[:, head(h)] * bend)).astype(BF16)
@@ -202,7 +205,7 @@
         gah = ga[:, head(h)]
         raw = dot(gah, v[:, head(h)], NT) * factor
         gs = jnp.where(causal, raw, 0.0).astype(BF16)
-        out = factor * dot(gah, prefix[head(h), :].astype(BF16), NT)
+        out = factor * dot(gah, prefix[head(h), :], NT)
         gq[:, head(h)] = (out + dot(gs, k[:, head(h)], NN)).astype(BF16)
         gk_part[:, head(h)] = dot(gs, q[:, head(h)], TN)
         gv_part[:, head(h)] = dot(scores[h], gah, TN)
@@ -219,7 +222,7 @@
         copies.append(copy)
 
     for h in range(heads):
-        suf = suffix[head(h), :].astype(BF16)
+        suf = suffix[head(h), :]
         gk[:, head(h)] = (factor * dot(v[:, head(h)], suf, NT) + gk_part[:, head(h)]).astype(BF16)
         send(h, gk, outs[0])
         gv[:, head(h)] = (factor * dot(k[:, head(h)], suf, NN) + gv_part[:, head(h)]).astype(BF16)
@@ -337,7 +340,7 @@
     )
     attended, stats, prefix = call(
         functools.partial(attend_body, heads, factor, group),
-        (wide, sds((2, tokens), F32), sds((width, HEAD), F32)),
+        (wide, sds((2, tokens), F32), sds((width, HEAD), BF16)),
         q_held, weighted, local, *prefix,
     )
     every = from_all(stats, "tp")
@@ -360,7 +363,7 @@
         (half, half),
         k_held, v_held, gk_part, gv_part, *suffix,
         dests=(HBM, HBM),
-        scratch=[state, held, held, pltpu.SemaphoreType.DMA((2 * heads,))],
+        scratch=[pltpu.VMEM((width, HEAD), BF16), held, held, pltpu.SemaphoreType.DMA((2 * heads,))],
     )
     return normed, grad_q, grad_k, grad_v
 

time: 41 us -> 41.2 us (level)
  no operation moved by 1% of the time
where the time goes in v3:
time: 41.2 us; the launch traced here: 41.1 us
  starting transfers between devices  23.3 us (57%)
  waiting for transfers between devices  11 us (27%)
  Pallas kernels  6.03 us (15%)
  between operations  0.75 us (2%)
    ppermute x26, starting transfers between devices, exchange(): return lax.ppermute(piece, ('ctx', 'tp'), pairs)  18 us
    ppermute x26, waiting for transfers between devices, exchange(): return lax.ppermute(piece, ('ctx', 'tp'), pairs)  6.21 us
    pallas_call x10, Pallas kernels, call(): pl.pallas_call(body, out_shape=outs, in_specs=ins or [VMEM] * len(args),...  6.03 us
    ppermute x2, starting transfers between devices, carried_in(): over = lax.ppermute(total, 'ctx', [(j, j ^ group) for j in both])  3.08 us
    ppermute x2, waiting for transfers between devices, carried_in(): over = lax.ppermute(total, 'ctx', [(j, j ^ group) for j in both])  2.43 us
    ppermute x3, waiting for transfers between devices, from_all(): lax.ppermute(part, axis, [(i, i ^ step if even else (i + step) % count) f...  2.39 us
    ppermute x3, starting transfers between devices, from_all(): lax.ppermute(part, axis, [(i, i ^ step if even else (i + step) % count) f...  2.18 us
  transfers between devices with their start and end apart: 31, of which 12 were waited for; matrix products, arithmetic and copies ran while one was open for 0% of the time, Pallas kernels for 7%

profile of v3, /device:TPU:0, one launch (start us, length us, event | category | flops | bytes accessed | tf_op | source)
XLA Modules:
  0.0 41.1 jit_solution(17501850469364170761)
XLA Ops:
  0.6 1.2 %shard_map.84 = (bf16[256,256]{1,0:T(8,128)(2,1)S(1)}, bf16[256,256]{1,0:T(8,128)(2,1)S(1)}, f32[64,128]{1,0:T(8,128)S(1)}, f32[64,128]{1,0:T(8,128)S(1)}, f32[6...) custom-call(bf16[256,256]{1,0:T(8,128)(2,1)} %k_hbm.1, ...), custom_call_target="tpu_custom_call" | custom-call | flops 10000000 | bytes 262144 | tf_op jit(solution)/shard_map/pallas_call | solution.py:33
  1.9 3.5 %collective-permute-start = (f32[64,128]{1,0:T(8,128)S(1)}, f32[64,128]{1,0:T(8,128)S(1)}, u32[]{:S(2)}, u32[]{:S(2)}) collective-permute-start(f32[64,128]{1,0:T(8,128)S(1)} %get-tuple-element.58), channel_id=1, source_target_pairs={{0,13},{1,12},{2,15},{3,14},{4,9},{5,8},{6,11},{7,10},{8,5},{9,4},... | collective-permute-start | bytes 98312 | tf_op jit(solution)/shard_map/ppermute | solution.py:241
  5.3 0.7 %collective-permute-start.1 = (f32[64,128]{1,0:T(8,128)S(1)}, f32[64,128]{1,0:T(8,128)S(1)}, u32[]{:S(2)}, u32[]{:S(2)}) collective-permute-start(f32[64,128]{1,0:T(8,128)S(1)} %get-tuple-element.59), channel_id=1, source_target_pairs={{0,9},{1,8},{2,11},{3,10},{4,13},{5,12},{6,15},{7,14},{8,1},{9,0},... | collective-permute-start | bytes 98312 | tf_op jit(solution)/shard_map/ppermute | solution.py:241
  6.3 0.5 %collective-permute-start.8 = (f32[64,128]{1,0:T(8,128)S(1)}, f32[64,128]{1,0:T(8,128)S(1)}, u32[]{:S(2)}, u32[]{:S(2)}) collective-permute-start(f32[64,128]{1,0:T(8,128)S(1)} %get-tuple-element.66), channel_id=1, source_target_pairs={{0,1},{1,0},{2,3},{3,2},{4,5},{5,4},{6,7},{7,6},{8,9},{9,8},{10,11... | collective-permute-start | bytes 98312 | tf_op jit(solution)/shard_map/ppermute | solution.py:241
  7.1 0.5 %collective-permute-start.9 = (f32[64,128]{1,0:T(8,128)S(1)}, f32[64,128]{1,0:T(8,128)S(1)}, u32[]{:S(2)}, u32[]{:S(2)}) collective-permute-start(f32[64,128]{1,0:T(8,128)S(1)} %get-tuple-element.68), channel_id=1, source_target_pairs={{0,1},{1,0},{2,3},{3,2},{4,5},{5,4},{6,7},{7,6},{8,9},{9,8},{10,11... | collective-permute-start | bytes 98312 | tf_op jit(solution)/shard_map/ppermute | solution.py:241
  7.6 1.1 %collective-permute-done.1.refs_1_ = f32[64,128]{1,0:T(8,128)S(1)} collective-permute-done((f32[64,128]{1,0:T(8,128)S(1)}, f32[64,128]{1,0:T(8,128)S(1)}, u32[]{:S(2)}, u32[]{:S(2)}) %collective-permute-start.1) | collective-permute-done | bytes 32800 | tf_op jit(solution)/shard_map/ppermute | solution.py:241
  8.7 1.0 %collective-permute-done.2.refs_2_ = f32[64,128]{1,0:T(8,128)S(1)} collective-permute-done((f32[64,128]{1,0:T(8,128)S(1)}, f32[64,128]{1,0:T(8,128)S(1)}, u32[]{:S(2)}, u32[]{:S(2)}) %collective-permute-start.2) | collective-permute-done | bytes 32800 | tf_op jit(solution)/shard_map/ppermute | solution.py:241
  10.0 1.9 %collective-permute-start.4 = (f32[64,128]{1,0:T(8,128)S(1)}, f32[64,128]{1,0:T(8,128)S(1)}, u32[]{:S(2)}, u32[]{:S(2)}) collective-permute-start(f32[64,128]{1,0:T(8,128)S(1)} %get-tuple-element.62), channel_id=1, source_target_pairs={{0,13},{1,12},{2,15},{3,14},{4,9},{5,8},{6,11},{7,10},{8,5},{9,4},... | collective-permute-start | bytes 98312 | tf_op jit(solution)/shard_map/ppermute | solution.py:241
  11.9 0.8 %collective-permute-start.5 = (f32[64,128]{1,0:T(8,128)S(1)}, f32[64,128]{1,0:T(8,128)S(1)}, u32[]{:S(2)}, u32[]{:S(2)}) collective-permute-start(f32[64,128]{1,0:T(8,128)S(1)} %get-tuple-element.63), channel_id=1, source_target_pairs={{0,9},{1,8},{2,11},{3,10},{4,13},{5,12},{6,15},{7,14},{8,1},{9,0},... | collective-permute-start | bytes 98312 | tf_op jit(solution)/shard_map/ppermute | solution.py:241
  12.8 0.5 %collective-permute-start.7 = (f32[64,128]{1,0:T(8,128)S(1)}, f32[64,128]{1,0:T(8,128)S(1)}, u32[]{:S(2)}, u32[]{:S(2)}) collective-permute-start(f32[64,128]{1,0:T(8,128)S(1)} %get-tuple-element.65), channel_id=1, source_target_pairs={{0,1},{1,0},{2,3},{3,2},{4,5},{5,4},{6,7},{7,6},{8,9},{9,8},{10,11... | collective-permute-start | bytes 98312 | tf_op jit(solution)/shard_map/ppermute | solution.py:241
  13.3 1.4 %collective-permute-done.10.refs_4_ = f32[64,128]{1,0:T(8,128)S(1)} collective-permute-done((f32[64,128]{1,0:T(8,128)S(1)}, f32[64,128]{1,0:T(8,128)S(1)}, u32[]{:S(2)}, u32[]{:S(2)}) %collective-permute-start.10) | collective-permute-done | bytes 32800 | tf_op jit(solution)/shard_map/ppermute | solution.py:272
  14.9 0.4 collective-permute-start.12
  15.3 0.9 %collective-permute-start.13 = (f32[64,128]{1,0:T(8,128)S(1)}, f32[64,128]{1,0:T(8,128)S(1)}, u32[]{:S(2)}, u32[]{:S(2)}) collective-permute-start(f32[64,128]{1,0:T(8,128)S(1)} %get-tuple-element.73), channel_id=1, source_target_pairs={{0,1},{1,0},{2,3},{3,2},{4,5},{5,4},{6,7},{7,6},{8,9},{9,8},{10,11... | collective-permute-start | bytes 98312 | tf_op jit(solution)/shard_map/ppermute | solution.py:241
  16.3 1.5 %shard_map.85 = (bf16[2,256,256]{2,1,0:T(8,128)(2,1)S(1)}, f32[256,256]{1,0:T(8,128)S(1)}, bf16[256,256]{1,0:T(8,128)(2,1)S(1)}, f32[256,256]{1,0:T(8,128)S(1)}, f32[2,128]{1,0:T(2,128)S(1)}) custom-call(bf16[256,256]{1,0:T(8,128)(2,1)S(1)} %get-tuple-element.53.k, bf16[256,256]{1,0:T(8,128)(2,1)S(1)} %get-tuple-element.54.v, bf16[256,256]{1,0:T(8,128)(2,1)} %q_hbm.1, ...), custom_call_target="tpu_custom_call" | custom-call | flops 67108864 | bytes 525312 | tf_op jit(solution)/shard_map/pallas_call | solution.py:33
  18.2 1.6 %collective-permute-start.17 = (f32[2,256]{1,0:T(2,128)S(1)}, f32[2,256]{1,0:T(2,128)S(1)}, u32[]{:S(2)}, u32[]{:S(2)}) collective-permute-start(f32[2,256]{1,0:T(2,128)S(1)} %get-tuple-element.76.refs_0_), channel_id=1, source_target_pairs={{0,2},{1,3},{2,0},{3,1},{4,6},{5,7},{6,4},{7,5},{8,10},{9,11},{10,... | collective-permute-start | bytes 6152 | tf_op jit(solution)/shard_map/ppermute | solution.py:292
  20.4 1.4 %collective-permute-done.17.refs_3_ = f32[2,256]{1,0:T(2,128)S(1)} collective-permute-done((f32[2,256]{1,0:T(2,128)S(1)}, f32[2,256]{1,0:T(2,128)S(1)}, u32[]{:S(2)}, u32[]{:S(2)}) %collective-permute-start.17) | collective-permute-done | bytes 2080 | tf_op jit(solution)/shard_map/ppermute | solution.py:292
  21.8 0.9 %collective-permute-done.16.refs_2_ = f32[2,256]{1,0:T(2,128)S(1)} collective-permute-done((f32[2,256]{1,0:T(2,128)S(1)}, f32[2,256]{1,0:T(2,128)S(1)}, u32[]{:S(2)}, u32[]{:S(2)}) %collective-permute-start.16) | collective-permute-done | bytes 2080 | tf_op jit(solution)/shard_map/ppermute | solution.py:292
  22.8 0.5 %shard_map.89 = (f32[256,128]{1,0:T(8,128)S(1)}, bf16[256,256]{1,0:T(8,128)(2,1)S(1)}, f32[64,128]{1,0:T(8,128)S(1)}, f32[64,128]{1,0:T(8,128)S(1)}, f32[64,128]{1,0:T(8,128)S(1)}, /*index=5*/f32[64,128]{1,0:T(8,128)S(1)}) custom-call(f32[256,256]{1,0:T(8,128)S(1)} %get-tuple-element.75.attended, f32[256,256]{1,0:T(8,128)S(1)} %get-tuple-element.56.weighted, ...), custom_call_target="tpu_custom_call" | custom-call | flops 10000000 | bytes 663552 | tf_op jit(solution)/shard_map/pallas_call | solution.py:33
  23.3 1.3 %collective-permute-start.18 = (f32[64,128]{1,0:T(8,128)S(1)}, f32[64,128]{1,0:T(8,128)S(1)}, u32[]{:S(2)}, u32[]{:S(2)}) collective-permute-start(f32[64,128]{1,0:T(8,128)S(1)} %get-tuple-element.86), channel_id=1, source_target_pairs={{0,13},{1,12},{2,15},{3,14},{4,9},{5,8},{6,11},{7,10},{8,5},{9,4},... | collective-permute-start | bytes 98312 | tf_op jit(solution)/shard_map/ppermute | solution.py:241
  24.6 0.9 %collective-permute-start.19 = (f32[64,128]{1,0:T(8,128)S(1)}, f32[64,128]{1,0:T(8,128)S(1)}, u32[]{:S(2)}, u32[]{:S(2)}) collective-permute-start(f32[64,128]{1,0:T(8,128)S(1)} %get-tuple-element.87), channel_id=1, source_target_pairs={{0,9},{1,8},{2,11},{3,10},{4,13},{5,12},{6,15},{7,14},{8,1},{9,0},... | collective-permute-start | bytes 98312 | tf_op jit(solution)/shard_map/ppermute | solution.py:241
  25.5 0.9 %collective-permute-start.20 = (f32[64,128]{1,0:T(8,128)S(1)}, f32[64,128]{1,0:T(8,128)S(1)}, u32[]{:S(2)}, u32[]{:S(2)}) collective-permute-start(f32[64,128]{1,0:T(8,128)S(1)} %get-tuple-element.88), channel_id=1, source_target_pairs={{0,5},{1,4},{2,7},{3,6},{4,1},{5,0},{6,3},{7,2},{8,13},{9,12},{10,... | collective-permute-start | bytes 98312 | tf_op jit(solution)/shard_map/ppermute | solution.py:241
  26.7 0.9 %collective-permute-done.18.refs_0_ = f32[64,128]{1,0:T(8,128)S(1)} collective-permute-done((f32[64,128]{1,0:T(8,128)S(1)}, f32[64,128]{1,0:T(8,128)S(1)}, u32[]{:S(2)}, u32[]{:S(2)}) %collective-permute-start.18) | collective-permute-done | bytes 32800 | tf_op jit(solution)/shard_map/ppermute | solution.py:241
  27.9 1.0 %collective-permute-done.20.refs_2_ = f32[64,128]{1,0:T(8,128)S(1)} collective-permute-done((f32[64,128]{1,0:T(8,128)S(1)}, f32[64,128]{1,0:T(8,128)S(1)}, u32[]{:S(2)}, u32[]{:S(2)}) %collective-permute-start.20) | collective-permute-done | bytes 32800 | tf_op jit(solution)/shard_map/ppermute | solution.py:241
  29.0 2.8 %collective-permute-start.22 = (f32[64,128]{1,0:T(8,128)S(1)}, f32[64,128]{1,0:T(8,128)S(1)}, u32[]{:S(2)}, u32[]{:S(2)}) collective-permute-start(f32[64,128]{1,0:T(8,128)S(1)} %get-tuple-element.91), channel_id=1, source_target_pairs={{0,16},{4,20},{8,24},{12,28},{16,0},{20,4},{24,8},{28,12},{1,17},{... | collective-permute-start | bytes 98312 | tf_op jit(solution)/shard_map/ppermute | solution.py:272
  31.8 0.4 %collective-permute-start.28 = (f32[64,128]{1,0:T(8,128)S(1)}, f32[64,128]{1,0:T(8,128)S(1)}, u32[]{:S(2)}, u32[]{:S(2)}) collective-permute-start(f32[64,128]{1,0:T(8,128)S(1)} %get-tuple-element.97), channel_id=1, source_target_pairs={{0,1},{1,0},{2,3},{3,2},{4,5},{5,4},{6,7},{7,6},{8,9},{9,8},{10,11... | collective-permute-start | bytes 98312 | tf_op jit(solution)/shard_map/ppermute | solution.py:241
  32.3 0.4 %collective-permute-start.30 = (f32[64,128]{1,0:T(8,128)S(1)}, f32[64,128]{1,0:T(8,128)S(1)}, u32[]{:S(2)}, u32[]{:S(2)}) collective-permute-start(f32[64,128]{1,0:T(8,128)S(1)} %get-tuple-element.99), channel_id=1, source_target_pairs={{0,1},{1,0},{2,3},{3,2},{4,5},{5,4},{6,7},{7,6},{8,9},{9,8},{10,11... | collective-permute-start | bytes 98312 | tf_op jit(solution)/shard_map/ppermute | solution.py:241
  32.8 1.1 %collective-permute-done.22.over = f32[64,128]{1,0:T(8,128)S(1)} collective-permute-done((f32[64,128]{1,0:T(8,128)S(1)}, f32[64,128]{1,0:T(8,128)S(1)}, u32[]{:S(2)}, u32[]{:S(2)}) %collective-permute-start.22) | collective-permute-done | bytes 32800 | tf_op jit(solution)/shard_map/ppermute | solution.py:272
  33.9 1.2 %collective-permute-start.23 = (f32[64,128]{1,0:T(8,128)S(1)}, f32[64,128]{1,0:T(8,128)S(1)}, u32[]{:S(2)}, u32[]{:S(2)}) collective-permute-start(f32[64,128]{1,0:T(8,128)S(1)} %get-tuple-element.92), channel_id=1, source_target_pairs={{0,13},{1,12},{2,15},{3,14},{4,9},{5,8},{6,11},{7,10},{8,5},{9,4},... | collective-permute-start | bytes 98312 | tf_op jit(solution)/shard_map/ppermute | solution.py:241
  35.1 1.6 %collective-permute-start.24 = (f32[64,128]{1,0:T(8,128)S(1)}, f32[64,128]{1,0:T(8,128)S(1)}, u32[]{:S(2)}, u32[]{:S(2)}) collective-permute-start(f32[64,128]{1,0:T(8,128)S(1)} %get-tuple-element.93), channel_id=1, source_target_pairs={{0,9},{1,8},{2,11},{3,10},{4,13},{5,12},{6,15},{7,14},{8,1},{9,0},... | collective-permute-start | bytes 98312 | tf_op jit(solution)/shard_map/ppermute | solution.py:241
  37.3 1.4 %shard_map.90 = (bf16[256,256]{1,0:T(8,128)(2,1)}, bf16[256,256]{1,0:T(8,128)(2,1)}, f32[256,256]{1,0:T(8,128)S(1)}, f32[256,256]{1,0:T(8,128)S(1)}) custom-call(bf16[256,256]{1,0:T(8,128)(2,1)S(1)} %get-tuple-element.77.ga, bf16[256,256]{1,0:T(8,128)(2,1)S(1)} %get-tuple-element.55.q, bf16[256,256]{1,0:T(8,128)(2,1)S(1)} %get-tuple-element.53.k, ...), custom_call_target="tpu_custom_call" | custom-call | flops 150994944 | bytes 1246208 | tf_op jit(solution)/shard_map/pallas_call | solution.py:33
  38.7 1.5 %collective-permute-done.25.refs_2_ = f32[64,128]{1,0:T(8,128)S(1)} collective-permute-done((f32[64,128]{1,0:T(8,128)S(1)}, f32[64,128]{1,0:T(8,128)S(1)}, u32[]{:S(2)}, u32[]{:S(2)}) %collective-permute-start.25) | collective-permute-done | bytes 32800 | tf_op jit(solution)/shard_map/ppermute | solution.py:241
  40.1 0.9 %shard_map.93 = (bf16[256,256]{1,0:T(8,128)(2,1)}, bf16[256,256]{1,0:T(8,128)(2,1)}) custom-call(bf16[256,256]{1,0:T(8,128)(2,1)S(1)} %get-tuple-element.53.k, bf16[256,256]{1,0:T(8,128)(2,1)S(1)} %get-tuple-element.54.v, f32[256,256]{1,0:T(8,128)S(1)} %get-tuple-element.84.gk_part, f32[256,256]{1,0:T(8,128)S(1)} %get-tuple-element.85.gv_part, ...), custom_call_target="tpu_custom_call" | custom-call | flops 10000000 | bytes 1048576 | tf_op jit(solution)/shard_map/pallas_call | solution.py:33
  (40 shorter events, 3.7 us)
Async XLA Ops:
  1.9 5.2 %collective-permute-start = (f32[64,128]{1,0:T(8,128)S(1)}, f32[64,128]{1,0:T(8,128)S(1)}, u32[]{:S(2)}, u32[]{:S(2)}) collective-permute-start(f32[64,128]{1,0:T(8,128)S(1)} %get-tuple-element.58), channel_id=1, source_target_pairs={{0,13},{1,12},{2,15},{3,14},{4,9},{5,8},{6,11},{7,10},{8,5},{9,4},... | collective-permute-start | bytes 98312 | tf_op jit(solution)/shard_map/ppermute | solution.py:241
  5.3 3.3 %collective-permute-start.1 = (f32[64,128]{1,0:T(8,128)S(1)}, f32[64,128]{1,0:T(8,128)S(1)}, u32[]{:S(2)}, u32[]{:S(2)}) collective-permute-start(f32[64,128]{1,0:T(8,128)S(1)} %get-tuple-element.59), channel_id=1, source_target_pairs={{0,9},{1,8},{2,11},{3,10},{4,13},{5,12},{6,15},{7,14},{8,1},{9,0},... | collective-permute-start | bytes 98312 | tf_op jit(solution)/shard_map/ppermute | solution.py:241
  6.1 3.6 %collective-permute-start.2 = (f32[64,128]{1,0:T(8,128)S(1)}, f32[64,128]{1,0:T(8,128)S(1)}, u32[]{:S(2)}, u32[]{:S(2)}) collective-permute-start(f32[64,128]{1,0:T(8,128)S(1)} %get-tuple-element.60), channel_id=1, source_target_pairs={{0,5},{1,4},{2,7},{3,6},{4,1},{5,0},{6,3},{7,2},{8,13},{9,12},{10,... | collective-permute-start | bytes 98312 | tf_op jit(solution)/shard_map/ppermute | solution.py:241
  6.3 3.4 %collective-permute-start.3 = (f32[64,128]{1,0:T(8,128)S(1)}, f32[64,128]{1,0:T(8,128)S(1)}, u32[]{:S(2)}, u32[]{:S(2)}) collective-permute-start(f32[64,128]{1,0:T(8,128)S(1)} %get-tuple-element.61), channel_id=1, source_target_pairs={{0,1},{1,0},{2,3},{3,2},{4,5},{5,4},{6,7},{7,6},{8,9},{9,8},{10,11... | collective-permute-start | bytes 98312 | tf_op jit(solution)/shard_map/ppermute | solution.py:241
  6.3 6.4 %collective-permute-start.8 = (f32[64,128]{1,0:T(8,128)S(1)}, f32[64,128]{1,0:T(8,128)S(1)}, u32[]{:S(2)}, u32[]{:S(2)}) collective-permute-start(f32[64,128]{1,0:T(8,128)S(1)} %get-tuple-element.66), channel_id=1, source_target_pairs={{0,1},{1,0},{2,3},{3,2},{4,5},{5,4},{6,7},{7,6},{8,9},{9,8},{10,11... | collective-permute-start | bytes 98312 | tf_op jit(solution)/shard_map/ppermute | solution.py:241
  7.1 5.6 %collective-permute-start.9 = (f32[64,128]{1,0:T(8,128)S(1)}, f32[64,128]{1,0:T(8,128)S(1)}, u32[]{:S(2)}, u32[]{:S(2)}) collective-permute-start(f32[64,128]{1,0:T(8,128)S(1)} %get-tuple-element.68), channel_id=1, source_target_pairs={{0,1},{1,0},{2,3},{3,2},{4,5},{5,4},{6,7},{7,6},{8,9},{9,8},{10,11... | collective-permute-start | bytes 98312 | tf_op jit(solution)/shard_map/ppermute | solution.py:241
  9.7 5.0 %collective-permute-start.10 = (f32[64,128]{1,0:T(8,128)S(1)}, f32[64,128]{1,0:T(8,128)S(1)}, u32[]{:S(2)}, u32[]{:S(2)}) collective-permute-start(f32[64,128]{1,0:T(8,128)S(1)} %get-tuple-element.70), channel_id=1, source_target_pairs={{0,16},{4,20},{8,24},{12,28},{16,0},{20,4},{24,8},{28,12},{1,17},{... | collective-permute-start | bytes 98312 | tf_op jit(solution)/shard_map/ppermute | solution.py:272
  10.0 4.9 %collective-permute-start.4 = (f32[64,128]{1,0:T(8,128)S(1)}, f32[64,128]{1,0:T(8,128)S(1)}, u32[]{:S(2)}, u32[]{:S(2)}) collective-permute-start(f32[64,128]{1,0:T(8,128)S(1)} %get-tuple-element.62), channel_id=1, source_target_pairs={{0,13},{1,12},{2,15},{3,14},{4,9},{5,8},{6,11},{7,10},{8,5},{9,4},... | collective-permute-start | bytes 98312 | tf_op jit(solution)/shard_map/ppermute | solution.py:241
  11.9 3.4 %collective-permute-start.5 = (f32[64,128]{1,0:T(8,128)S(1)}, f32[64,128]{1,0:T(8,128)S(1)}, u32[]{:S(2)}, u32[]{:S(2)}) collective-permute-start(f32[64,128]{1,0:T(8,128)S(1)} %get-tuple-element.63), channel_id=1, source_target_pairs={{0,9},{1,8},{2,11},{3,10},{4,13},{5,12},{6,15},{7,14},{8,1},{9,0},... | collective-permute-start | bytes 98312 | tf_op jit(solution)/shard_map/ppermute | solution.py:241
  12.6 3.6 %collective-permute-start.6 = (f32[64,128]{1,0:T(8,128)S(1)}, f32[64,128]{1,0:T(8,128)S(1)}, u32[]{:S(2)}, u32[]{:S(2)}) collective-permute-start(f32[64,128]{1,0:T(8,128)S(1)} %get-tuple-element.64), channel_id=1, source_target_pairs={{0,5},{1,4},{2,7},{3,6},{4,1},{5,0},{6,3},{7,2},{8,13},{9,12},{10,... | collective-permute-start | bytes 98312 | tf_op jit(solution)/shard_map/ppermute | solution.py:241
  12.8 5.0 %collective-permute-start.7 = (f32[64,128]{1,0:T(8,128)S(1)}, f32[64,128]{1,0:T(8,128)S(1)}, u32[]{:S(2)}, u32[]{:S(2)}) collective-permute-start(f32[64,128]{1,0:T(8,128)S(1)} %get-tuple-element.65), channel_id=1, source_target_pairs={{0,1},{1,0},{2,3},{3,2},{4,5},{5,4},{6,7},{7,6},{8,9},{9,8},{10,11... | collective-permute-start | bytes 98312 | tf_op jit(solution)/shard_map/ppermute | solution.py:241
  14.7 3.1 %collective-permute-start.11 = (f32[64,128]{1,0:T(8,128)S(1)}, f32[64,128]{1,0:T(8,128)S(1)}, u32[]{:S(2)}, u32[]{:S(2)}) collective-permute-start(f32[64,128]{1,0:T(8,128)S(1)} %get-tuple-element.71), channel_id=1, source_target_pairs={{0,1},{1,0},{2,3},{3,2},{4,5},{5,4},{6,7},{7,6},{8,9},{9,8},{10,11... | collective-permute-start | bytes 98312 | tf_op jit(solution)/shard_map/ppermute | solution.py:241
  14.9 2.9 %collective-permute-start.12 = (f32[64,128]{1,0:T(8,128)S(1)}, f32[64,128]{1,0:T(8,128)S(1)}, u32[]{:S(2)}, u32[]{:S(2)}) collective-permute-start(f32[64,128]{1,0:T(8,128)S(1)} %get-tuple-element.72), channel_id=1, source_target_pairs={{0,1},{1,0},{2,3},{3,2},{4,5},{5,4},{6,7},{7,6},{8,9},{9,8},{10,11... | collective-permute-start | bytes 98312 | tf_op jit(solution)/shard_map/ppermute | solution.py:241
  15.3 2.6 %collective-permute-start.13 = (f32[64,128]{1,0:T(8,128)S(1)}, f32[64,128]{1,0:T(8,128)S(1)}, u32[]{:S(2)}, u32[]{:S(2)}) collective-permute-start(f32[64,128]{1,0:T(8,128)S(1)} %get-tuple-element.73), channel_id=1, source_target_pairs={{0,1},{1,0},{2,3},{3,2},{4,5},{5,4},{6,7},{7,6},{8,9},{9,8},{10,11... | collective-permute-start | bytes 98312 | tf_op jit(solution)/shard_map/ppermute | solution.py:241
  16.2 1.6 %collective-permute-start.14 = (f32[64,128]{1,0:T(8,128)S(1)}, f32[64,128]{1,0:T(8,128)S(1)}, u32[]{:S(2)}, u32[]{:S(2)}) collective-permute-start(f32[64,128]{1,0:T(8,128)S(1)} %get-tuple-element.74), channel_id=1, source_target_pairs={{0,1},{1,0},{2,3},{3,2},{4,5},{5,4},{6,7},{7,6},{8,9},{9,8},{10,11... | collective-permute-start | bytes 98312 | tf_op jit(solution)/shard_map/ppermute | solution.py:241
  18.2 3.6 %collective-permute-start.17 = (f32[2,256]{1,0:T(2,128)S(1)}, f32[2,256]{1,0:T(2,128)S(1)}, u32[]{:S(2)}, u32[]{:S(2)}) collective-permute-start(f32[2,256]{1,0:T(2,128)S(1)} %get-tuple-element.76.refs_0_), channel_id=1, source_target_pairs={{0,2},{1,3},{2,0},{3,1},{4,6},{5,7},{6,4},{7,5},{8,10},{9,11},{10,... | collective-permute-start | bytes 6152 | tf_op jit(solution)/shard_map/ppermute | solution.py:292
  19.8 3.0 %collective-permute-start.16 = (f32[2,256]{1,0:T(2,128)S(1)}, f32[2,256]{1,0:T(2,128)S(1)}, u32[]{:S(2)}, u32[]{:S(2)}) collective-permute-start(f32[2,256]{1,0:T(2,128)S(1)} %get-tuple-element.76.refs_0_), channel_id=1, source_target_pairs={{0,3},{1,2},{2,1},{3,0},{4,7},{5,6},{6,5},{7,4},{8,11},{9,10},{10,... | collective-permute-start | bytes 6152 | tf_op jit(solution)/shard_map/ppermute | solution.py:292
  20.0 2.8 %collective-permute-start.15 = (f32[2,256]{1,0:T(2,128)S(1)}, f32[2,256]{1,0:T(2,128)S(1)}, u32[]{:S(2)}, u32[]{:S(2)}) collective-permute-start(f32[2,256]{1,0:T(2,128)S(1)} %get-tuple-element.76.refs_0_), channel_id=1, source_target_pairs={{0,1},{1,0},{2,3},{3,2},{4,5},{5,4},{6,7},{7,6},{8,9},{9,8},{10,11... | collective-permute-start | bytes 6152 | tf_op jit(solution)/shard_map/ppermute | solution.py:292
  23.3 4.3 %collective-permute-start.18 = (f32[64,128]{1,0:T(8,128)S(1)}, f32[64,128]{1,0:T(8,128)S(1)}, u32[]{:S(2)}, u32[]{:S(2)}) collective-permute-start(f32[64,128]{1,0:T(8,128)S(1)} %get-tuple-element.86), channel_id=1, source_target_pairs={{0,13},{1,12},{2,15},{3,14},{4,9},{5,8},{6,11},{7,10},{8,5},{9,4},... | collective-permute-start | bytes 98312 | tf_op jit(solution)/shard_map/ppermute | solution.py:241
  24.6 3.4 %collective-permute-start.19 = (f32[64,128]{1,0:T(8,128)S(1)}, f32[64,128]{1,0:T(8,128)S(1)}, u32[]{:S(2)}, u32[]{:S(2)}) collective-permute-start(f32[64,128]{1,0:T(8,128)S(1)} %get-tuple-element.87), channel_id=1, source_target_pairs={{0,9},{1,8},{2,11},{3,10},{4,13},{5,12},{6,15},{7,14},{8,1},{9,0},... | collective-permute-start | bytes 98312 | tf_op jit(solution)/shard_map/ppermute | solution.py:241
  25.5 3.4 %collective-permute-start.20 = (f32[64,128]{1,0:T(8,128)S(1)}, f32[64,128]{1,0:T(8,128)S(1)}, u32[]{:S(2)}, u32[]{:S(2)}) collective-permute-start(f32[64,128]{1,0:T(8,128)S(1)} %get-tuple-element.88), channel_id=1, source_target_pairs={{0,5},{1,4},{2,7},{3,6},{4,1},{5,0},{6,3},{7,2},{8,13},{9,12},{10,... | collective-permute-start | bytes 98312 | tf_op jit(solution)/shard_map/ppermute | solution.py:241
  26.4 2.5 %collective-permute-start.21 = (f32[64,128]{1,0:T(8,128)S(1)}, f32[64,128]{1,0:T(8,128)S(1)}, u32[]{:S(2)}, u32[]{:S(2)}) collective-permute-start(f32[64,128]{1,0:T(8,128)S(1)} %get-tuple-element.89), channel_id=1, source_target_pairs={{0,1},{1,0},{2,3},{3,2},{4,5},{5,4},{6,7},{7,6},{8,9},{9,8},{10,11... | collective-permute-start | bytes 98312 | tf_op jit(solution)/shard_map/ppermute | solution.py:241
  29.0 4.9 %collective-permute-start.22 = (f32[64,128]{1,0:T(8,128)S(1)}, f32[64,128]{1,0:T(8,128)S(1)}, u32[]{:S(2)}, u32[]{:S(2)}) collective-permute-start(f32[64,128]{1,0:T(8,128)S(1)} %get-tuple-element.91), channel_id=1, source_target_pairs={{0,16},{4,20},{8,24},{12,28},{16,0},{20,4},{24,8},{28,12},{1,17},{... | collective-permute-start | bytes 98312 | tf_op jit(solution)/shard_map/ppermute | solution.py:272
  31.7 3.3 %collective-permute-start.27 = (f32[64,128]{1,0:T(8,128)S(1)}, f32[64,128]{1,0:T(8,128)S(1)}, u32[]{:S(2)}, u32[]{:S(2)}) collective-permute-start(f32[64,128]{1,0:T(8,128)S(1)} %get-tuple-element.96), channel_id=1, source_target_pairs={{0,1},{1,0},{2,3},{3,2},{4,5},{5,4},{6,7},{7,6},{8,9},{9,8},{10,11... | collective-permute-start | bytes 98312 | tf_op jit(solution)/shard_map/ppermute | solution.py:241
  31.8 4.9 %collective-permute-start.28 = (f32[64,128]{1,0:T(8,128)S(1)}, f32[64,128]{1,0:T(8,128)S(1)}, u32[]{:S(2)}, u32[]{:S(2)}) collective-permute-start(f32[64,128]{1,0:T(8,128)S(1)} %get-tuple-element.97), channel_id=1, source_target_pairs={{0,1},{1,0},{2,3},{3,2},{4,5},{5,4},{6,7},{7,6},{8,9},{9,8},{10,11... | collective-permute-start | bytes 98312 | tf_op jit(solution)/shard_map/ppermute | solution.py:241
  32.3 4.7 %collective-permute-start.29 = (f32[64,128]{1,0:T(8,128)S(1)}, f32[64,128]{1,0:T(8,128)S(1)}, u32[]{:S(2)}, u32[]{:S(2)}) collective-permute-start(f32[64,128]{1,0:T(8,128)S(1)} %get-tuple-element.98), channel_id=1, source_target_pairs={{0,1},{1,0},{2,3},{3,2},{4,5},{5,4},{6,7},{7,6},{8,9},{9,8},{10,11... | collective-permute-start | bytes 98312 | tf_op jit(solution)/shard_map/ppermute | solution.py:241
  32.3 6.3 %collective-permute-start.30 = (f32[64,128]{1,0:T(8,128)S(1)}, f32[64,128]{1,0:T(8,128)S(1)}, u32[]{:S(2)}, u32[]{:S(2)}) collective-permute-start(f32[64,128]{1,0:T(8,128)S(1)} %get-tuple-element.99), channel_id=1, source_target_pairs={{0,1},{1,0},{2,3},{3,2},{4,5},{5,4},{6,7},{7,6},{8,9},{9,8},{10,11... | collective-permute-start | bytes 98312 | tf_op jit(solution)/shard_map/ppermute | solution.py:241
  33.9 4.8 %collective-permute-start.23 = (f32[64,128]{1,0:T(8,128)S(1)}, f32[64,128]{1,0:T(8,128)S(1)}, u32[]{:S(2)}, u32[]{:S(2)}) collective-permute-start(f32[64,128]{1,0:T(8,128)S(1)} %get-tuple-element.92), channel_id=1, source_target_pairs={{0,13},{1,12},{2,15},{3,14},{4,9},{5,8},{6,11},{7,10},{8,5},{9,4},... | collective-permute-start | bytes 98312 | tf_op jit(solution)/shard_map/ppermute | solution.py:241
  35.1 3.6 %collective-permute-start.24 = (f32[64,128]{1,0:T(8,128)S(1)}, f32[64,128]{1,0:T(8,128)S(1)}, u32[]{:S(2)}, u32[]{:S(2)}) collective-permute-start(f32[64,128]{1,0:T(8,128)S(1)} %get-tuple-element.93), channel_id=1, source_target_pairs={{0,9},{1,8},{2,11},{3,10},{4,13},{5,12},{6,15},{7,14},{8,1},{9,0},... | collective-permute-start | bytes 98312 | tf_op jit(solution)/shard_map/ppermute | solution.py:241
  36.7 3.4 %collective-permute-start.25 = (f32[64,128]{1,0:T(8,128)S(1)}, f32[64,128]{1,0:T(8,128)S(1)}, u32[]{:S(2)}, u32[]{:S(2)}) collective-permute-start(f32[64,128]{1,0:T(8,128)S(1)} %get-tuple-element.94), channel_id=1, source_target_pairs={{0,5},{1,4},{2,7},{3,6},{4,1},{5,0},{6,3},{7,2},{8,13},{9,12},{10,... | collective-permute-start | bytes 98312 | tf_op jit(solution)/shard_map/ppermute | solution.py:241
  37.0 3.1 %collective-permute-start.26 = (f32[64,128]{1,0:T(8,128)S(1)}, f32[64,128]{1,0:T(8,128)S(1)}, u32[]{:S(2)}, u32[]{:S(2)}) collective-permute-start(f32[64,128]{1,0:T(8,128)S(1)} %get-tuple-element.95), channel_id=1, source_target_pairs={{0,1},{1,0},{2,3},{3,2},{4,5},{5,4},{6,7},{7,6},{8,9},{9,8},{10,11... | collective-permute-start | bytes 98312 | tf_op jit(solution)/shard_map/ppermute | solution.py:241

commit v4 on v1

--- a/solution.py
+++ b/solution.py
@@ -56,8 +56,8 @@
     return scratch.at[pl.ds(pl.multiple_of(place * rows, rows), rows), :]
 
 
-def partner(i, group):
-    return group - 1 - i
+def step_of(i, odd):
+    return (3, 2 - odd, 1 + odd, 0)[i]
 
 
 def give(scratch, group, outs):
@@ -65,8 +65,9 @@
         outs[0][...] = scratch[...].reshape(outs[0].shape)
         return
     place = lax.rem(lax.axis_index("ctx"), group)
+    odd = lax.rem(lax.axis_index("tp"), 2)
     for i, out in enumerate(outs):
-        out[...] = rows_of(scratch, group, lax.bitwise_xor(place, partner(i, group)))[...]
+        out[...] = rows_of(scratch, group, lax.bitwise_xor(place, step_of(i, odd)))[...]
 
 
 def take(ins, scratch, group):
@@ -74,8 +75,9 @@
         scratch[...] = ins[0][...].reshape(scratch.shape)
         return
     place = lax.rem(lax.axis_index("ctx"), group)
+    odd = 1 - lax.rem(lax.axis_index("tp"), 2)
     for i, piece in enumerate(ins):
-        rows_of(scratch, group, lax.bitwise_xor(place, partner(i, group)))[...] = piece[...]
+        rows_of(scratch, group, lax.bitwise_xor(place, step_of(i, odd)))[...] = piece[...]
 
 
 def running_sums(scratch, parts, reverse):
@@ -125,8 +127,9 @@
 
 def add_body(group, sums, over, *outs):
     place = lax.rem(lax.axis_index("ctx"), group)
+    odd = lax.rem(lax.axis_index("tp"), 2)
     for i, out in enumerate(outs):
-        out[...] = rows_of(sums, group, lax.bitwise_xor(place, partner(i, group)))[...] + over[...]
+        out[...] = rows_of(sums, group, lax.bitwise_xor(place, step_of(i, odd)))[...] + over[...]
 
 
 def late_body(group, reverse, *refs):
@@ -143,8 +146,9 @@
         return
     early = lax.axis_index("ctx") < group
     place = lax.rem(lax.axis_index("ctx"), group)
+    odd = 1 - lax.rem(lax.axis_index("tp"), 2)
     for i in range(many):
-        rows = rows_of(scratch, group, lax.bitwise_xor(place, partner(i, group)))
+        rows = rows_of(scratch, group, lax.bitwise_xor(place, step_of(i, odd)))
         rows[...] = jnp.where(early, pieces[i][...], pieces[many + i][...])
 
 
@@ -231,7 +235,7 @@
 def exchange(piece, i, active, group):
     ways = lax.axis_size("tp")
     pairs = [
-        (j * ways + t, (j ^ partner(i, group) if j in active else j) * ways + (t ^ 1))
+        (j * ways + t, (j ^ step_of(i, t % 2) if j in active else j) * ways + (t ^ 1))
         for j in range(2 * group)
         for t in range(ways)
     ]

time: 41 us -> 41.2 us (level)
  starting transfers between devices: 23.2 us -> 25.7 us
  waiting for transfers between devices: 11 us -> 8.83 us
    ppermute x2, starting transfers between devices: 3.02 us -> 4.61 us  [carried_in(): over = lax.ppermute(total, 'ctx', [(j, j ^ group) for j in both])]
    ppermute x2, waiting for transfers between devices: 2.48 us -> 1.24 us  [carried_in(): over = lax.ppermute(total, 'ctx', [(j, j ^ group) for j in both])]
    ppermute x26, waiting for transfers between devices: 6.16 us -> 5.19 us  [exchange(): return lax.ppermute(piece, ('ctx', 'tp'), pairs)]
    ppermute x26, starting transfers between devices: 18 us -> 18.8 us  [exchange(): return lax.ppermute(piece, ('ctx', 'tp'), pairs)]
where the time goes in v4:
time: 41.2 us; the launch traced here: 41.1 us
  starting transfers between devices  25.7 us (62%)
  waiting for transfers between devices  8.83 us (21%)
  Pallas kernels  5.85 us (14%)
  between operations  0.75 us (2%)
    ppermute x26, starting transfers between devices, exchange(): return lax.ppermute(piece, ('ctx', 'tp'), pairs)  18.8 us
    pallas_call x10, Pallas kernels, call(): pl.pallas_call(body, out_shape=outs, in_specs=ins or [VMEM] * len(args),...  5.85 us
    ppermute x26, waiting for transfers between devices, exchange(): return lax.ppermute(piece, ('ctx', 'tp'), pairs)  5.19 us
    ppermute x2, starting transfers between devices, carried_in(): over = lax.ppermute(total, 'ctx', [(j, j ^ group) for j in both])  4.61 us
    ppermute x3, waiting for transfers between devices, from_all(): lax.ppermute(part, axis, [(i, i ^ step if even else (i + step) % count) f...  2.39 us
    ppermute x3, starting transfers between devices, from_all(): lax.ppermute(part, axis, [(i, i ^ step if even else (i + step) % count) f...  2.2 us
    ppermute x2, waiting for transfers between devices, carried_in(): over = lax.ppermute(total, 'ctx', [(j, j ^ group) for j in both])  1.24 us
  transfers between devices with their start and end apart: 31, of which 12 were waited for; matrix products, arithmetic and copies ran while one was open for 0% of the time, Pallas kernels for 7%

profile of v4, /device:TPU:0, one launch (start us, length us, event | category | flops | bytes accessed | tf_op | source)
XLA Modules:
  0.0 41.1 jit_solution(7132151067566986656)
XLA Ops:
  0.6 1.2 %shard_map.84 = (bf16[256,256]{1,0:T(8,128)(2,1)S(1)}, bf16[256,256]{1,0:T(8,128)(2,1)S(1)}, f32[64,128]{1,0:T(8,128)S(1)}, f32[64,128]{1,0:T(8,128)S(1)}, f32[6...) custom-call(bf16[256,256]{1,0:T(8,128)(2,1)} %k_hbm.1, ...), custom_call_target="tpu_custom_call" | custom-call | flops 10000000 | bytes 262144 | tf_op jit(solution)/shard_map/pallas_call | solution.py:33
  1.9 3.5 %collective-permute-start = (f32[64,128]{1,0:T(8,128)S(1)}, f32[64,128]{1,0:T(8,128)S(1)}, u32[]{:S(2)}, u32[]{:S(2)}) collective-permute-start(f32[64,128]{1,0:T(8,128)S(1)} %get-tuple-element.58), channel_id=1, source_target_pairs={{0,13},{1,12},{2,15},{3,14},{4,9},{5,8},{6,11},{7,10},{8,5},{9,4},... | collective-permute-start | bytes 98312 | tf_op jit(solution)/shard_map/ppermute | solution.py:242
  5.3 0.7 %collective-permute-start.1 = (f32[64,128]{1,0:T(8,128)S(1)}, f32[64,128]{1,0:T(8,128)S(1)}, u32[]{:S(2)}, u32[]{:S(2)}) collective-permute-start(f32[64,128]{1,0:T(8,128)S(1)} %get-tuple-element.59), channel_id=1, source_target_pairs={{0,9},{1,4},{2,11},{3,6},{4,13},{5,0},{6,15},{7,2},{8,1},{9,12},{1... | collective-permute-start | bytes 98312 | tf_op jit(solution)/shard_map/ppermute | solution.py:242
  6.1 1.0 %collective-permute-start.2 = (f32[64,128]{1,0:T(8,128)S(1)}, f32[64,128]{1,0:T(8,128)S(1)}, u32[]{:S(2)}, u32[]{:S(2)}) collective-permute-start(f32[64,128]{1,0:T(8,128)S(1)} %get-tuple-element.60), channel_id=1, source_target_pairs={{0,5},{1,8},{2,7},{3,10},{4,1},{5,12},{6,3},{7,14},{8,13},{9,0},{1... | collective-permute-start | bytes 98312 | tf_op jit(solution)/shard_map/ppermute | solution.py:242
  7.1 0.7 %collective-permute-start.3 = (f32[64,128]{1,0:T(8,128)S(1)}, f32[64,128]{1,0:T(8,128)S(1)}, u32[]{:S(2)}, u32[]{:S(2)}) collective-permute-start(f32[64,128]{1,0:T(8,128)S(1)} %get-tuple-element.61), channel_id=1, source_target_pairs={{0,1},{1,0},{2,3},{3,2},{4,5},{5,4},{6,7},{7,6},{8,9},{9,8},{10,11... | collective-permute-start | bytes 98312 | tf_op jit(solution)/shard_map/ppermute | solution.py:242
  7.8 0.5 %collective-permute-start.9 = (f32[64,128]{1,0:T(8,128)S(1)}, f32[64,128]{1,0:T(8,128)S(1)}, u32[]{:S(2)}, u32[]{:S(2)}) collective-permute-start(f32[64,128]{1,0:T(8,128)S(1)} %get-tuple-element.68), channel_id=1, source_target_pairs={{0,1},{1,0},{2,3},{3,2},{4,5},{5,4},{6,7},{7,6},{8,9},{9,8},{10,11... | collective-permute-start | bytes 98312 | tf_op jit(solution)/shard_map/ppermute | solution.py:242
  8.7 1.0 %collective-permute-done.2.refs_2_ = f32[64,128]{1,0:T(8,128)S(1)} collective-permute-done((f32[64,128]{1,0:T(8,128)S(1)}, f32[64,128]{1,0:T(8,128)S(1)}, u32[]{:S(2)}, u32[]{:S(2)}) %collective-permute-start.2) | collective-permute-done | bytes 32800 | tf_op jit(solution)/shard_map/ppermute | solution.py:242
  9.7 0.9 %collective-permute-start.10 = (f32[64,128]{1,0:T(8,128)S(1)}, f32[64,128]{1,0:T(8,128)S(1)}, u32[]{:S(2)}, u32[]{:S(2)}) collective-permute-start(f32[64,128]{1,0:T(8,128)S(1)} %get-tuple-element.70), channel_id=1, source_target_pairs={{0,16},{4,20},{8,24},{12,28},{16,0},{20,4},{24,8},{28,12},{1,17},{... | collective-permute-start | bytes 98312 | tf_op jit(solution)/shard_map/ppermute | solution.py:273
  10.6 1.3 %collective-permute-start.4 = (f32[64,128]{1,0:T(8,128)S(1)}, f32[64,128]{1,0:T(8,128)S(1)}, u32[]{:S(2)}, u32[]{:S(2)}) collective-permute-start(f32[64,128]{1,0:T(8,128)S(1)} %get-tuple-element.62), channel_id=1, source_target_pairs={{0,13},{1,12},{2,15},{3,14},{4,9},{5,8},{6,11},{7,10},{8,5},{9,4},... | collective-permute-start | bytes 98312 | tf_op jit(solution)/shard_map/ppermute | solution.py:242
  11.8 0.8 %collective-permute-start.5 = (f32[64,128]{1,0:T(8,128)S(1)}, f32[64,128]{1,0:T(8,128)S(1)}, u32[]{:S(2)}, u32[]{:S(2)}) collective-permute-start(f32[64,128]{1,0:T(8,128)S(1)} %get-tuple-element.63), channel_id=1, source_target_pairs={{0,9},{1,4},{2,11},{3,6},{4,13},{5,0},{6,15},{7,2},{8,1},{9,12},{1... | collective-permute-start | bytes 98312 | tf_op jit(solution)/shard_map/ppermute | solution.py:242
  12.6 1.0 %collective-permute-start.6 = (f32[64,128]{1,0:T(8,128)S(1)}, f32[64,128]{1,0:T(8,128)S(1)}, u32[]{:S(2)}, u32[]{:S(2)}) collective-permute-start(f32[64,128]{1,0:T(8,128)S(1)} %get-tuple-element.64), channel_id=1, source_target_pairs={{0,5},{1,8},{2,7},{3,10},{4,1},{5,12},{6,3},{7,14},{8,13},{9,0},{1... | collective-permute-start | bytes 98312 | tf_op jit(solution)/shard_map/ppermute | solution.py:242
  13.6 0.7 %collective-permute-start.7 = (f32[64,128]{1,0:T(8,128)S(1)}, f32[64,128]{1,0:T(8,128)S(1)}, u32[]{:S(2)}, u32[]{:S(2)}) collective-permute-start(f32[64,128]{1,0:T(8,128)S(1)} %get-tuple-element.65), channel_id=1, source_target_pairs={{0,1},{1,0},{2,3},{3,2},{4,5},{5,4},{6,7},{7,6},{8,9},{9,8},{10,11... | collective-permute-start | bytes 98312 | tf_op jit(solution)/shard_map/ppermute | solution.py:242
  14.7 0.7 %collective-permute-done.4.refs_0_ = f32[64,128]{1,0:T(8,128)S(1)} collective-permute-done((f32[64,128]{1,0:T(8,128)S(1)}, f32[64,128]{1,0:T(8,128)S(1)}, u32[]{:S(2)}, u32[]{:S(2)}) %collective-permute-start.4) | collective-permute-done | bytes 32800 | tf_op jit(solution)/shard_map/ppermute | solution.py:242
  15.7 0.7 %collective-permute-start.13 = (f32[64,128]{1,0:T(8,128)S(1)}, f32[64,128]{1,0:T(8,128)S(1)}, u32[]{:S(2)}, u32[]{:S(2)}) collective-permute-start(f32[64,128]{1,0:T(8,128)S(1)} %get-tuple-element.73), channel_id=1, source_target_pairs={{0,1},{1,0},{2,3},{3,2},{4,5},{5,4},{6,7},{7,6},{8,9},{9,8},{10,11... | collective-permute-start | bytes 98312 | tf_op jit(solution)/shard_map/ppermute | solution.py:242
  16.3 1.5 %shard_map.85 = (bf16[2,256,256]{2,1,0:T(8,128)(2,1)S(1)}, f32[256,256]{1,0:T(8,128)S(1)}, bf16[256,256]{1,0:T(8,128)(2,1)S(1)}, f32[256,256]{1,0:T(8,128)S(1)}, f32[2,128]{1,0:T(2,128)S(1)}) custom-call(bf16[256,256]{1,0:T(8,128)(2,1)S(1)} %get-tuple-element.53.k, bf16[256,256]{1,0:T(8,128)(2,1)S(1)} %get-tuple-element.54.v, bf16[256,256]{1,0:T(8,128)(2,1)} %q_hbm.1, ...), custom_call_target="tpu_custom_call" | custom-call | flops 67108864 | bytes 525312 | tf_op jit(solution)/shard_map/pallas_call | solution.py:33
  18.2 1.6 %collective-permute-start.17 = (f32[2,256]{1,0:T(2,128)S(1)}, f32[2,256]{1,0:T(2,128)S(1)}, u32[]{:S(2)}, u32[]{:S(2)}) collective-permute-start(f32[2,256]{1,0:T(2,128)S(1)} %get-tuple-element.76.refs_0_), channel_id=1, source_target_pairs={{0,2},{1,3},{2,0},{3,1},{4,6},{5,7},{6,4},{7,5},{8,10},{9,11},{10,... | collective-permute-start | bytes 6152 | tf_op jit(solution)/shard_map/ppermute | solution.py:293
  20.4 1.4 %collective-permute-done.17.refs_3_ = f32[2,256]{1,0:T(2,128)S(1)} collective-permute-done((f32[2,256]{1,0:T(2,128)S(1)}, f32[2,256]{1,0:T(2,128)S(1)}, u32[]{:S(2)}, u32[]{:S(2)}) %collective-permute-start.17) | collective-permute-done | bytes 2080 | tf_op jit(solution)/shard_map/ppermute | solution.py:293
  21.9 0.9 %collective-permute-done.16.refs_2_ = f32[2,256]{1,0:T(2,128)S(1)} collective-permute-done((f32[2,256]{1,0:T(2,128)S(1)}, f32[2,256]{1,0:T(2,128)S(1)}, u32[]{:S(2)}, u32[]{:S(2)}) %collective-permute-start.16) | collective-permute-done | bytes 2080 | tf_op jit(solution)/shard_map/ppermute | solution.py:293
  23.2 1.3 %collective-permute-start.18 = (f32[64,128]{1,0:T(8,128)S(1)}, f32[64,128]{1,0:T(8,128)S(1)}, u32[]{:S(2)}, u32[]{:S(2)}) collective-permute-start(f32[64,128]{1,0:T(8,128)S(1)} %get-tuple-element.86), channel_id=1, source_target_pairs={{0,13},{1,12},{2,15},{3,14},{4,9},{5,8},{6,11},{7,10},{8,5},{9,4},... | collective-permute-start | bytes 98312 | tf_op jit(solution)/shard_map/ppermute | solution.py:242
  24.5 0.9 %collective-permute-start.19 = (f32[64,128]{1,0:T(8,128)S(1)}, f32[64,128]{1,0:T(8,128)S(1)}, u32[]{:S(2)}, u32[]{:S(2)}) collective-permute-start(f32[64,128]{1,0:T(8,128)S(1)} %get-tuple-element.87), channel_id=1, source_target_pairs={{0,9},{1,4},{2,11},{3,6},{4,13},{5,0},{6,15},{7,2},{8,1},{9,12},{1... | collective-permute-start | bytes 98312 | tf_op jit(solution)/shard_map/ppermute | solution.py:242
  25.4 0.8 %collective-permute-start.20 = (f32[64,128]{1,0:T(8,128)S(1)}, f32[64,128]{1,0:T(8,128)S(1)}, u32[]{:S(2)}, u32[]{:S(2)}) collective-permute-start(f32[64,128]{1,0:T(8,128)S(1)} %get-tuple-element.88), channel_id=1, source_target_pairs={{0,5},{1,8},{2,7},{3,10},{4,1},{5,12},{6,3},{7,14},{8,13},{9,0},{1... | collective-permute-start | bytes 98312 | tf_op jit(solution)/shard_map/ppermute | solution.py:242
  26.6 0.8 %collective-permute-done.18.refs_0_ = f32[64,128]{1,0:T(8,128)S(1)} collective-permute-done((f32[64,128]{1,0:T(8,128)S(1)}, f32[64,128]{1,0:T(8,128)S(1)}, u32[]{:S(2)}, u32[]{:S(2)}) %collective-permute-start.18) | collective-permute-done | bytes 32800 | tf_op jit(solution)/shard_map/ppermute | solution.py:242
  27.5 0.7 %collective-permute-done.19.refs_1_ = f32[64,128]{1,0:T(8,128)S(1)} collective-permute-done((f32[64,128]{1,0:T(8,128)S(1)}, f32[64,128]{1,0:T(8,128)S(1)}, u32[]{:S(2)}, u32[]{:S(2)}) %collective-permute-start.19) | collective-permute-done | bytes 32800 | tf_op jit(solution)/shard_map/ppermute | solution.py:242
  28.2 0.6 %collective-permute-done.20.refs_2_ = f32[64,128]{1,0:T(8,128)S(1)} collective-permute-done((f32[64,128]{1,0:T(8,128)S(1)}, f32[64,128]{1,0:T(8,128)S(1)}, u32[]{:S(2)}, u32[]{:S(2)}) %collective-permute-start.20) | collective-permute-done | bytes 32800 | tf_op jit(solution)/shard_map/ppermute | solution.py:242
  28.8 3.7 %collective-permute-start.22 = (f32[64,128]{1,0:T(8,128)S(1)}, f32[64,128]{1,0:T(8,128)S(1)}, u32[]{:S(2)}, u32[]{:S(2)}) collective-permute-start(f32[64,128]{1,0:T(8,128)S(1)} %get-tuple-element.91), channel_id=1, source_target_pairs={{0,16},{4,20},{8,24},{12,28},{16,0},{20,4},{24,8},{28,12},{1,17},{... | collective-permute-start | bytes 98312 | tf_op jit(solution)/shard_map/ppermute | solution.py:273
  32.6 0.5 %collective-permute-start.28 = (f32[64,128]{1,0:T(8,128)S(1)}, f32[64,128]{1,0:T(8,128)S(1)}, u32[]{:S(2)}, u32[]{:S(2)}) collective-permute-start(f32[64,128]{1,0:T(8,128)S(1)} %get-tuple-element.97), channel_id=1, source_target_pairs={{0,1},{1,0},{2,3},{3,2},{4,5},{5,4},{6,7},{7,6},{8,9},{9,8},{10,11... | collective-permute-start | bytes 98312 | tf_op jit(solution)/shard_map/ppermute | solution.py:242
  33.6 1.0 %collective-permute-done.22.over = f32[64,128]{1,0:T(8,128)S(1)} collective-permute-done((f32[64,128]{1,0:T(8,128)S(1)}, f32[64,128]{1,0:T(8,128)S(1)}, u32[]{:S(2)}, u32[]{:S(2)}) %collective-permute-start.22) | collective-permute-done | bytes 32800 | tf_op jit(solution)/shard_map/ppermute | solution.py:273
  34.9 1.8 %collective-permute-start.24 = (f32[64,128]{1,0:T(8,128)S(1)}, f32[64,128]{1,0:T(8,128)S(1)}, u32[]{:S(2)}, u32[]{:S(2)}) collective-permute-start(f32[64,128]{1,0:T(8,128)S(1)} %get-tuple-element.93), channel_id=1, source_target_pairs={{0,9},{1,4},{2,11},{3,6},{4,13},{5,0},{6,15},{7,2},{8,1},{9,12},{1... | collective-permute-start | bytes 98312 | tf_op jit(solution)/shard_map/ppermute | solution.py:242
  36.9 1.1 %collective-permute-start.26 = (f32[64,128]{1,0:T(8,128)S(1)}, f32[64,128]{1,0:T(8,128)S(1)}, u32[]{:S(2)}, u32[]{:S(2)}) collective-permute-start(f32[64,128]{1,0:T(8,128)S(1)} %get-tuple-element.95), channel_id=1, source_target_pairs={{0,1},{1,0},{2,3},{3,2},{4,5},{5,4},{6,7},{7,6},{8,9},{9,8},{10,11... | collective-permute-start | bytes 98312 | tf_op jit(solution)/shard_map/ppermute | solution.py:242
  38.0 1.4 %shard_map.90 = (bf16[256,256]{1,0:T(8,128)(2,1)}, bf16[256,256]{1,0:T(8,128)(2,1)}, f32[256,256]{1,0:T(8,128)S(1)}, f32[256,256]{1,0:T(8,128)S(1)}) custom-call(bf16[256,256]{1,0:T(8,128)(2,1)S(1)} %get-tuple-element.77.ga, bf16[256,256]{1,0:T(8,128)(2,1)S(1)} %get-tuple-element.55.q, bf16[256,256]{1,0:T(8,128)(2,1)S(1)} %get-tuple-element.53.k, ...), custom_call_target="tpu_custom_call" | custom-call | flops 150994944 | bytes 1311744 | tf_op jit(solution)/shard_map/pallas_call | solution.py:33
  39.4 0.7 %collective-permute-done.25.refs_2_ = f32[64,128]{1,0:T(8,128)S(1)} collective-permute-done((f32[64,128]{1,0:T(8,128)S(1)}, f32[64,128]{1,0:T(8,128)S(1)}, u32[]{:S(2)}, u32[]{:S(2)}) %collective-permute-start.25) | collective-permute-done | bytes 32800 | tf_op jit(solution)/shard_map/ppermute | solution.py:242
  40.1 0.9 %shard_map.93 = (bf16[256,256]{1,0:T(8,128)(2,1)}, bf16[256,256]{1,0:T(8,128)(2,1)}) custom-call(bf16[256,256]{1,0:T(8,128)(2,1)S(1)} %get-tuple-element.53.k, bf16[256,256]{1,0:T(8,128)(2,1)S(1)} %get-tuple-element.54.v, f32[256,256]{1,0:T(8,128)S(1)} %get-tuple-element.84.gk_part, f32[256,256]{1,0:T(8,128)S(1)} %get-tuple-element.85.gv_part, ...), custom_call_target="tpu_custom_call" | custom-call | flops 10000000 | bytes 1048576 | tf_op jit(solution)/shard_map/pallas_call | solution.py:33
  (40 shorter events, 3.9 us)
Async XLA Ops:
  1.9 5.9 %collective-permute-start = (f32[64,128]{1,0:T(8,128)S(1)}, f32[64,128]{1,0:T(8,128)S(1)}, u32[]{:S(2)}, u32[]{:S(2)}) collective-permute-start(f32[64,128]{1,0:T(8,128)S(1)} %get-tuple-element.58), channel_id=1, source_target_pairs={{0,13},{1,12},{2,15},{3,14},{4,9},{5,8},{6,11},{7,10},{8,5},{9,4},... | collective-permute-start | bytes 98312 | tf_op jit(solution)/shard_map/ppermute | solution.py:242
  5.3 3.3 %collective-permute-start.1 = (f32[64,128]{1,0:T(8,128)S(1)}, f32[64,128]{1,0:T(8,128)S(1)}, u32[]{:S(2)}, u32[]{:S(2)}) collective-permute-start(f32[64,128]{1,0:T(8,128)S(1)} %get-tuple-element.59), channel_id=1, source_target_pairs={{0,9},{1,4},{2,11},{3,6},{4,13},{5,0},{6,15},{7,2},{8,1},{9,12},{1... | collective-permute-start | bytes 98312 | tf_op jit(solution)/shard_map/ppermute | solution.py:242
  6.1 3.6 %collective-permute-start.2 = (f32[64,128]{1,0:T(8,128)S(1)}, f32[64,128]{1,0:T(8,128)S(1)}, u32[]{:S(2)}, u32[]{:S(2)}) collective-permute-start(f32[64,128]{1,0:T(8,128)S(1)} %get-tuple-element.60), channel_id=1, source_target_pairs={{0,5},{1,8},{2,7},{3,10},{4,1},{5,12},{6,3},{7,14},{8,13},{9,0},{1... | collective-permute-start | bytes 98312 | tf_op jit(solution)/shard_map/ppermute | solution.py:242
  7.1 2.6 %collective-permute-start.3 = (f32[64,128]{1,0:T(8,128)S(1)}, f32[64,128]{1,0:T(8,128)S(1)}, u32[]{:S(2)}, u32[]{:S(2)}) collective-permute-start(f32[64,128]{1,0:T(8,128)S(1)} %get-tuple-element.61), channel_id=1, source_target_pairs={{0,1},{1,0},{2,3},{3,2},{4,5},{5,4},{6,7},{7,6},{8,9},{9,8},{10,11... | collective-permute-start | bytes 98312 | tf_op jit(solution)/shard_map/ppermute | solution.py:242
  7.8 4.9 %collective-permute-start.8 = (f32[64,128]{1,0:T(8,128)S(1)}, f32[64,128]{1,0:T(8,128)S(1)}, u32[]{:S(2)}, u32[]{:S(2)}) collective-permute-start(f32[64,128]{1,0:T(8,128)S(1)} %get-tuple-element.66), channel_id=1, source_target_pairs={{0,1},{1,0},{2,3},{3,2},{4,5},{5,4},{6,7},{7,6},{8,9},{9,8},{10,11... | collective-permute-start | bytes 98312 | tf_op jit(solution)/shard_map/ppermute | solution.py:242
  7.8 5.8 %collective-permute-start.9 = (f32[64,128]{1,0:T(8,128)S(1)}, f32[64,128]{1,0:T(8,128)S(1)}, u32[]{:S(2)}, u32[]{:S(2)}) collective-permute-start(f32[64,128]{1,0:T(8,128)S(1)} %get-tuple-element.68), channel_id=1, source_target_pairs={{0,1},{1,0},{2,3},{3,2},{4,5},{5,4},{6,7},{7,6},{8,9},{9,8},{10,11... | collective-permute-start | bytes 98312 | tf_op jit(solution)/shard_map/ppermute | solution.py:242
  9.7 4.9 %collective-permute-start.10 = (f32[64,128]{1,0:T(8,128)S(1)}, f32[64,128]{1,0:T(8,128)S(1)}, u32[]{:S(2)}, u32[]{:S(2)}) collective-permute-start(f32[64,128]{1,0:T(8,128)S(1)} %get-tuple-element.70), channel_id=1, source_target_pairs={{0,16},{4,20},{8,24},{12,28},{16,0},{20,4},{24,8},{28,12},{1,17},{... | collective-permute-start | bytes 98312 | tf_op jit(solution)/shard_map/ppermute | solution.py:273
  10.6 4.8 %collective-permute-start.4 = (f32[64,128]{1,0:T(8,128)S(1)}, f32[64,128]{1,0:T(8,128)S(1)}, u32[]{:S(2)}, u32[]{:S(2)}) collective-permute-start(f32[64,128]{1,0:T(8,128)S(1)} %get-tuple-element.62), channel_id=1, source_target_pairs={{0,13},{1,12},{2,15},{3,14},{4,9},{5,8},{6,11},{7,10},{8,5},{9,4},... | collective-permute-start | bytes 98312 | tf_op jit(solution)/shard_map/ppermute | solution.py:242
  11.8 3.8 %collective-permute-start.5 = (f32[64,128]{1,0:T(8,128)S(1)}, f32[64,128]{1,0:T(8,128)S(1)}, u32[]{:S(2)}, u32[]{:S(2)}) collective-permute-start(f32[64,128]{1,0:T(8,128)S(1)} %get-tuple-element.63), channel_id=1, source_target_pairs={{0,9},{1,4},{2,11},{3,6},{4,13},{5,0},{6,15},{7,2},{8,1},{9,12},{1... | collective-permute-start | bytes 98312 | tf_op jit(solution)/shard_map/ppermute | solution.py:242
  12.6 3.7 %collective-permute-start.6 = (f32[64,128]{1,0:T(8,128)S(1)}, f32[64,128]{1,0:T(8,128)S(1)}, u32[]{:S(2)}, u32[]{:S(2)}) collective-permute-start(f32[64,128]{1,0:T(8,128)S(1)} %get-tuple-element.64), channel_id=1, source_target_pairs={{0,5},{1,8},{2,7},{3,10},{4,1},{5,12},{6,3},{7,14},{8,13},{9,0},{1... | collective-permute-start | bytes 98312 | tf_op jit(solution)/shard_map/ppermute | solution.py:242
  13.6 4.2 %collective-permute-start.7 = (f32[64,128]{1,0:T(8,128)S(1)}, f32[64,128]{1,0:T(8,128)S(1)}, u32[]{:S(2)}, u32[]{:S(2)}) collective-permute-start(f32[64,128]{1,0:T(8,128)S(1)} %get-tuple-element.65), channel_id=1, source_target_pairs={{0,1},{1,0},{2,3},{3,2},{4,5},{5,4},{6,7},{7,6},{8,9},{9,8},{10,11... | collective-permute-start | bytes 98312 | tf_op jit(solution)/shard_map/ppermute | solution.py:242
  14.6 3.2 %collective-permute-start.11 = (f32[64,128]{1,0:T(8,128)S(1)}, f32[64,128]{1,0:T(8,128)S(1)}, u32[]{:S(2)}, u32[]{:S(2)}) collective-permute-start(f32[64,128]{1,0:T(8,128)S(1)} %get-tuple-element.71), channel_id=1, source_target_pairs={{0,1},{1,0},{2,3},{3,2},{4,5},{5,4},{6,7},{7,6},{8,9},{9,8},{10,11... | collective-permute-start | bytes 98312 | tf_op jit(solution)/shard_map/ppermute | solution.py:242
  15.3 2.5 %collective-permute-start.12 = (f32[64,128]{1,0:T(8,128)S(1)}, f32[64,128]{1,0:T(8,128)S(1)}, u32[]{:S(2)}, u32[]{:S(2)}) collective-permute-start(f32[64,128]{1,0:T(8,128)S(1)} %get-tuple-element.72), channel_id=1, source_target_pairs={{0,1},{1,0},{2,3},{3,2},{4,5},{5,4},{6,7},{7,6},{8,9},{9,8},{10,11... | collective-permute-start | bytes 98312 | tf_op jit(solution)/shard_map/ppermute | solution.py:242
  15.7 2.2 %collective-permute-start.13 = (f32[64,128]{1,0:T(8,128)S(1)}, f32[64,128]{1,0:T(8,128)S(1)}, u32[]{:S(2)}, u32[]{:S(2)}) collective-permute-start(f32[64,128]{1,0:T(8,128)S(1)} %get-tuple-element.73), channel_id=1, source_target_pairs={{0,1},{1,0},{2,3},{3,2},{4,5},{5,4},{6,7},{7,6},{8,9},{9,8},{10,11... | collective-permute-start | bytes 98312 | tf_op jit(solution)/shard_map/ppermute | solution.py:242
  16.3 1.5 %collective-permute-start.14 = (f32[64,128]{1,0:T(8,128)S(1)}, f32[64,128]{1,0:T(8,128)S(1)}, u32[]{:S(2)}, u32[]{:S(2)}) collective-permute-start(f32[64,128]{1,0:T(8,128)S(1)} %get-tuple-element.74), channel_id=1, source_target_pairs={{0,1},{1,0},{2,3},{3,2},{4,5},{5,4},{6,7},{7,6},{8,9},{9,8},{10,11... | collective-permute-start | bytes 98312 | tf_op jit(solution)/shard_map/ppermute | solution.py:242
  18.2 3.6 %collective-permute-start.17 = (f32[2,256]{1,0:T(2,128)S(1)}, f32[2,256]{1,0:T(2,128)S(1)}, u32[]{:S(2)}, u32[]{:S(2)}) collective-permute-start(f32[2,256]{1,0:T(2,128)S(1)} %get-tuple-element.76.refs_0_), channel_id=1, source_target_pairs={{0,2},{1,3},{2,0},{3,1},{4,6},{5,7},{6,4},{7,5},{8,10},{9,11},{10,... | collective-permute-start | bytes 6152 | tf_op jit(solution)/shard_map/ppermute | solution.py:293
  19.8 3.0 %collective-permute-start.16 = (f32[2,256]{1,0:T(2,128)S(1)}, f32[2,256]{1,0:T(2,128)S(1)}, u32[]{:S(2)}, u32[]{:S(2)}) collective-permute-start(f32[2,256]{1,0:T(2,128)S(1)} %get-tuple-element.76.refs_0_), channel_id=1, source_target_pairs={{0,3},{1,2},{2,1},{3,0},{4,7},{5,6},{6,5},{7,4},{8,11},{9,10},{10,... | collective-permute-start | bytes 6152 | tf_op jit(solution)/shard_map/ppermute | solution.py:293
  20.1 2.7 %collective-permute-start.15 = (f32[2,256]{1,0:T(2,128)S(1)}, f32[2,256]{1,0:T(2,128)S(1)}, u32[]{:S(2)}, u32[]{:S(2)}) collective-permute-start(f32[2,256]{1,0:T(2,128)S(1)} %get-tuple-element.76.refs_0_), channel_id=1, source_target_pairs={{0,1},{1,0},{2,3},{3,2},{4,5},{5,4},{6,7},{7,6},{8,9},{9,8},{10,11... | collective-permute-start | bytes 6152 | tf_op jit(solution)/shard_map/ppermute | solution.py:293
  23.2 4.3 %collective-permute-start.18 = (f32[64,128]{1,0:T(8,128)S(1)}, f32[64,128]{1,0:T(8,128)S(1)}, u32[]{:S(2)}, u32[]{:S(2)}) collective-permute-start(f32[64,128]{1,0:T(8,128)S(1)} %get-tuple-element.86), channel_id=1, source_target_pairs={{0,13},{1,12},{2,15},{3,14},{4,9},{5,8},{6,11},{7,10},{8,5},{9,4},... | collective-permute-start | bytes 98312 | tf_op jit(solution)/shard_map/ppermute | solution.py:242
  24.5 3.7 %collective-permute-start.19 = (f32[64,128]{1,0:T(8,128)S(1)}, f32[64,128]{1,0:T(8,128)S(1)}, u32[]{:S(2)}, u32[]{:S(2)}) collective-permute-start(f32[64,128]{1,0:T(8,128)S(1)} %get-tuple-element.87), channel_id=1, source_target_pairs={{0,9},{1,4},{2,11},{3,6},{4,13},{5,0},{6,15},{7,2},{8,1},{9,12},{1... | collective-permute-start | bytes 98312 | tf_op jit(solution)/shard_map/ppermute | solution.py:242
  25.4 3.4 %collective-permute-start.20 = (f32[64,128]{1,0:T(8,128)S(1)}, f32[64,128]{1,0:T(8,128)S(1)}, u32[]{:S(2)}, u32[]{:S(2)}) collective-permute-start(f32[64,128]{1,0:T(8,128)S(1)} %get-tuple-element.88), channel_id=1, source_target_pairs={{0,5},{1,8},{2,7},{3,10},{4,1},{5,12},{6,3},{7,14},{8,13},{9,0},{1... | collective-permute-start | bytes 98312 | tf_op jit(solution)/shard_map/ppermute | solution.py:242
  26.2 2.5 %collective-permute-start.21 = (f32[64,128]{1,0:T(8,128)S(1)}, f32[64,128]{1,0:T(8,128)S(1)}, u32[]{:S(2)}, u32[]{:S(2)}) collective-permute-start(f32[64,128]{1,0:T(8,128)S(1)} %get-tuple-element.89), channel_id=1, source_target_pairs={{0,1},{1,0},{2,3},{3,2},{4,5},{5,4},{6,7},{7,6},{8,9},{9,8},{10,11... | collective-permute-start | bytes 98312 | tf_op jit(solution)/shard_map/ppermute | solution.py:242
  28.8 5.8 %collective-permute-start.22 = (f32[64,128]{1,0:T(8,128)S(1)}, f32[64,128]{1,0:T(8,128)S(1)}, u32[]{:S(2)}, u32[]{:S(2)}) collective-permute-start(f32[64,128]{1,0:T(8,128)S(1)} %get-tuple-element.91), channel_id=1, source_target_pairs={{0,16},{4,20},{8,24},{12,28},{16,0},{20,4},{24,8},{28,12},{1,17},{... | collective-permute-start | bytes 98312 | tf_op jit(solution)/shard_map/ppermute | solution.py:273
  32.6 2.3 %collective-permute-start.27 = (f32[64,128]{1,0:T(8,128)S(1)}, f32[64,128]{1,0:T(8,128)S(1)}, u32[]{:S(2)}, u32[]{:S(2)}) collective-permute-start(f32[64,128]{1,0:T(8,128)S(1)} %get-tuple-element.96), channel_id=1, source_target_pairs={{0,1},{1,0},{2,3},{3,2},{4,5},{5,4},{6,7},{7,6},{8,9},{9,8},{10,11... | collective-permute-start | bytes 98312 | tf_op jit(solution)/shard_map/ppermute | solution.py:242
  32.6 4.2 %collective-permute-start.28 = (f32[64,128]{1,0:T(8,128)S(1)}, f32[64,128]{1,0:T(8,128)S(1)}, u32[]{:S(2)}, u32[]{:S(2)}) collective-permute-start(f32[64,128]{1,0:T(8,128)S(1)} %get-tuple-element.97), channel_id=1, source_target_pairs={{0,1},{1,0},{2,3},{3,2},{4,5},{5,4},{6,7},{7,6},{8,9},{9,8},{10,11... | collective-permute-start | bytes 98312 | tf_op jit(solution)/shard_map/ppermute | solution.py:242
  33.1 3.9 %collective-permute-start.29 = (f32[64,128]{1,0:T(8,128)S(1)}, f32[64,128]{1,0:T(8,128)S(1)}, u32[]{:S(2)}, u32[]{:S(2)}) collective-permute-start(f32[64,128]{1,0:T(8,128)S(1)} %get-tuple-element.98), channel_id=1, source_target_pairs={{0,1},{1,0},{2,3},{3,2},{4,5},{5,4},{6,7},{7,6},{8,9},{9,8},{10,11... | collective-permute-start | bytes 98312 | tf_op jit(solution)/shard_map/ppermute | solution.py:242
  33.1 6.3 %collective-permute-start.30 = (f32[64,128]{1,0:T(8,128)S(1)}, f32[64,128]{1,0:T(8,128)S(1)}, u32[]{:S(2)}, u32[]{:S(2)}) collective-permute-start(f32[64,128]{1,0:T(8,128)S(1)} %get-tuple-element.99), channel_id=1, source_target_pairs={{0,1},{1,0},{2,3},{3,2},{4,5},{5,4},{6,7},{7,6},{8,9},{9,8},{10,11... | collective-permute-start | bytes 98312 | tf_op jit(solution)/shard_map/ppermute | solution.py:242
  34.6 4.8 %collective-permute-start.23 = (f32[64,128]{1,0:T(8,128)S(1)}, f32[64,128]{1,0:T(8,128)S(1)}, u32[]{:S(2)}, u32[]{:S(2)}) collective-permute-start(f32[64,128]{1,0:T(8,128)S(1)} %get-tuple-element.92), channel_id=1, source_target_pairs={{0,13},{1,12},{2,15},{3,14},{4,9},{5,8},{6,11},{7,10},{8,5},{9,4},... | collective-permute-start | bytes 98312 | tf_op jit(solution)/shard_map/ppermute | solution.py:242
  34.9 4.5 %collective-permute-start.24 = (f32[64,128]{1,0:T(8,128)S(1)}, f32[64,128]{1,0:T(8,128)S(1)}, u32[]{:S(2)}, u32[]{:S(2)}) collective-permute-start(f32[64,128]{1,0:T(8,128)S(1)} %get-tuple-element.93), channel_id=1, source_target_pairs={{0,9},{1,4},{2,11},{3,6},{4,13},{5,0},{6,15},{7,2},{8,1},{9,12},{1... | collective-permute-start | bytes 98312 | tf_op jit(solution)/shard_map/ppermute | solution.py:242
  36.7 3.4 %collective-permute-start.25 = (f32[64,128]{1,0:T(8,128)S(1)}, f32[64,128]{1,0:T(8,128)S(1)}, u32[]{:S(2)}, u32[]{:S(2)}) collective-permute-start(f32[64,128]{1,0:T(8,128)S(1)} %get-tuple-element.94), channel_id=1, source_target_pairs={{0,5},{1,8},{2,7},{3,10},{4,1},{5,12},{6,3},{7,14},{8,13},{9,0},{1... | collective-permute-start | bytes 98312 | tf_op jit(solution)/shard_map/ppermute | solution.py:242
  36.9 3.2 %collective-permute-start.26 = (f32[64,128]{1,0:T(8,128)S(1)}, f32[64,128]{1,0:T(8,128)S(1)}, u32[]{:S(2)}, u32[]{:S(2)}) collective-permute-start(f32[64,128]{1,0:T(8,128)S(1)} %get-tuple-element.95), channel_id=1, source_target_pairs={{0,1},{1,0},{2,3},{3,2},{4,5},{5,4},{6,7},{7,6},{8,9},{9,8},{10,11... | collective-permute-start | bytes 98312 | tf_op jit(solution)/shard_map/ppermute | solution.py:242

commit v5 on v4

--- a/solution.py
+++ b/solution.py
@@ -10,8 +10,8 @@
 HEAD = 128
 
 epsilon = 1e-06
-ALONE = (0, 2)
-SHARED = (1, 3)
+ALONE = (0, 1, 2)
+SHARED = (3,)
 F32 = jnp.float32
 BF16 = jnp.bfloat16
 

time: 41.2 us -> 40.9 us (level)
  starting transfers between devices: 25.7 us -> 24.9 us
  waiting for transfers between devices: 8.83 us -> 9.27 us
    ppermute x26 -> x27, starting transfers between devices: 18.8 us -> 17.6 us  [exchange(): return lax.ppermute(piece, ('ctx', 'tp'), pairs)]
    ppermute x2, waiting for transfers between devices: 1.24 us -> 2.37 us  [carried_in(): over = lax.ppermute(total, 'ctx', [(j, j ^ group) for j in both])]
    ppermute x26 -> x27, waiting for transfers between devices: 5.19 us -> 4.53 us  [exchange(): return lax.ppermute(piece, ('ctx', 'tp'), pairs)]
  transfers between devices with their start and end apart: 31 -> 32, of which waited for: 12 -> 12; matrix products, arithmetic and copies ran while one was open for 0% -> 0% of each run, Pallas kernels for 7% -> 7%
where the time goes in v5:
time: 40.9 us; the launch traced here: 40.8 us
  starting transfers between devices  24.9 us (61%)
  waiting for transfers between devices  9.27 us (23%)
  Pallas kernels  5.86 us (14%)
  between operations  0.76 us (2%)
    ppermute x27, starting transfers between devices, exchange(): return lax.ppermute(piece, ('ctx', 'tp'), pairs)  17.6 us
    pallas_call x10, Pallas kernels, call(): pl.pallas_call(body, out_shape=outs, in_specs=ins or [VMEM] * len(args),...  5.86 us
    ppermute x2, starting transfers between devices, carried_in(): over = lax.ppermute(total, 'ctx', [(j, j ^ group) for j in both])  4.99 us
    ppermute x27, waiting for transfers between devices, exchange(): return lax.ppermute(piece, ('ctx', 'tp'), pairs)  4.53 us
    ppermute x2, waiting for transfers between devices, carried_in(): over = lax.ppermute(total, 'ctx', [(j, j ^ group) for j in both])  2.37 us
    ppermute x3, waiting for transfers between devices, from_all(): lax.ppermute(part, axis, [(i, i ^ step if even else (i + step) % count) f...  2.36 us
    ppermute x3, starting transfers between devices, from_all(): lax.ppermute(part, axis, [(i, i ^ step if even else (i + step) % count) f...  2.24 us
  transfers between devices with their start and end apart: 32, of which 12 were waited for; matrix products, arithmetic and copies ran while one was open for 0% of the time, Pallas kernels for 7%

profile of v5, /device:TPU:0, one launch (start us, length us, event | category | flops | bytes accessed | tf_op | source)
XLA Modules:
  0.0 40.8 jit_solution(1859623164507026368)
XLA Ops:
  0.6 1.2 %shard_map.84 = (bf16[256,256]{1,0:T(8,128)(2,1)S(1)}, bf16[256,256]{1,0:T(8,128)(2,1)S(1)}, f32[64,128]{1,0:T(8,128)S(1)}, f32[64,128]{1,0:T(8,128)S(1)}, f32[6...) custom-call(bf16[256,256]{1,0:T(8,128)(2,1)} %k_hbm.1, ...), custom_call_target="tpu_custom_call" | custom-call | flops 10000000 | bytes 262144 | tf_op jit(solution)/shard_map/pallas_call | solution.py:33
  1.9 3.5 %collective-permute-start = (f32[64,128]{1,0:T(8,128)S(1)}, f32[64,128]{1,0:T(8,128)S(1)}, u32[]{:S(2)}, u32[]{:S(2)}) collective-permute-start(f32[64,128]{1,0:T(8,128)S(1)} %get-tuple-element.58), channel_id=1, source_target_pairs={{0,13},{1,12},{2,15},{3,14},{4,9},{5,8},{6,11},{7,10},{8,5},{9,4},... | collective-permute-start | bytes 98312 | tf_op jit(solution)/shard_map/ppermute | solution.py:242
  5.3 0.7 %collective-permute-start.1 = (f32[64,128]{1,0:T(8,128)S(1)}, f32[64,128]{1,0:T(8,128)S(1)}, u32[]{:S(2)}, u32[]{:S(2)}) collective-permute-start(f32[64,128]{1,0:T(8,128)S(1)} %get-tuple-element.59), channel_id=1, source_target_pairs={{0,9},{1,4},{2,11},{3,6},{4,13},{5,0},{6,15},{7,2},{8,1},{9,12},{1... | collective-permute-start | bytes 98312 | tf_op jit(solution)/shard_map/ppermute | solution.py:242
  6.1 1.0 %collective-permute-start.2 = (f32[64,128]{1,0:T(8,128)S(1)}, f32[64,128]{1,0:T(8,128)S(1)}, u32[]{:S(2)}, u32[]{:S(2)}) collective-permute-start(f32[64,128]{1,0:T(8,128)S(1)} %get-tuple-element.60), channel_id=1, source_target_pairs={{0,5},{1,8},{2,7},{3,10},{4,1},{5,12},{6,3},{7,14},{8,13},{9,0},{1... | collective-permute-start | bytes 98312 | tf_op jit(solution)/shard_map/ppermute | solution.py:242
  7.1 0.7 %collective-permute-start.3 = (f32[64,128]{1,0:T(8,128)S(1)}, f32[64,128]{1,0:T(8,128)S(1)}, u32[]{:S(2)}, u32[]{:S(2)}) collective-permute-start(f32[64,128]{1,0:T(8,128)S(1)} %get-tuple-element.61), channel_id=1, source_target_pairs={{0,1},{1,0},{2,3},{3,2},{4,5},{5,4},{6,7},{7,6},{8,9},{9,8},{10,11... | collective-permute-start | bytes 98312 | tf_op jit(solution)/shard_map/ppermute | solution.py:242
  7.8 0.5 %collective-permute-start.9 = (f32[64,128]{1,0:T(8,128)S(1)}, f32[64,128]{1,0:T(8,128)S(1)}, u32[]{:S(2)}, u32[]{:S(2)}) collective-permute-start(f32[64,128]{1,0:T(8,128)S(1)} %get-tuple-element.67), channel_id=1, source_target_pairs={{0,1},{1,0},{2,3},{3,2},{4,5},{5,4},{6,7},{7,6},{8,9},{9,8},{10,11... | collective-permute-start | bytes 98312 | tf_op jit(solution)/shard_map/ppermute | solution.py:242
  8.7 1.1 %collective-permute-start.10 = (f32[64,128]{1,0:T(8,128)S(1)}, f32[64,128]{1,0:T(8,128)S(1)}, u32[]{:S(2)}, u32[]{:S(2)}) collective-permute-start(f32[64,128]{1,0:T(8,128)S(1)} %get-tuple-element.68), channel_id=1, source_target_pairs={{0,1},{1,0},{2,3},{3,2},{4,5},{5,4},{6,7},{7,6},{8,9},{9,8},{10,11... | collective-permute-start | bytes 98312 | tf_op jit(solution)/shard_map/ppermute | solution.py:242
  9.8 1.2 %collective-permute-start.11 = (f32[64,128]{1,0:T(8,128)S(1)}, f32[64,128]{1,0:T(8,128)S(1)}, u32[]{:S(2)}, u32[]{:S(2)}) collective-permute-start(f32[64,128]{1,0:T(8,128)S(1)} %get-tuple-element.70), channel_id=1, source_target_pairs={{0,16},{4,20},{8,24},{12,28},{16,0},{20,4},{24,8},{28,12},{1,17},{... | collective-permute-start | bytes 98312 | tf_op jit(solution)/shard_map/ppermute | solution.py:273
  11.2 1.5 %collective-permute-start.5 = (f32[64,128]{1,0:T(8,128)S(1)}, f32[64,128]{1,0:T(8,128)S(1)}, u32[]{:S(2)}, u32[]{:S(2)}) collective-permute-start(f32[64,128]{1,0:T(8,128)S(1)} %get-tuple-element.63), channel_id=1, source_target_pairs={{0,9},{1,4},{2,11},{3,6},{4,13},{5,0},{6,15},{7,2},{8,1},{9,12},{1... | collective-permute-start | bytes 98312 | tf_op jit(solution)/shard_map/ppermute | solution.py:242
  13.0 0.4 %collective-permute-start.7 = (f32[64,128]{1,0:T(8,128)S(1)}, f32[64,128]{1,0:T(8,128)S(1)}, u32[]{:S(2)}, u32[]{:S(2)}) collective-permute-start(f32[64,128]{1,0:T(8,128)S(1)} %get-tuple-element.65), channel_id=1, source_target_pairs={{0,1},{1,0},{2,3},{3,2},{4,5},{5,4},{6,7},{7,6},{8,9},{9,8},{10,11... | collective-permute-start | bytes 98312 | tf_op jit(solution)/shard_map/ppermute | solution.py:242
  13.4 1.2 %collective-permute-done.11.refs_4_ = f32[64,128]{1,0:T(8,128)S(1)} collective-permute-done((f32[64,128]{1,0:T(8,128)S(1)}, f32[64,128]{1,0:T(8,128)S(1)}, u32[]{:S(2)}, u32[]{:S(2)}) %collective-permute-start.11) | collective-permute-done | bytes 32800 | tf_op jit(solution)/shard_map/ppermute | solution.py:273
  14.8 0.5 %collective-permute-done.4.refs_0_ = f32[64,128]{1,0:T(8,128)S(1)} collective-permute-done((f32[64,128]{1,0:T(8,128)S(1)}, f32[64,128]{1,0:T(8,128)S(1)}, u32[]{:S(2)}, u32[]{:S(2)}) %collective-permute-start.4) | collective-permute-done | bytes 32800 | tf_op jit(solution)/shard_map/ppermute | solution.py:242
  16.2 1.5 %shard_map.85 = (bf16[2,256,256]{2,1,0:T(8,128)(2,1)S(1)}, f32[256,256]{1,0:T(8,128)S(1)}, bf16[256,256]{1,0:T(8,128)(2,1)S(1)}, f32[256,256]{1,0:T(8,128)S(1)}, f32[2,128]{1,0:T(2,128)S(1)}) custom-call(bf16[256,256]{1,0:T(8,128)(2,1)S(1)} %get-tuple-element.53.k, bf16[256,256]{1,0:T(8,128)(2,1)S(1)} %get-tuple-element.54.v, bf16[256,256]{1,0:T(8,128)(2,1)} %q_hbm.1, ...), custom_call_target="tpu_custom_call" | custom-call | flops 67108864 | bytes 525312 | tf_op jit(solution)/shard_map/pallas_call | solution.py:33
  18.1 1.6 %collective-permute-start.18 = (f32[2,256]{1,0:T(2,128)S(1)}, f32[2,256]{1,0:T(2,128)S(1)}, u32[]{:S(2)}, u32[]{:S(2)}) collective-permute-start(f32[2,256]{1,0:T(2,128)S(1)} %get-tuple-element.76.refs_0_), channel_id=1, source_target_pairs={{0,2},{1,3},{2,0},{3,1},{4,6},{5,7},{6,4},{7,5},{8,10},{9,11},{10,... | collective-permute-start | bytes 6152 | tf_op jit(solution)/shard_map/ppermute | solution.py:293
  20.3 1.4 %collective-permute-done.18.refs_3_ = f32[2,256]{1,0:T(2,128)S(1)} collective-permute-done((f32[2,256]{1,0:T(2,128)S(1)}, f32[2,256]{1,0:T(2,128)S(1)}, u32[]{:S(2)}, u32[]{:S(2)}) %collective-permute-start.18) | collective-permute-done | bytes 2080 | tf_op jit(solution)/shard_map/ppermute | solution.py:293
  21.8 0.9 %collective-permute-done.17.refs_2_ = f32[2,256]{1,0:T(2,128)S(1)} collective-permute-done((f32[2,256]{1,0:T(2,128)S(1)}, f32[2,256]{1,0:T(2,128)S(1)}, u32[]{:S(2)}, u32[]{:S(2)}) %collective-permute-start.17) | collective-permute-done | bytes 2080 | tf_op jit(solution)/shard_map/ppermute | solution.py:293
  23.1 1.5 %collective-permute-start.19 = (f32[64,128]{1,0:T(8,128)S(1)}, f32[64,128]{1,0:T(8,128)S(1)}, u32[]{:S(2)}, u32[]{:S(2)}) collective-permute-start(f32[64,128]{1,0:T(8,128)S(1)} %get-tuple-element.86), channel_id=1, source_target_pairs={{0,13},{1,12},{2,15},{3,14},{4,9},{5,8},{6,11},{7,10},{8,5},{9,4},... | collective-permute-start | bytes 98312 | tf_op jit(solution)/shard_map/ppermute | solution.py:242
  24.6 1.1 %collective-permute-start.20 = (f32[64,128]{1,0:T(8,128)S(1)}, f32[64,128]{1,0:T(8,128)S(1)}, u32[]{:S(2)}, u32[]{:S(2)}) collective-permute-start(f32[64,128]{1,0:T(8,128)S(1)} %get-tuple-element.87), channel_id=1, source_target_pairs={{0,9},{1,4},{2,11},{3,6},{4,13},{5,0},{6,15},{7,2},{8,1},{9,12},{1... | collective-permute-start | bytes 98312 | tf_op jit(solution)/shard_map/ppermute | solution.py:242
  25.7 0.6 %collective-permute-start.21 = (f32[64,128]{1,0:T(8,128)S(1)}, f32[64,128]{1,0:T(8,128)S(1)}, u32[]{:S(2)}, u32[]{:S(2)}) collective-permute-start(f32[64,128]{1,0:T(8,128)S(1)} %get-tuple-element.88), channel_id=1, source_target_pairs={{0,5},{1,8},{2,7},{3,10},{4,1},{5,12},{6,3},{7,14},{8,13},{9,0},{1... | collective-permute-start | bytes 98312 | tf_op jit(solution)/shard_map/ppermute | solution.py:242
  26.6 0.8 %collective-permute-done.19.refs_0_ = f32[64,128]{1,0:T(8,128)S(1)} collective-permute-done((f32[64,128]{1,0:T(8,128)S(1)}, f32[64,128]{1,0:T(8,128)S(1)}, u32[]{:S(2)}, u32[]{:S(2)}) %collective-permute-start.19) | collective-permute-done | bytes 32800 | tf_op jit(solution)/shard_map/ppermute | solution.py:242
  27.4 0.7 %collective-permute-done.20.refs_1_ = f32[64,128]{1,0:T(8,128)S(1)} collective-permute-done((f32[64,128]{1,0:T(8,128)S(1)}, f32[64,128]{1,0:T(8,128)S(1)}, u32[]{:S(2)}, u32[]{:S(2)}) %collective-permute-start.20) | collective-permute-done | bytes 32800 | tf_op jit(solution)/shard_map/ppermute | solution.py:242
  28.1 1.0 %collective-permute-done.21.refs_2_ = f32[64,128]{1,0:T(8,128)S(1)} collective-permute-done((f32[64,128]{1,0:T(8,128)S(1)}, f32[64,128]{1,0:T(8,128)S(1)}, u32[]{:S(2)}, u32[]{:S(2)}) %collective-permute-start.21) | collective-permute-done | bytes 32800 | tf_op jit(solution)/shard_map/ppermute | solution.py:242
  29.1 3.8 %collective-permute-start.23 = (f32[64,128]{1,0:T(8,128)S(1)}, f32[64,128]{1,0:T(8,128)S(1)}, u32[]{:S(2)}, u32[]{:S(2)}) collective-permute-start(f32[64,128]{1,0:T(8,128)S(1)} %get-tuple-element.91), channel_id=1, source_target_pairs={{0,16},{4,20},{8,24},{12,28},{16,0},{20,4},{24,8},{28,12},{1,17},{... | collective-permute-start | bytes 98312 | tf_op jit(solution)/shard_map/ppermute | solution.py:273
  32.8 0.5 %collective-permute-start.29 = (f32[64,128]{1,0:T(8,128)S(1)}, f32[64,128]{1,0:T(8,128)S(1)}, u32[]{:S(2)}, u32[]{:S(2)}) collective-permute-start(f32[64,128]{1,0:T(8,128)S(1)} %get-tuple-element.97), channel_id=1, source_target_pairs={{0,1},{1,0},{2,3},{3,2},{4,5},{5,4},{6,7},{7,6},{8,9},{9,8},{10,11... | collective-permute-start | bytes 98312 | tf_op jit(solution)/shard_map/ppermute | solution.py:242
  33.3 0.5 %collective-permute-start.31 = (f32[64,128]{1,0:T(8,128)S(1)}, f32[64,128]{1,0:T(8,128)S(1)}, u32[]{:S(2)}, u32[]{:S(2)}) collective-permute-start(f32[64,128]{1,0:T(8,128)S(1)} %get-tuple-element.99), channel_id=1, source_target_pairs={{0,1},{1,0},{2,3},{3,2},{4,5},{5,4},{6,7},{7,6},{8,9},{9,8},{10,11... | collective-permute-start | bytes 98312 | tf_op jit(solution)/shard_map/ppermute | solution.py:242
  33.8 1.1 %collective-permute-done.23.over = f32[64,128]{1,0:T(8,128)S(1)} collective-permute-done((f32[64,128]{1,0:T(8,128)S(1)}, f32[64,128]{1,0:T(8,128)S(1)}, u32[]{:S(2)}, u32[]{:S(2)}) %collective-permute-start.23) | collective-permute-done | bytes 32800 | tf_op jit(solution)/shard_map/ppermute | solution.py:273
  35.1 1.4 %collective-permute-start.25 = (f32[64,128]{1,0:T(8,128)S(1)}, f32[64,128]{1,0:T(8,128)S(1)}, u32[]{:S(2)}, u32[]{:S(2)}) collective-permute-start(f32[64,128]{1,0:T(8,128)S(1)} %get-tuple-element.93), channel_id=1, source_target_pairs={{0,9},{1,4},{2,11},{3,6},{4,13},{5,0},{6,15},{7,2},{8,1},{9,12},{1... | collective-permute-start | bytes 98312 | tf_op jit(solution)/shard_map/ppermute | solution.py:242
  36.5 0.4 %collective-permute-start.26 = (f32[64,128]{1,0:T(8,128)S(1)}, f32[64,128]{1,0:T(8,128)S(1)}, u32[]{:S(2)}, u32[]{:S(2)}) collective-permute-start(f32[64,128]{1,0:T(8,128)S(1)} %get-tuple-element.94), channel_id=1, source_target_pairs={{0,5},{1,8},{2,7},{3,10},{4,1},{5,12},{6,3},{7,14},{8,13},{9,0},{1... | collective-permute-start | bytes 98312 | tf_op jit(solution)/shard_map/ppermute | solution.py:242
  36.9 0.6 %collective-permute-start.27 = (f32[64,128]{1,0:T(8,128)S(1)}, f32[64,128]{1,0:T(8,128)S(1)}, u32[]{:S(2)}, u32[]{:S(2)}) collective-permute-start(f32[64,128]{1,0:T(8,128)S(1)} %get-tuple-element.95), channel_id=1, source_target_pairs={{0,1},{1,0},{2,3},{3,2},{4,5},{5,4},{6,7},{7,6},{8,9},{9,8},{10,11... | collective-permute-start | bytes 98312 | tf_op jit(solution)/shard_map/ppermute | solution.py:242
  37.5 1.4 %shard_map.90 = (bf16[256,256]{1,0:T(8,128)(2,1)}, bf16[256,256]{1,0:T(8,128)(2,1)}, f32[256,256]{1,0:T(8,128)S(1)}, f32[256,256]{1,0:T(8,128)S(1)}) custom-call(bf16[256,256]{1,0:T(8,128)(2,1)S(1)} %get-tuple-element.77.ga, bf16[256,256]{1,0:T(8,128)(2,1)S(1)} %get-tuple-element.55.q, bf16[256,256]{1,0:T(8,128)(2,1)S(1)} %get-tuple-element.53.k, ...), custom_call_target="tpu_custom_call" | custom-call | flops 150994944 | bytes 1311744 | tf_op jit(solution)/shard_map/pallas_call | solution.py:33
  39.3 0.5 %collective-permute-done.26.refs_2_ = f32[64,128]{1,0:T(8,128)S(1)} collective-permute-done((f32[64,128]{1,0:T(8,128)S(1)}, f32[64,128]{1,0:T(8,128)S(1)}, u32[]{:S(2)}, u32[]{:S(2)}) %collective-permute-start.26) | collective-permute-done | bytes 32800 | tf_op jit(solution)/shard_map/ppermute | solution.py:242
  39.8 0.9 %shard_map.93 = (bf16[256,256]{1,0:T(8,128)(2,1)}, bf16[256,256]{1,0:T(8,128)(2,1)}) custom-call(bf16[256,256]{1,0:T(8,128)(2,1)S(1)} %get-tuple-element.53.k, bf16[256,256]{1,0:T(8,128)(2,1)S(1)} %get-tuple-element.54.v, f32[256,256]{1,0:T(8,128)S(1)} %get-tuple-element.84.gk_part, f32[256,256]{1,0:T(8,128)S(1)} %get-tuple-element.85.gv_part, ...), custom_call_target="tpu_custom_call" | custom-call | flops 10000000 | bytes 1048576 | tf_op jit(solution)/shard_map/pallas_call | solution.py:33
  (42 shorter events, 4.1 us)
Async XLA Ops:
  1.9 5.9 %collective-permute-start = (f32[64,128]{1,0:T(8,128)S(1)}, f32[64,128]{1,0:T(8,128)S(1)}, u32[]{:S(2)}, u32[]{:S(2)}) collective-permute-start(f32[64,128]{1,0:T(8,128)S(1)} %get-tuple-element.58), channel_id=1, source_target_pairs={{0,13},{1,12},{2,15},{3,14},{4,9},{5,8},{6,11},{7,10},{8,5},{9,4},... | collective-permute-start | bytes 98312 | tf_op jit(solution)/shard_map/ppermute | solution.py:242
  5.3 3.3 %collective-permute-start.1 = (f32[64,128]{1,0:T(8,128)S(1)}, f32[64,128]{1,0:T(8,128)S(1)}, u32[]{:S(2)}, u32[]{:S(2)}) collective-permute-start(f32[64,128]{1,0:T(8,128)S(1)} %get-tuple-element.59), channel_id=1, source_target_pairs={{0,9},{1,4},{2,11},{3,6},{4,13},{5,0},{6,15},{7,2},{8,1},{9,12},{1... | collective-permute-start | bytes 98312 | tf_op jit(solution)/shard_map/ppermute | solution.py:242
  6.1 3.7 %collective-permute-start.2 = (f32[64,128]{1,0:T(8,128)S(1)}, f32[64,128]{1,0:T(8,128)S(1)}, u32[]{:S(2)}, u32[]{:S(2)}) collective-permute-start(f32[64,128]{1,0:T(8,128)S(1)} %get-tuple-element.60), channel_id=1, source_target_pairs={{0,5},{1,8},{2,7},{3,10},{4,1},{5,12},{6,3},{7,14},{8,13},{9,0},{1... | collective-permute-start | bytes 98312 | tf_op jit(solution)/shard_map/ppermute | solution.py:242
  7.1 2.7 %collective-permute-start.3 = (f32[64,128]{1,0:T(8,128)S(1)}, f32[64,128]{1,0:T(8,128)S(1)}, u32[]{:S(2)}, u32[]{:S(2)}) collective-permute-start(f32[64,128]{1,0:T(8,128)S(1)} %get-tuple-element.61), channel_id=1, source_target_pairs={{0,1},{1,0},{2,3},{3,2},{4,5},{5,4},{6,7},{7,6},{8,9},{9,8},{10,11... | collective-permute-start | bytes 98312 | tf_op jit(solution)/shard_map/ppermute | solution.py:242
  7.8 3.5 %collective-permute-start.8 = (f32[64,128]{1,0:T(8,128)S(1)}, f32[64,128]{1,0:T(8,128)S(1)}, u32[]{:S(2)}, u32[]{:S(2)}) collective-permute-start(f32[64,128]{1,0:T(8,128)S(1)} %get-tuple-element.66), channel_id=1, source_target_pairs={{0,1},{1,0},{2,3},{3,2},{4,5},{5,4},{6,7},{7,6},{8,9},{9,8},{10,11... | collective-permute-start | bytes 98312 | tf_op jit(solution)/shard_map/ppermute | solution.py:242
  7.8 5.0 %collective-permute-start.9 = (f32[64,128]{1,0:T(8,128)S(1)}, f32[64,128]{1,0:T(8,128)S(1)}, u32[]{:S(2)}, u32[]{:S(2)}) collective-permute-start(f32[64,128]{1,0:T(8,128)S(1)} %get-tuple-element.67), channel_id=1, source_target_pairs={{0,1},{1,0},{2,3},{3,2},{4,5},{5,4},{6,7},{7,6},{8,9},{9,8},{10,11... | collective-permute-start | bytes 98312 | tf_op jit(solution)/shard_map/ppermute | solution.py:242
  8.7 4.3 %collective-permute-start.10 = (f32[64,128]{1,0:T(8,128)S(1)}, f32[64,128]{1,0:T(8,128)S(1)}, u32[]{:S(2)}, u32[]{:S(2)}) collective-permute-start(f32[64,128]{1,0:T(8,128)S(1)} %get-tuple-element.68), channel_id=1, source_target_pairs={{0,1},{1,0},{2,3},{3,2},{4,5},{5,4},{6,7},{7,6},{8,9},{9,8},{10,11... | collective-permute-start | bytes 98312 | tf_op jit(solution)/shard_map/ppermute | solution.py:242
  9.8 4.9 %collective-permute-start.11 = (f32[64,128]{1,0:T(8,128)S(1)}, f32[64,128]{1,0:T(8,128)S(1)}, u32[]{:S(2)}, u32[]{:S(2)}) collective-permute-start(f32[64,128]{1,0:T(8,128)S(1)} %get-tuple-element.70), channel_id=1, source_target_pairs={{0,16},{4,20},{8,24},{12,28},{16,0},{20,4},{24,8},{28,12},{1,17},{... | collective-permute-start | bytes 98312 | tf_op jit(solution)/shard_map/ppermute | solution.py:273
  11.0 4.2 %collective-permute-start.4 = (f32[64,128]{1,0:T(8,128)S(1)}, f32[64,128]{1,0:T(8,128)S(1)}, u32[]{:S(2)}, u32[]{:S(2)}) collective-permute-start(f32[64,128]{1,0:T(8,128)S(1)} %get-tuple-element.62), channel_id=1, source_target_pairs={{0,13},{1,12},{2,15},{3,14},{4,9},{5,8},{6,11},{7,10},{8,5},{9,4},... | collective-permute-start | bytes 98312 | tf_op jit(solution)/shard_map/ppermute | solution.py:242
  11.2 4.2 %collective-permute-start.5 = (f32[64,128]{1,0:T(8,128)S(1)}, f32[64,128]{1,0:T(8,128)S(1)}, u32[]{:S(2)}, u32[]{:S(2)}) collective-permute-start(f32[64,128]{1,0:T(8,128)S(1)} %get-tuple-element.63), channel_id=1, source_target_pairs={{0,9},{1,4},{2,11},{3,6},{4,13},{5,0},{6,15},{7,2},{8,1},{9,12},{1... | collective-permute-start | bytes 98312 | tf_op jit(solution)/shard_map/ppermute | solution.py:242
  12.8 3.3 %collective-permute-start.6 = (f32[64,128]{1,0:T(8,128)S(1)}, f32[64,128]{1,0:T(8,128)S(1)}, u32[]{:S(2)}, u32[]{:S(2)}) collective-permute-start(f32[64,128]{1,0:T(8,128)S(1)} %get-tuple-element.64), channel_id=1, source_target_pairs={{0,5},{1,8},{2,7},{3,10},{4,1},{5,12},{6,3},{7,14},{8,13},{9,0},{1... | collective-permute-start | bytes 98312 | tf_op jit(solution)/shard_map/ppermute | solution.py:242
  13.0 4.7 %collective-permute-start.7 = (f32[64,128]{1,0:T(8,128)S(1)}, f32[64,128]{1,0:T(8,128)S(1)}, u32[]{:S(2)}, u32[]{:S(2)}) collective-permute-start(f32[64,128]{1,0:T(8,128)S(1)} %get-tuple-element.65), channel_id=1, source_target_pairs={{0,1},{1,0},{2,3},{3,2},{4,5},{5,4},{6,7},{7,6},{8,9},{9,8},{10,11... | collective-permute-start | bytes 98312 | tf_op jit(solution)/shard_map/ppermute | solution.py:242
  14.7 3.0 %collective-permute-start.12 = (f32[64,128]{1,0:T(8,128)S(1)}, f32[64,128]{1,0:T(8,128)S(1)}, u32[]{:S(2)}, u32[]{:S(2)}) collective-permute-start(f32[64,128]{1,0:T(8,128)S(1)} %get-tuple-element.71), channel_id=1, source_target_pairs={{0,1},{1,0},{2,3},{3,2},{4,5},{5,4},{6,7},{7,6},{8,9},{9,8},{10,11... | collective-permute-start | bytes 98312 | tf_op jit(solution)/shard_map/ppermute | solution.py:242
  15.3 2.4 %collective-permute-start.13 = (f32[64,128]{1,0:T(8,128)S(1)}, f32[64,128]{1,0:T(8,128)S(1)}, u32[]{:S(2)}, u32[]{:S(2)}) collective-permute-start(f32[64,128]{1,0:T(8,128)S(1)} %get-tuple-element.72), channel_id=1, source_target_pairs={{0,1},{1,0},{2,3},{3,2},{4,5},{5,4},{6,7},{7,6},{8,9},{9,8},{10,11... | collective-permute-start | bytes 98312 | tf_op jit(solution)/shard_map/ppermute | solution.py:242
  15.5 2.3 %collective-permute-start.14 = (f32[64,128]{1,0:T(8,128)S(1)}, f32[64,128]{1,0:T(8,128)S(1)}, u32[]{:S(2)}, u32[]{:S(2)}) collective-permute-start(f32[64,128]{1,0:T(8,128)S(1)} %get-tuple-element.73), channel_id=1, source_target_pairs={{0,1},{1,0},{2,3},{3,2},{4,5},{5,4},{6,7},{7,6},{8,9},{9,8},{10,11... | collective-permute-start | bytes 98312 | tf_op jit(solution)/shard_map/ppermute | solution.py:242
  16.1 1.6 %collective-permute-start.15 = (f32[64,128]{1,0:T(8,128)S(1)}, f32[64,128]{1,0:T(8,128)S(1)}, u32[]{:S(2)}, u32[]{:S(2)}) collective-permute-start(f32[64,128]{1,0:T(8,128)S(1)} %get-tuple-element.74), channel_id=1, source_target_pairs={{0,1},{1,0},{2,3},{3,2},{4,5},{5,4},{6,7},{7,6},{8,9},{9,8},{10,11... | collective-permute-start | bytes 98312 | tf_op jit(solution)/shard_map/ppermute | solution.py:242
  18.1 3.7 %collective-permute-start.18 = (f32[2,256]{1,0:T(2,128)S(1)}, f32[2,256]{1,0:T(2,128)S(1)}, u32[]{:S(2)}, u32[]{:S(2)}) collective-permute-start(f32[2,256]{1,0:T(2,128)S(1)} %get-tuple-element.76.refs_0_), channel_id=1, source_target_pairs={{0,2},{1,3},{2,0},{3,1},{4,6},{5,7},{6,4},{7,5},{8,10},{9,11},{10,... | collective-permute-start | bytes 6152 | tf_op jit(solution)/shard_map/ppermute | solution.py:293
  19.7 3.0 %collective-permute-start.17 = (f32[2,256]{1,0:T(2,128)S(1)}, f32[2,256]{1,0:T(2,128)S(1)}, u32[]{:S(2)}, u32[]{:S(2)}) collective-permute-start(f32[2,256]{1,0:T(2,128)S(1)} %get-tuple-element.76.refs_0_), channel_id=1, source_target_pairs={{0,3},{1,2},{2,1},{3,0},{4,7},{5,6},{6,5},{7,4},{8,11},{9,10},{10,... | collective-permute-start | bytes 6152 | tf_op jit(solution)/shard_map/ppermute | solution.py:293
  19.9 2.8 %collective-permute-start.16 = (f32[2,256]{1,0:T(2,128)S(1)}, f32[2,256]{1,0:T(2,128)S(1)}, u32[]{:S(2)}, u32[]{:S(2)}) collective-permute-start(f32[2,256]{1,0:T(2,128)S(1)} %get-tuple-element.76.refs_0_), channel_id=1, source_target_pairs={{0,1},{1,0},{2,3},{3,2},{4,5},{5,4},{6,7},{7,6},{8,9},{9,8},{10,11... | collective-permute-start | bytes 6152 | tf_op jit(solution)/shard_map/ppermute | solution.py:293
  23.1 4.3 %collective-permute-start.19 = (f32[64,128]{1,0:T(8,128)S(1)}, f32[64,128]{1,0:T(8,128)S(1)}, u32[]{:S(2)}, u32[]{:S(2)}) collective-permute-start(f32[64,128]{1,0:T(8,128)S(1)} %get-tuple-element.86), channel_id=1, source_target_pairs={{0,13},{1,12},{2,15},{3,14},{4,9},{5,8},{6,11},{7,10},{8,5},{9,4},... | collective-permute-start | bytes 98312 | tf_op jit(solution)/shard_map/ppermute | solution.py:242
  24.6 3.5 %collective-permute-start.20 = (f32[64,128]{1,0:T(8,128)S(1)}, f32[64,128]{1,0:T(8,128)S(1)}, u32[]{:S(2)}, u32[]{:S(2)}) collective-permute-start(f32[64,128]{1,0:T(8,128)S(1)} %get-tuple-element.87), channel_id=1, source_target_pairs={{0,9},{1,4},{2,11},{3,6},{4,13},{5,0},{6,15},{7,2},{8,1},{9,12},{1... | collective-permute-start | bytes 98312 | tf_op jit(solution)/shard_map/ppermute | solution.py:242
  25.7 3.3 %collective-permute-start.21 = (f32[64,128]{1,0:T(8,128)S(1)}, f32[64,128]{1,0:T(8,128)S(1)}, u32[]{:S(2)}, u32[]{:S(2)}) collective-permute-start(f32[64,128]{1,0:T(8,128)S(1)} %get-tuple-element.88), channel_id=1, source_target_pairs={{0,5},{1,8},{2,7},{3,10},{4,1},{5,12},{6,3},{7,14},{8,13},{9,0},{1... | collective-permute-start | bytes 98312 | tf_op jit(solution)/shard_map/ppermute | solution.py:242
  26.3 2.7 %collective-permute-start.22 = (f32[64,128]{1,0:T(8,128)S(1)}, f32[64,128]{1,0:T(8,128)S(1)}, u32[]{:S(2)}, u32[]{:S(2)}) collective-permute-start(f32[64,128]{1,0:T(8,128)S(1)} %get-tuple-element.89), channel_id=1, source_target_pairs={{0,1},{1,0},{2,3},{3,2},{4,5},{5,4},{6,7},{7,6},{8,9},{9,8},{10,11... | collective-permute-start | bytes 98312 | tf_op jit(solution)/shard_map/ppermute | solution.py:242
  29.1 5.9 %collective-permute-start.23 = (f32[64,128]{1,0:T(8,128)S(1)}, f32[64,128]{1,0:T(8,128)S(1)}, u32[]{:S(2)}, u32[]{:S(2)}) collective-permute-start(f32[64,128]{1,0:T(8,128)S(1)} %get-tuple-element.91), channel_id=1, source_target_pairs={{0,16},{4,20},{8,24},{12,28},{16,0},{20,4},{24,8},{28,12},{1,17},{... | collective-permute-start | bytes 98312 | tf_op jit(solution)/shard_map/ppermute | solution.py:273
  32.8 2.2 %collective-permute-start.28 = (f32[64,128]{1,0:T(8,128)S(1)}, f32[64,128]{1,0:T(8,128)S(1)}, u32[]{:S(2)}, u32[]{:S(2)}) collective-permute-start(f32[64,128]{1,0:T(8,128)S(1)} %get-tuple-element.96), channel_id=1, source_target_pairs={{0,1},{1,0},{2,3},{3,2},{4,5},{5,4},{6,7},{7,6},{8,9},{9,8},{10,11... | collective-permute-start | bytes 98312 | tf_op jit(solution)/shard_map/ppermute | solution.py:242
  32.8 3.6 %collective-permute-start.29 = (f32[64,128]{1,0:T(8,128)S(1)}, f32[64,128]{1,0:T(8,128)S(1)}, u32[]{:S(2)}, u32[]{:S(2)}) collective-permute-start(f32[64,128]{1,0:T(8,128)S(1)} %get-tuple-element.97), channel_id=1, source_target_pairs={{0,1},{1,0},{2,3},{3,2},{4,5},{5,4},{6,7},{7,6},{8,9},{9,8},{10,11... | collective-permute-start | bytes 98312 | tf_op jit(solution)/shard_map/ppermute | solution.py:242
  33.3 3.6 %collective-permute-start.30 = (f32[64,128]{1,0:T(8,128)S(1)}, f32[64,128]{1,0:T(8,128)S(1)}, u32[]{:S(2)}, u32[]{:S(2)}) collective-permute-start(f32[64,128]{1,0:T(8,128)S(1)} %get-tuple-element.98), channel_id=1, source_target_pairs={{0,1},{1,0},{2,3},{3,2},{4,5},{5,4},{6,7},{7,6},{8,9},{9,8},{10,11... | collective-permute-start | bytes 98312 | tf_op jit(solution)/shard_map/ppermute | solution.py:242
  33.3 5.6 %collective-permute-start.31 = (f32[64,128]{1,0:T(8,128)S(1)}, f32[64,128]{1,0:T(8,128)S(1)}, u32[]{:S(2)}, u32[]{:S(2)}) collective-permute-start(f32[64,128]{1,0:T(8,128)S(1)} %get-tuple-element.99), channel_id=1, source_target_pairs={{0,1},{1,0},{2,3},{3,2},{4,5},{5,4},{6,7},{7,6},{8,9},{9,8},{10,11... | collective-permute-start | bytes 98312 | tf_op jit(solution)/shard_map/ppermute | solution.py:242
  35.0 4.3 %collective-permute-start.24 = (f32[64,128]{1,0:T(8,128)S(1)}, f32[64,128]{1,0:T(8,128)S(1)}, u32[]{:S(2)}, u32[]{:S(2)}) collective-permute-start(f32[64,128]{1,0:T(8,128)S(1)} %get-tuple-element.92), channel_id=1, source_target_pairs={{0,13},{1,12},{2,15},{3,14},{4,9},{5,8},{6,11},{7,10},{8,5},{9,4},... | collective-permute-start | bytes 98312 | tf_op jit(solution)/shard_map/ppermute | solution.py:242
  35.1 4.2 %collective-permute-start.25 = (f32[64,128]{1,0:T(8,128)S(1)}, f32[64,128]{1,0:T(8,128)S(1)}, u32[]{:S(2)}, u32[]{:S(2)}) collective-permute-start(f32[64,128]{1,0:T(8,128)S(1)} %get-tuple-element.93), channel_id=1, source_target_pairs={{0,9},{1,4},{2,11},{3,6},{4,13},{5,0},{6,15},{7,2},{8,1},{9,12},{1... | collective-permute-start | bytes 98312 | tf_op jit(solution)/shard_map/ppermute | solution.py:242
  36.5 3.3 %collective-permute-start.26 = (f32[64,128]{1,0:T(8,128)S(1)}, f32[64,128]{1,0:T(8,128)S(1)}, u32[]{:S(2)}, u32[]{:S(2)}) collective-permute-start(f32[64,128]{1,0:T(8,128)S(1)} %get-tuple-element.94), channel_id=1, source_target_pairs={{0,5},{1,8},{2,7},{3,10},{4,1},{5,12},{6,3},{7,14},{8,13},{9,0},{1... | collective-permute-start | bytes 98312 | tf_op jit(solution)/shard_map/ppermute | solution.py:242
  36.9 2.9 %collective-permute-start.27 = (f32[64,128]{1,0:T(8,128)S(1)}, f32[64,128]{1,0:T(8,128)S(1)}, u32[]{:S(2)}, u32[]{:S(2)}) collective-permute-start(f32[64,128]{1,0:T(8,128)S(1)} %get-tuple-element.95), channel_id=1, source_target_pairs={{0,1},{1,0},{2,3},{3,2},{4,5},{5,4},{6,7},{7,6},{8,9},{9,8},{10,11... | collective-permute-start | bytes 98312 | tf_op jit(solution)/shard_map/ppermute | solution.py:242
